TPU v7x, 32 devices: a whole 2x2x4 slice. The times are simulated.
32 devices in a mesh: energy: 8 (over z, y), slab: 4 (over x, core).
Axes of the slice: x: 2, y: 2, z: 4, core: 2. Of those that a mesh axis runs over, the one named last changes fastest.
Arguments:
- green_prev: bfloat16 [8, 4, 2, 512, 512], P('energy', 'slab'), may hold values from -6 to 6
- slab_inverse: bfloat16 [4, 2, 512, 512], P('slab')
- coupling_block: bfloat16 [512, 512], replicated
- phonon_coupling: bfloat16 [4, 512, 512], P(None, 'energy'), may hold values from -0.1796875 to 0.1796875
- offset: float32 [8], P('energy'), may hold values from -0.5 to 0.5
- occupation: float32 [8], P('energy'), may hold values from 0.05 to 1
- pair_source: int32 [8, 6], replicated, may hold values from 0 to 7
- pair_mode: int32 [8, 6], replicated, may hold values from 0 to 3
- active_slabs: int32 [8], P('energy'), may hold values from 1 to 4, as said below
Outputs:
- green_new: bfloat16 [8, 4, 2, 512, 512], P('energy', 'slab')
- density: float32 [4, 512], P('slab')
Inputs may be any that keep to these rules, and one draw needn't show every extreme that they name: `active_slabs`: some energy scatters in all 4 slabs.
All inputs are finite; a program needn't handle non-finite values.
Results may differ from a plain program's by a relative error of at most 0.012.
Values may be sent and summed in bfloat16 or wider, within the bound.
No kernel may reach another device: no remote copies, remote signals or barrier semaphores. Data moves between devices by JAX's collectives and lax.ppermute only.
A program may use at most 128 MiB of HBM per device.

v0:
```python
import jax
import jax.numpy as jnp
from jax import lax
from jax.sharding import PartitionSpec as P


def from_behind(x, axis, by):
    size = lax.axis_size(axis)
    pairs = [(i, i + by) for i in range(size) if 0 <= i + by < size]
    return lax.ppermute(x, axis, pairs)


def product_left(matrix, stacked):

    def single(first, second):
        return jnp.einsum("ij,ejk->eik", first, second, preferred_element_type=jnp.float32)

    real_part = single(matrix[0], stacked[:, 0]) - single(matrix[1], stacked[:, 1])
    imag_part = single(matrix[0], stacked[:, 1]) + single(matrix[1], stacked[:, 0])
    return jnp.stack((real_part, imag_part), axis=1)


def product_right(stacked, matrix):

    def single(first, second):
        return jnp.einsum("eij,jk->eik", first, second, preferred_element_type=jnp.float32)

    real_part = single(stacked[:, 0], matrix[0]) - single(stacked[:, 1], matrix[1])
    imag_part = single(stacked[:, 0], matrix[1]) + single(stacked[:, 1], matrix[0])
    return jnp.stack((real_part, imag_part), axis=1)


def product_right_transposed(stacked, matrix):

    def single(first, second):
        return jnp.einsum("eij,kj->eik", first, second, preferred_element_type=jnp.float32)

    real_part = single(stacked[:, 0], matrix[0]) - single(stacked[:, 1], matrix[1])
    imag_part = single(stacked[:, 0], matrix[1]) + single(stacked[:, 1], matrix[0])
    return jnp.stack((real_part, imag_part), axis=1)


def advance_with(factor, base_part, incoming):
    left_block = product_left(factor, incoming).astype(jnp.bfloat16)
    return (product_right_transposed(left_block, factor) + base_part).astype(jnp.bfloat16)


def local(
    green_prev,
    slab_inverse,
    coupling_block,
    phonon_coupling,
    offset,
    occupation,
    pair_source,
    pair_mode,
    active_slabs,
):
    energy_count = pair_source.shape[0]
    mode_count = phonon_coupling.shape[0]
    orbital_count = coupling_block.shape[0]
    energy_iota = jnp.arange(energy_count, dtype=jnp.int32)
    mode_iota = jnp.arange(mode_count, dtype=jnp.int32)
    source_hot = (pair_source[:, :, None] == energy_iota[None, None, :]).astype(jnp.float32)
    mode_hot = (pair_mode[:, :, None] == mode_iota[None, None, :]).astype(jnp.float32)
    weights = jnp.einsum("epf,epm->mef", source_hot, mode_hot).astype(jnp.bfloat16)
    inverse = slab_inverse[0]
    couple = jnp.stack(
        (
            jnp.dot(inverse[0], coupling_block, preferred_element_type=jnp.float32),
            jnp.dot(inverse[1], coupling_block, preferred_element_type=jnp.float32),
        )
    ).astype(jnp.bfloat16)
    row_block = lax.all_to_all(green_prev, "energy", split_axis=3, concat_axis=0, tiled=True)
    summed = jnp.zeros(row_block.shape, jnp.float32)
    for mode_index in range(mode_count):
        combined = jnp.einsum(
            "ef,fkcrn->ekcrn", weights[mode_index], row_block, preferred_element_type=jnp.float32
        )
        summed = summed + phonon_coupling[mode_index].astype(jnp.float32) * combined
    self_energy = lax.all_to_all(
        summed.astype(jnp.bfloat16), "energy", split_axis=0, concat_axis=3, tiled=True
    )[:, 0]
    slab_pos = lax.axis_index("slab")
    active_mask = (slab_pos < active_slabs).astype(jnp.float32)
    identity_matrix = jnp.eye(orbital_count, dtype=jnp.float32)
    total_real = (
        active_mask[:, None, None] * self_energy[:, 0].astype(jnp.float32)
        + offset[:, None, None] * identity_matrix[None]
    )
    total_imag = active_mask[:, None, None] * self_energy[:, 1].astype(jnp.float32)
    sig_total = jnp.stack((total_real, total_imag), axis=1).astype(jnp.bfloat16)
    half_product = product_left(inverse, sig_total).astype(jnp.bfloat16)
    base_block = inverse.astype(jnp.float32)[None] + product_right(half_product, inverse)

    def advance(incoming):
        return advance_with(couple, base_block, incoming)

    current = jnp.zeros(base_block.shape, jnp.bfloat16)
    for section in range(lax.axis_size("slab")):
        received = from_behind(current, "slab", 1)
        current = lax.cond(
            slab_pos == section, advance, lambda unused, kept=current: kept, received
        )
    diagonal_imag = jnp.diagonal(current[:, 1], axis1=1, axis2=2).astype(jnp.float32)
    local_terms = -jnp.sum(occupation[:, None] * diagonal_imag, axis=0)
    density = lax.psum(local_terms, "energy")
    return (current[:, None], density[None])


def solution(mesh):
    in_specs = (
        P("energy", "slab", None, None, None),
        P("slab", None, None, None),
        P(),
        P(None, "energy", None),
        P("energy"),
        P("energy"),
        P(),
        P(),
        P("energy"),
    )
    out_specs = (P("energy", "slab", None, None, None), P("slab", None))
    return jax.shard_map(local, mesh=mesh, in_specs=in_specs, out_specs=out_specs, check_vma=False)
```

profile of v0, /device:TPU:2, one launch (start us, length us, event | category | flops | bytes accessed | tf_op | source)
XLA Modules:
  0.0 165.5 jit_solution(12639551744509074830)
XLA Ops:
  0.7 3.3 %copy.13 = bf16[1,1,2,512,512]{4,2,1,0,3:T(2,128)(2,1)} copy(bf16[1,1,2,512,512]{4,3,2,1,0:T(8,128)(2,1)} %param.17) | data formatting | bytes 2097152 | tf_op args[0]
  4.0 5.8 %all-to-all-start = ((bf16[1,1,2,512,512]{4,2,1,0,3:T(2,128)(2,1)}), bf16[1,1,2,512,512]{4,2,1,0,3:T(2,128)(2,1)S(1)}, u32[]{:S(2)}, u32[]{:S(2)}) async-start(bf16[1,1,2,512,512]{4,2,1,0,3:T(2,128)(2,1)} %copy.13), calls=%async_computation | async-start | bytes 2097152 | tf_op jit(solution)/shard_map/all_to_all | solution.py:74
  9.9 0.2 fusion.149
  10.2 25.5 %all-to-all-done = bf16[1,1,2,512,512]{4,2,1,0,3:T(2,128)(2,1)S(1)} async-done(((bf16[1,1,2,512,512]{4,2,1,0,3:T(2,128)(2,1)}), bf16[1,1,2,512,512]{4,2,1,0,3:T(2,128)(2,1)S(1)}, u32[]{:S(2)}, u32[]{:S(2)}) %all-to-all-start) | async-done | bytes 1048608 | tf_op jit(solution)/shard_map/all_to_all | solution.py:74
  35.6 1.2 fusion.151
  36.9 1.2 fusion.153
  38.1 1.2 fusion.155
  39.3 1.8 %fusion.140 = bf16[8,1,2,64,512]{4,0,3,2,1:T(8,128)(2,1)S(1)} fusion(f32[8,2,64,512]{3,0,2,1:T(8,128)S(1)} %fusion.151, f32[8,2,64,512]{3,0,2,1:T(8,128)S(1)} %fusion.153, f32[8,2,64,512]{3,0,2,1:T(8,128)S(1)} %fusion.155, f32[64,512]{1,0:T(8,128)S(1)} %get-tuple-element.55, f32[64,512]{1,0:T(8,128)S(1)} %get-tuple-element.56, ...), kind=kOutput, calls=%fused_computation.163 | convolution fusion | flops 12582912 | bytes 8913024 | tf_op jit(solution)/shard_map/ef,fkcrn->ekcrn/dot_general | solution.py:77
  41.1 1.3 copy.16
  42.4 4.4 %all-to-all-start.1 = ((bf16[8,1,2,64,512]{4,3,2,1,0:T(8,128)(2,1)}), bf16[8,1,2,64,512]{4,3,2,1,0:T(8,128)(2,1)}, u32[]{:S(2)}, u32[]{:S(2)}) async-start(bf16[8,1,2,64,512]{4,3,2,1,0:T(8,128)(2,1)} %copy.16), calls=%async_computation.1 | async-start | bytes 2097152 | tf_op jit(solution)/shard_map/all_to_all | solution.py:81
  46.8 1.0 broadcast_in_dim.10
  47.8 1.9 %collective-permute-start = (bf16[1,2,512,512]{3,2,1,0:T(8,128)(2,1)}, bf16[1,2,512,512]{3,2,1,0:T(8,128)(2,1)}, u32[]{:S(2)}, u32[]{:S(2)}) collective-permute-start(bf16[1,2,512,512]{3,2,1,0:T(8,128)(2,1)} %broadcast_in_dim.10), channel_id=1, source_target_pairs={{0,1},{1,2},{2,3},{4,5},{5,6},{6,7},{8,9},{9,10},{10,11},{12,13},{... | collective-permute-start | bytes 3145736 | tf_op jit(solution)/shard_map/ppermute | solution.py:10
  51.0 0.4 fusion.147
  51.5 0.4 fusion.148
  51.9 0.1 pad_maximum_fusion
  52.0 20.3 %all-to-all-done.1 = bf16[8,1,2,64,512]{4,3,2,1,0:T(8,128)(2,1)} async-done(((bf16[8,1,2,64,512]{4,3,2,1,0:T(8,128)(2,1)}), bf16[8,1,2,64,512]{4,3,2,1,0:T(8,128)(2,1)}, u32[]{:S(2)}, u32[]{:S(2)}) %all-to-all-start.1) | async-done | bytes 1048608 | tf_op jit(solution)/shard_map/all_to_all | solution.py:81
  72.4 1.3 copy.17
  73.7 0.5 fusion.170
  74.2 0.5 fusion.174
  74.7 0.5 fusion.146
  75.2 0.5 fusion.145
  75.7 0.5 fusion.172
  76.1 0.5 fusion.142
  76.6 0.5 fusion.163
  77.1 0.5 fusion.141
  77.6 1.7 maximum_add_fusion.4
  79.2 0.3 conditional.4
  79.5 1.0 copy-done.6
  80.4 1.9 %collective-permute-start.1 = (bf16[1,2,512,512]{3,2,1,0:T(8,128)(2,1)}, bf16[1,2,512,512]{3,2,1,0:T(8,128)(2,1)S(1)}, u32[]{:S(2)}, u32[]{:S(2)}) collective-permute-start(bf16[1,2,512,512]{3,2,1,0:T(8,128)(2,1)} %copy-done.6), channel_id=1, source_target_pairs={{0,1},{1,2},{2,3},{4,5},{5,6},{6,7},{8,9},{9,10},{10,11},{12,13},{... | collective-permute-start | bytes 3145736 | tf_op jit(solution)/shard_map/ppermute | solution.py:10
  82.4 14.4 %collective-permute-done.1 = bf16[1,2,512,512]{3,2,1,0:T(8,128)(2,1)S(1)} collective-permute-done((bf16[1,2,512,512]{3,2,1,0:T(8,128)(2,1)}, bf16[1,2,512,512]{3,2,1,0:T(8,128)(2,1)S(1)}, u32[]{:S(2)}, u32[]{:S(2)}) %collective-permute-start.1) | collective-permute-done | bytes 1048608 | tf_op jit(solution)/shard_map/ppermute | solution.py:10
  96.8 1.9 %collective-permute-start.2 = (bf16[1,2,512,512]{3,2,1,0:T(8,128)(2,1)}, bf16[1,2,512,512]{3,2,1,0:T(8,128)(2,1)S(1)}, u32[]{:S(2)}, u32[]{:S(2)}) collective-permute-start(bf16[1,2,512,512]{3,2,1,0:T(8,128)(2,1)} %get-tuple-element.62), channel_id=1, source_target_pairs={{0,1},{1,2},{2,3},{4,5},{5,6},{6,7},{8,9},{9,10},{10,11},{12,13},{... | collective-permute-start | bytes 3145736 | tf_op jit(solution)/shard_map/ppermute | solution.py:10
  98.7 18.4 %collective-permute-done.2 = bf16[1,2,512,512]{3,2,1,0:T(8,128)(2,1)S(1)} collective-permute-done((bf16[1,2,512,512]{3,2,1,0:T(8,128)(2,1)}, bf16[1,2,512,512]{3,2,1,0:T(8,128)(2,1)S(1)}, u32[]{:S(2)}, u32[]{:S(2)}) %collective-permute-start.2) | collective-permute-done | bytes 1048608 | tf_op jit(solution)/shard_map/ppermute | solution.py:10
  117.1 6.4 %conditional.6 = (bf16[1,2,512,512]{3,2,1,0:T(8,128)(2,1)}) conditional(s32[]{:T(128)} %convert_element_type.161, bf16[1,2,512,512]{3,2,1,0:T(8,128)(2,1)} %get-tuple-element.62, (bf16[1,2,512,512]{3,2,1,0:T(8,128)(2,1)S(1)}, bf16[2,512,512]{2,1,0:T(8,128)(2,1)S(1)}, f32[1,2,512,512]{3,2,1,0:T(8,128)}) %tuple.35), branch_computations={%region_4.0_spmd, %region_5.0_spmd} | conditional | flops 2150629376 | bytes 33554468 | solution.py:102
  117.1 0.5 fusion.89
  117.6 0.5 fusion.76
  118.1 0.5 fusion.77
  118.5 0.5 fusion.82
  119.0 0.5 fusion.75
  119.5 0.5 fusion.71
  120.0 0.5 fusion.87
  120.5 0.5 fusion.72
  121.0 1.1 copy-done.3
  122.1 1.3 fusion.70
  123.4 1.9 %collective-permute-start.3 = (bf16[1,2,512,512]{3,2,1,0:T(8,128)(2,1)}, bf16[1,2,512,512]{3,2,1,0:T(8,128)(2,1)S(1)}, u32[]{:S(2)}, u32[]{:S(2)}) collective-permute-start(bf16[1,2,512,512]{3,2,1,0:T(8,128)(2,1)} %get-tuple-element.63), channel_id=1, source_target_pairs={{0,1},{1,2},{2,3},{4,5},{5,6},{6,7},{8,9},{9,10},{10,11},{12,13},{... | collective-permute-start | bytes 3145736 | tf_op jit(solution)/shard_map/ppermute | solution.py:10
  126.0 13.7 %collective-permute-done.3 = bf16[1,2,512,512]{3,2,1,0:T(8,128)(2,1)S(1)} collective-permute-done((bf16[1,2,512,512]{3,2,1,0:T(8,128)(2,1)}, bf16[1,2,512,512]{3,2,1,0:T(8,128)(2,1)S(1)}, u32[]{:S(2)}, u32[]{:S(2)}) %collective-permute-start.3) | collective-permute-done | bytes 1048608 | tf_op jit(solution)/shard_map/ppermute | solution.py:10
  139.7 1.1 slice_bitcast_fusion
  140.8 4.8 %gather_fusion = bf16[512]{0:T(512)(128)(2,1)S(1)} fusion(bf16[512,512]{1,0:T(8,128)(2,1)S(1)} %slice_bitcast_fusion, s32[512]{0:T(512)S(1)} %bitcast.313), kind=kCustom, calls=%fused_computation | custom fusion | bytes 6144 | tf_op jit(solution)/shard_map/jit(diagonal)/gather | solution.py:105
  145.7 19.8 %psum.7 = f32[1,512]{1,0:T(1,128)} all-reduce(f32[1,512]{1,0:T(1,128)S(1)} %bitcast.323), channel_id=1, replica_groups=mesh['energy'=8,'slab'=4] {'energy'}, use_global_device_ids=true, to_apply=%region_8.9 | all-reduce | flops 512 | bytes 4096 | tf_op jit(solution)/shard_map/psum | solution.py:107
  (20 shorter events, 0.2 us)
Async XLA Ops:
  0.6 50.4 %copy-start = (bf16[512,512]{1,0:T(8,128)(2,1)S(1)}, bf16[512,512]{1,0:T(8,128)(2,1)}, u32[]{:S(2)}) copy-start(bf16[512,512]{1,0:T(8,128)(2,1)} %param.19) | copy-start | bytes 1572868
  0.6 9.2 %copy-start.8 = (s32[8,6]{1,0:T(8,128)S(1)}, s32[8,6]{1,0:T(8,128)}, u32[]{:S(2)}) copy-start(s32[8,6]{1,0:T(8,128)} %param.23) | copy-start | bytes 580
  0.7 9.2 %copy-start.9 = (s32[8,6]{1,0:T(8,128)S(1)}, s32[8,6]{1,0:T(8,128)}, u32[]{:S(2)}) copy-start(s32[8,6]{1,0:T(8,128)} %param.24) | copy-start | bytes 580
  0.7 9.4 %copy-start.7 = (bf16[4,64,512]{2,1,0:T(8,128)(2,1)S(1)}, bf16[4,64,512]{2,1,0:T(8,128)(2,1)}, u32[]{:S(2)}) copy-start(bf16[4,64,512]{2,1,0:T(8,128)(2,1)} %param.20) | copy-start | bytes 786436
  4.0 31.6 %all-to-all-start = ((bf16[1,1,2,512,512]{4,2,1,0,3:T(2,128)(2,1)}), bf16[1,1,2,512,512]{4,2,1,0,3:T(2,128)(2,1)S(1)}, u32[]{:S(2)}, u32[]{:S(2)}) async-start(bf16[1,1,2,512,512]{4,2,1,0,3:T(2,128)(2,1)} %copy.13), calls=%async_computation | async-start | bytes 2097152 | tf_op jit(solution)/shard_map/all_to_all | solution.py:74
  42.4 8.6 %copy-start.5 = (bf16[1,2,512,512]{3,2,1,0:T(8,128)(2,1)S(1)}, bf16[1,2,512,512]{3,2,1,0:T(8,128)(2,1)}, u32[]{:S(2)}) copy-start(bf16[1,2,512,512]{3,2,1,0:T(8,128)(2,1)} %param.18) | copy-start | bytes 3145732
  42.4 30.0 %all-to-all-start.1 = ((bf16[8,1,2,64,512]{4,3,2,1,0:T(8,128)(2,1)}), bf16[8,1,2,64,512]{4,3,2,1,0:T(8,128)(2,1)}, u32[]{:S(2)}, u32[]{:S(2)}) async-start(bf16[8,1,2,64,512]{4,3,2,1,0:T(8,128)(2,1)} %copy.16), calls=%async_computation.1 | async-start | bytes 2097152 | tf_op jit(solution)/shard_map/all_to_all | solution.py:81
  47.8 31.4 %collective-permute-start = (bf16[1,2,512,512]{3,2,1,0:T(8,128)(2,1)}, bf16[1,2,512,512]{3,2,1,0:T(8,128)(2,1)}, u32[]{:S(2)}, u32[]{:S(2)}) collective-permute-start(bf16[1,2,512,512]{3,2,1,0:T(8,128)(2,1)} %broadcast_in_dim.10), channel_id=1, source_target_pairs={{0,1},{1,2},{2,3},{4,5},{5,6},{6,7},{8,9},{9,10},{10,11},{12,13},{... | collective-permute-start | bytes 3145736 | tf_op jit(solution)/shard_map/ppermute | solution.py:10
  79.5 1.0 copy-start.6
  80.4 16.3 %collective-permute-start.1 = (bf16[1,2,512,512]{3,2,1,0:T(8,128)(2,1)}, bf16[1,2,512,512]{3,2,1,0:T(8,128)(2,1)S(1)}, u32[]{:S(2)}, u32[]{:S(2)}) collective-permute-start(bf16[1,2,512,512]{3,2,1,0:T(8,128)(2,1)} %copy-done.6), channel_id=1, source_target_pairs={{0,1},{1,2},{2,3},{4,5},{5,6},{6,7},{8,9},{9,10},{10,11},{12,13},{... | collective-permute-start | bytes 3145736 | tf_op jit(solution)/shard_map/ppermute | solution.py:10
  96.8 20.3 %collective-permute-start.2 = (bf16[1,2,512,512]{3,2,1,0:T(8,128)(2,1)}, bf16[1,2,512,512]{3,2,1,0:T(8,128)(2,1)S(1)}, u32[]{:S(2)}, u32[]{:S(2)}) collective-permute-start(bf16[1,2,512,512]{3,2,1,0:T(8,128)(2,1)} %get-tuple-element.62), channel_id=1, source_target_pairs={{0,1},{1,2},{2,3},{4,5},{5,6},{6,7},{8,9},{9,10},{10,11},{12,13},{... | collective-permute-start | bytes 3145736 | tf_op jit(solution)/shard_map/ppermute | solution.py:10
  120.5 1.6 copy-start.3
  123.4 16.3 %collective-permute-start.3 = (bf16[1,2,512,512]{3,2,1,0:T(8,128)(2,1)}, bf16[1,2,512,512]{3,2,1,0:T(8,128)(2,1)S(1)}, u32[]{:S(2)}, u32[]{:S(2)}) collective-permute-start(bf16[1,2,512,512]{3,2,1,0:T(8,128)(2,1)} %get-tuple-element.63), channel_id=1, source_target_pairs={{0,1},{1,2},{2,3},{4,5},{5,6},{6,7},{8,9},{9,10},{10,11},{12,13},{... | collective-permute-start | bytes 3145736 | tf_op jit(solution)/shard_map/ppermute | solution.py:10
where the time goes:
time: 166 us
  waiting for transfers between devices  92.3 us (56%)
  blocking collectives  19.8 us (12%)
  starting transfers between devices  17.8 us (11%)
  local copies, waits for them, and re-layouts  15.1 us (9%)
  matrix products  14.3 us (9%)
  other arithmetic  3.14 us (2%)
  between operations  2.84 us (2%)
    ppermute x4, waiting for transfers between devices, from_behind(): return lax.ppermute(x, axis, pairs)  46.5 us
    all_to_all x1, waiting for transfers between devices, local(): lax.all_to_all(green_prev, 'energy', split_axis=3, concat_axis=0, tiled=T...  25.5 us
    all_to_all x1, waiting for transfers between devices, local(): lax.all_to_all(summed.astype(jnp.bfloat16), 'energy', split_axis=0, conca...  20.3 us
    psum x1, blocking collectives, local(): density = lax.psum(local_terms, 'energy')  19.8 us
    ppermute x4, starting transfers between devices, from_behind(): return lax.ppermute(x, axis, pairs)  7.63 us
    all_to_all x1, starting transfers between devices, local(): lax.all_to_all(green_prev, 'energy', split_axis=3, concat_axis=0, tiled=T...  5.83 us
    dot_general x4, matrix products, local(): jnp.einsum('ef,fkcrn->ekcrn', weights[mode_index], row_block, preferred_e...  5.49 us
    gather x1, local copies, waits for them, and re-layouts, local(): jnp.diagonal(current[:, 1], axis1=1, axis2=2).astype(jnp.float32)  4.85 us
  transfers between devices with their start and end apart: 6, of which 5 were waited for; matrix products, arithmetic and copies ran while one was open for 5% of the time, Pallas kernels for 0%

commit v1 on v0

v1 whole, which is shorter than its diff:
```python
import functools

import jax
import jax.numpy as jnp
from jax import lax
from jax.experimental import pallas as pl
from jax.experimental.pallas import tpu as pltpu
from jax.sharding import PartitionSpec as P

BF16 = jnp.bfloat16
F32 = jnp.float32
VMEM = pl.BlockSpec(memory_space=pltpu.VMEM)
SMEM = pl.BlockSpec(memory_space=pltpu.SMEM)
VMEM_LIMIT = 48 * 2**20


def mxu(first, second):
    return jnp.dot(first, second, preferred_element_type=F32)


def mxu_nt(first, second):
    return lax.dot_general(first, second, (((1,), (1,)), ((), ())), preferred_element_type=F32)


def call(kernel, out_shape, in_specs, scratch=(), flops=0, bytes_accessed=0):
    return pl.pallas_call(
        kernel,
        out_shape=out_shape,
        in_specs=in_specs,
        out_specs=jax.tree.map(lambda _: VMEM, out_shape),
        scratch_shapes=list(scratch),
        compiler_params=pltpu.CompilerParams(vmem_limit_bytes=VMEM_LIMIT),
        cost_estimate=pl.CostEstimate(flops=flops, bytes_accessed=bytes_accessed, transcendentals=0),
    )


def embed_store(ref, column):
    n = column.shape[1]
    real, imag = column[:n], column[n:]
    ref[:n, :n] = real
    ref[n:, n:] = real
    ref[n:, :n] = imag
    ref[:n, n:] = -imag


def mix_kernel(place_ref, source_ref, mode_ref, phonon_ref, *refs):
    energies = (len(refs) - 2) // 2
    pieces, outs = refs[:energies], refs[energies : 2 * energies]
    green, phonon = refs[2 * energies :]
    place = place_ref[0]
    pairs = source_ref.shape[1]
    rows, n = phonon_ref.shape[1:]
    phonon[...] = phonon_ref[...].astype(F32)
    for distance in range(energies):
        green[distance] = pieces[distance][...].astype(F32)
    step = 16

    @pl.loop(0, rows // step)
    def _(block):
        at = pl.ds(pl.multiple_of(block * step, step), step)
        for distance in range(energies):
            energy = place ^ distance
            real = jnp.zeros((step, n), F32)
            imag = jnp.zeros((step, n), F32)
            for pair in range(pairs):
                origin = source_ref[energy, pair] ^ place
                factor = phonon[mode_ref[energy, pair], at, :]
                real = real + factor * green[origin, 0, at, :]
                imag = imag + factor * green[origin, 1, at, :]
            outs[distance][at, :n] = real.astype(BF16)
            outs[distance][at, n:] = imag.astype(BF16)


def mix(place, source, mode, phonon, pieces):
    energies = len(pieces)
    _, rows, n = pieces[0].shape
    return call(
        mix_kernel,
        [jax.ShapeDtypeStruct((rows, 2 * n), BF16)] * energies,
        [SMEM] * 3 + [VMEM] * (energies + 1),
        [pltpu.VMEM((energies, 2, rows, n), F32), pltpu.VMEM(phonon.shape, F32)],
        flops=energies * 24 * rows * n * 16,
        bytes_accessed=energies * rows * n * 8,
    )(place, source, mode, phonon, *pieces)


def right_kernel(place_ref, scalar_ref, right_ref, inverse_ref, *refs):
    pieces, out_ref, rows_ref = refs[:-2], refs[-2], refs[-1]
    count = len(pieces)
    rows = pieces[0].shape[0]
    n = inverse_ref.shape[1]
    base = place_ref[0]
    for index, piece in enumerate(pieces):
        at = (place_ref[1] ^ index) & (count - 1)
        rows_ref[pl.ds(pl.multiple_of(at * rows, rows), rows), :] = piece[...]
    mask, offset = scalar_ref[0], scalar_ref[1]
    start = pl.multiple_of(base * (rows * count), rows * count)
    total = count * rows
    eye = (
        lax.broadcasted_iota(jnp.int32, (total, n), 0) + start
        == lax.broadcasted_iota(jnp.int32, (total, n), 1)
    ).astype(F32)
    for part in range(2):
        product = mxu(rows_ref[...], right_ref[:, part * n : (part + 1) * n])
        own = inverse_ref[part, pl.ds(start, total), :].astype(F32)
        value = mask * product + offset * own
        if part == 0:
            value = value + eye
        out_ref[:, part * n : (part + 1) * n] = value.astype(BF16)


def right_rows(place, scalars, right, inverse, pieces):
    rows = pieces[0].shape[0]
    total = rows * len(pieces)
    n = inverse.shape[1]
    return call(
        right_kernel,
        jax.ShapeDtypeStruct((total, 2 * n), BF16),
        [SMEM, SMEM] + [VMEM] * (2 + len(pieces)),
        [pltpu.VMEM((total, 2 * n), BF16)],
        flops=8 * total * n * n,
        bytes_accessed=8 * n * n,
    )(place, scalars, right, inverse, *pieces)


def own_matrices_kernel(core_ref, low_ref, high_ref, self_ref, coupling_ref, low_col, high_embed, factor_embed):
    n = coupling_ref.shape[0]
    coupling = coupling_ref[...]
    low_col[...] = mxu(low_ref[...], coupling).astype(BF16)
    embed_store(high_embed, mxu(high_ref[...], coupling).astype(BF16))

    @pl.when(core_ref[0] == 0)
    def _():
        embed_store(factor_embed, mxu(high_embed[...], self_ref[...]).astype(BF16))

    @pl.when(core_ref[0] != 0)
    def _():
        factor_embed[...] = jnp.zeros_like(factor_embed)


def own_matrices(core, low, high, own, coupling):
    n = coupling.shape[0]
    square = jax.ShapeDtypeStruct((2 * n, 2 * n), BF16)
    return call(
        own_matrices_kernel,
        [jax.ShapeDtypeStruct((2 * n, n), BF16), square, square],
        [SMEM] + [VMEM] * 4,
        flops=16 * n**3,
        bytes_accessed=28 * n * n,
    )(core, low, high, own, coupling)


def far_matrices_kernel(core_ref, chain_ref, far_high_ref, far_self_ref, coupling_ref, high_embed, moves, factors, embed, column):
    n = coupling_ref.shape[0]
    core = core_ref[0]
    embed_store(embed, chain_ref[...])

    @pl.when(core == 0)
    def _():
        far_high = mxu(far_high_ref[...], coupling_ref[...]).astype(BF16)
        column[...] = mxu(embed[...], far_high).astype(BF16)
        embed_store(embed, column[...])

    @pl.when(core != 0)
    def _():
        column[...] = chain_ref[...]

    low, high = core, 1 - core
    moves[low] = embed[...]
    column[...] = mxu(high_embed[...], column[...]).astype(BF16)
    embed_store(moves.at[high], column[...])
    for place in range(2):
        embed_store(factors.at[place], mxu(moves[place], far_self_ref[...]).astype(BF16))


def far_matrices(core, chain, far_high, far_self, coupling, high_embed):
    n = coupling.shape[0]
    pair = jax.ShapeDtypeStruct((2, 2 * n, 2 * n), BF16)
    return call(
        far_matrices_kernel,
        [pair, pair],
        [SMEM] + [VMEM] * 5,
        [pltpu.VMEM((2 * n, 2 * n), BF16), pltpu.VMEM((2 * n, n), BF16)],
        flops=36 * n**3,
        bytes_accessed=28 * n * n,
    )(core, chain, far_high, far_self, coupling, high_embed)


def left_kernel(bases_ref, *refs, plan, out_index):
    refs = list(refs)
    out_ref, rows_ref, column_ref = refs[-3:]
    n = out_ref.shape[1]
    total = None
    cursor = 0
    for has_move, chunks, index in plan:
        for chunk in range(chunks):
            block = refs[cursor]
            cursor += 1
            size = block.shape[0]
            start = pl.multiple_of(bases_ref[chunk] * size, size)
            rows_ref[pl.ds(start, size), :] = block[...]
        if has_move:
            move = refs[cursor]
            cursor += 1
            move = move if index is None else move.at[index]
            for part in range(2):
                column_ref[part * n : (part + 1) * n, :] = mxu_nt(
                    rows_ref[...], move[part * n : (part + 1) * n, :]
                ).astype(BF16)
        else:
            column_ref[:n, :] = rows_ref[:, :n]
            column_ref[n:, :] = rows_ref[:, n:]
        factor = refs[cursor]
        cursor += 1
        factor = factor if index is None else factor.at[index]
        product = mxu(factor[...], column_ref[...])
        total = product if total is None else total + product
    out_ref[...] = total.astype(out_ref.dtype)


def left_sum(bases, terms, dtype, n):
    plan, arrays = [], []
    for chunks, move, factor, index in terms:
        plan.append((move is not None, len(chunks), index))
        arrays += list(chunks)
        if move is not None:
            arrays.append(move)
        arrays.append(factor)
    return call(
        functools.partial(left_kernel, plan=tuple(plan), out_index=None),
        jax.ShapeDtypeStruct((2 * n, n), dtype),
        [SMEM] + [VMEM] * len(arrays),
        [pltpu.VMEM((n, 2 * n), BF16), pltpu.VMEM((2 * n, n), BF16)],
        flops=16 * n**3 * len(terms),
        bytes_accessed=16 * n * n * len(terms),
    )(bases, *arrays)


def finish_kernel(scalar_ref, own_ref, partner_ref, green_ref, density_ref):
    n = own_ref.shape[1]
    green = (own_ref[...] + partner_ref[...].astype(F32)).astype(BF16)
    green_ref[...] = green
    eye = lax.broadcasted_iota(jnp.int32, (n, n), 0) == lax.broadcasted_iota(jnp.int32, (n, n), 1)
    diagonal = jnp.sum(jnp.where(eye, green[n:].astype(F32), 0.0), axis=0, keepdims=True)
    density_ref[...] = -scalar_ref[0] * diagonal


def finish(scalars, own, partner):
    n = own.shape[1]
    return call(
        finish_kernel,
        [jax.ShapeDtypeStruct((2 * n, n), BF16), jax.ShapeDtypeStruct((1, n), F32)],
        [SMEM, VMEM, VMEM],
        flops=8 * n * n,
        bytes_accessed=16 * n * n,
    )(scalars, own, partner)


def exchange(x, axis, distance):
    size = lax.axis_size(axis)
    return lax.ppermute(x, axis, [(i, i ^ distance) for i in range(size)])


def shift(x, axis, by):
    size = lax.axis_size(axis)
    return lax.ppermute(x, axis, [(i, i + by) for i in range(size - by)])


def local(
    green_prev,
    slab_inverse,
    coupling_block,
    phonon_coupling,
    offset,
    occupation,
    pair_source,
    pair_mode,
    active_slabs,
):
    energies = pair_source.shape[0]
    n = coupling_block.shape[0]
    rows = n // energies
    slabs = lax.axis_size("slab")
    place = lax.axis_index("energy").astype(jnp.int32)
    slab = lax.axis_index("slab").astype(jnp.int32)
    core = slab & 1
    place_one = place[None]
    core_one = core[None]
    inverse = slab_inverse[0]
    column = inverse.reshape(2 * n, n)
    green = green_prev[0, 0]

    pieces = []
    for distance in range(energies):
        piece = lax.dynamic_slice_in_dim(green, (place ^ distance) * rows, rows, axis=1)
        pieces.append(piece if distance == 0 else exchange(piece, "energy", distance))

    partner = exchange(column, "slab", 1)
    low = jnp.where(core == 0, column, partner)
    high = jnp.where(core == 0, partner, column)
    right = jnp.concatenate(
        (
            jnp.concatenate((inverse[0], inverse[1]), axis=1),
            jnp.concatenate((-inverse[1], inverse[0]), axis=1),
        ),
        axis=0,
    )
    own_embed = jnp.concatenate(
        (
            jnp.concatenate((inverse[0], -inverse[1]), axis=1),
            jnp.concatenate((inverse[1], inverse[0]), axis=1),
        ),
        axis=0,
    )
    low_col, high_embed, own_factor = own_matrices(core_one, low, high, column, coupling_block)
    far = []
    chain = low_col
    for back in range(2, slabs, 2):
        far_self = shift(column, "slab", back)
        far_partner = exchange(far_self, "slab", 1)
        far_high = jnp.where(core == 0, far_partner, far_self)
        far.append(far_matrices(core_one, chain, far_high, far_self, coupling_block, high_embed))
        if back + 2 < slabs:
            far_low = jnp.where(core == 0, far_self, far_partner)
            for block in (far_high, far_low):
                step = jnp.dot(block, coupling_block, preferred_element_type=F32).astype(BF16)
                real, imag = chain[:n], chain[n:]
                chain = jnp.concatenate(
                    (
                        jnp.dot(real, step[:n], preferred_element_type=F32)
                        - jnp.dot(imag, step[n:], preferred_element_type=F32),
                        jnp.dot(real, step[n:], preferred_element_type=F32)
                        + jnp.dot(imag, step[:n], preferred_element_type=F32),
                    ),
                    axis=0,
                ).astype(BF16)

    mixed = mix(place_one, pair_source, pair_mode, phonon_coupling, pieces)
    back = [mixed[0]] + [exchange(mixed[d], "energy", d) for d in range(1, energies)]

    mask = (slab < active_slabs).astype(F32)
    scalars = jnp.concatenate((mask, offset))
    groups = [(0, energies // 2), (energies // 2, 3 * energies // 4), (3 * energies // 4, energies)]
    bases, own_chunks = [], []
    for first, last in groups:
        count = last - first
        base = (place ^ first) // count
        bases.append(base)
        own_chunks.append(
            right_rows(jnp.stack((base, place ^ first)), scalars, right, inverse, back[first:last])
        )
    bases = jnp.stack(bases)
    far_chunks = [
        [shift(chunk, "slab", 2 * (index + 1)) for chunk in own_chunks] for index in range(len(far))
    ]
    to_partner = left_sum(
        bases,
        [(own_chunks, high_embed, own_factor, None)]
        + [(chunks, moves, factors, 1) for chunks, (moves, factors) in zip(far_chunks, far)],
        BF16,
        n,
    )
    from_partner = exchange(to_partner, "slab", 1)
    own_sum = left_sum(
        bases,
        [(own_chunks, None, own_embed, None)]
        + [(chunks, moves, factors, 0) for chunks, (moves, factors) in zip(far_chunks, far)],
        F32,
        n,
    )
    current, terms = finish(occupation, own_sum, from_partner)
    spread = jnp.broadcast_to(terms[None], (energies, 1, n))
    density = jnp.sum(lax.all_to_all(spread, "energy", 0, 0, tiled=True), axis=0)
    return (current.reshape(1, 1, 2, n, n), density)


def solution(mesh):
    in_specs = (
        P("energy", "slab", None, None, None),
        P("slab", None, None, None),
        P(),
        P(None, "energy", None),
        P("energy"),
        P("energy"),
        P(),
        P(),
        P("energy"),
    )
    out_specs = (P("energy", "slab", None, None, None), P("slab", None))
    return jax.shard_map(local, mesh=mesh, in_specs=in_specs, out_specs=out_specs, check_vma=False)
```

time: 166 us -> 135 us (0.81)
  the two profiles are of different devices: /device:TPU:2 before, /device:TPU:0 now
where the time goes in v1:
time: 135 us
  starting transfers between devices  45.7 us (34%)
  Pallas kernels  37.7 us (28%)
  local copies, waits for them, and re-layouts  15.1 us (11%)
  other arithmetic  13.3 us (10%)
  blocking collectives  11.2 us (8%)
  waiting for transfers between devices  8.64 us (6%)
  between operations  2.83 us (2%)
    ppermute x17, starting transfers between devices, exchange(): return lax.ppermute(x, axis, [(i, i ^ distance) for i in range(size)])  35.9 us
    pallas_call x2, Pallas kernels, left_sum(): call(functools.partial(left_kernel, plan=tuple(plan), out_index=None), ja...  16.3 us
    unnamed x46, local copies, waits for them, and re-layouts  11.7 us
    all_to_all x1, blocking collectives, local(): lax.all_to_all(spread, 'energy', 0, 0, tiled=True)  11.2 us
    ppermute x4, starting transfers between devices, shift(): return lax.ppermute(x, axis, [(i, i + by) for i in range(size - by)])  9.79 us
    concatenate x1, other arithmetic, local(): jnp.concatenate((jnp.concatenate((inverse[0], -inverse[1]), axis=1), jnp....  9.61 us
    pallas_call x1, Pallas kernels, far_matrices(): call(far_matrices_kernel, [pair, pair], [SMEM] + [VMEM] * 5, [pltpu.VMEM(...  9.09 us
    ppermute x17, waiting for transfers between devices, exchange(): return lax.ppermute(x, axis, [(i, i ^ distance) for i in range(size)])  8.62 us
  transfers between devices with their start and end apart: 21, of which 7 were waited for; matrix products, arithmetic and copies ran while one was open for 12% of the time, Pallas kernels for 21%

profile of v1, /device:TPU:0, one launch (start us, length us, event | category | flops | bytes accessed | tf_op | source)
XLA Modules:
  0.0 134.5 jit_solution(12453421280494546312)
XLA Ops:
  1.2 5.6 %collective-permute-start.18 = (bf16[1024,512]{1,0:T(8,128)(2,1)}, bf16[1024,512]{1,0:T(8,128)(2,1)}, u32[]{:S(2)}, u32[]{:S(2)}) collective-permute-start(bf16[1024,512]{1,0:T(8,128)(2,1)} %bitcast.38), channel_id=1, source_target_pairs={{0,2},{1,3},{4,6},{5,7},{8,10},{9,11},{12,14},{13,15},{16,18},{17,... | collective-permute-start | bytes 3145736 | tf_op jit(solution)/shard_map/ppermute | solution.py:266
  6.7 2.1 %dynamic-slice_bitcast_fusion = (bf16[2,64,512]{2,1,0:T(8,128)(2,1)}, bf16[2,64,512]{2,1,0:T(8,128)(2,1)}, bf16[2,64,512]{2,1,0:T(8,128)(2,1)S(1)}, bf16[2,64,51...) fusion(bf16[1,1,2,512,512]{4,3,2,1,0:T(8,128)(2,1)} %param.9, ...), kind=kLoop, calls=%fused_computation.11 | loop fusion | bytes 2097184 | tf_op jit(solution)/shard_map/dynamic_slice | solution.py:295
  8.8 1.5 %collective-permute-start = (bf16[2,64,512]{2,1,0:T(8,128)(2,1)S(1)}, bf16[2,64,512]{2,1,0:T(8,128)(2,1)S(1)}, u32[]{:S(2)}, u32[]{:S(2)}) collective-permute-start(bf16[2,64,512]{2,1,0:T(8,128)(2,1)S(1)} %get-tuple-element.41), channel_id=1, source_target_pairs={{0,4},{4,0},{8,12},{12,8},{16,20},{20,16},{24,28},{28,24},{1,5},{5... | collective-permute-start | bytes 393224 | tf_op jit(solution)/shard_map/ppermute | solution.py:261
  10.3 1.6 %collective-permute-start.1 = (bf16[2,64,512]{2,1,0:T(8,128)(2,1)S(1)}, bf16[2,64,512]{2,1,0:T(8,128)(2,1)S(1)}, u32[]{:S(2)}, u32[]{:S(2)}) collective-permute-start(bf16[2,64,512]{2,1,0:T(8,128)(2,1)S(1)} %get-tuple-element.40), channel_id=1, source_target_pairs={{0,8},{4,12},{8,0},{12,4},{16,24},{20,28},{24,16},{28,20},{1,9},{5... | collective-permute-start | bytes 393224 | tf_op jit(solution)/shard_map/ppermute | solution.py:261
  12.3 1.3 slice_bitcast_fusion
  13.6 0.7 collective-permute-done.refs_1_
  14.3 2.6 %collective-permute-start.3 = (bf16[2,64,512]{2,1,0:T(8,128)(2,1)S(1)}, bf16[2,64,512]{2,1,0:T(8,128)(2,1)S(1)}, u32[]{:S(2)}, u32[]{:S(2)}) collective-permute-start(bf16[2,64,512]{2,1,0:T(8,128)(2,1)S(1)} %get-tuple-element.38), channel_id=1, source_target_pairs={{0,16},{4,20},{8,24},{12,28},{16,0},{20,4},{24,8},{28,12},{1,17},{... | collective-permute-start | bytes 393224 | tf_op jit(solution)/shard_map/ppermute | solution.py:261
  16.9 0.6 copy-done.6
  17.6 1.7 %collective-permute-start.4 = (bf16[2,64,512]{2,1,0:T(8,128)(2,1)}, bf16[2,64,512]{2,1,0:T(8,128)(2,1)}, u32[]{:S(2)}, u32[]{:S(2)}) collective-permute-start(bf16[2,64,512]{2,1,0:T(8,128)(2,1)} %get-tuple-element.37), channel_id=1, source_target_pairs={{0,20},{4,16},{8,28},{12,24},{16,4},{20,0},{24,12},{28,8},{1,21},{... | collective-permute-start | bytes 393224 | tf_op jit(solution)/shard_map/ppermute | solution.py:261
  19.7 0.6 copy-done.8
  20.3 2.8 %collective-permute-start.5 = (bf16[2,64,512]{2,1,0:T(8,128)(2,1)}, bf16[2,64,512]{2,1,0:T(8,128)(2,1)}, u32[]{:S(2)}, u32[]{:S(2)}) collective-permute-start(bf16[2,64,512]{2,1,0:T(8,128)(2,1)} %get-tuple-element.43), channel_id=1, source_target_pairs={{0,24},{4,28},{8,16},{12,20},{16,8},{20,12},{24,0},{28,4},{1,25},{... | collective-permute-start | bytes 393224 | tf_op jit(solution)/shard_map/ppermute | solution.py:261
  23.1 0.7 copy-done.10
  23.8 9.9 %collective-permute-start.6 = (bf16[2,64,512]{2,1,0:T(8,128)(2,1)}, bf16[2,64,512]{2,1,0:T(8,128)(2,1)}, u32[]{:S(2)}, u32[]{:S(2)}) collective-permute-start(bf16[2,64,512]{2,1,0:T(8,128)(2,1)} %get-tuple-element.36), channel_id=1, source_target_pairs={{0,28},{4,24},{8,20},{12,16},{16,12},{20,8},{24,4},{28,0},{1,29},{... | collective-permute-start | bytes 393224 | tf_op jit(solution)/shard_map/ppermute | solution.py:261
  33.7 9.6 %fusion.1 = (bf16[1024,1024]{1,0:T(8,128)(2,1)}, bf16[1024,1024]{1,0:T(8,128)(2,1)S(1)}) fusion(bf16[512,512]{1,0:T(8,128)(2,1)S(1)} %get-tuple-element.45, bf16[512,512]{1,0:T(8,128)(2,1)S(1)} %get-tuple-element.44, bf16[512,512]{1,0:T(8,128)(2,1)S(1)} %fusion.2), kind=kLoop, calls=%fused_computation.5 | loop fusion | flops 14680064 | bytes 5767168 | tf_op jit(solution)/shard_map/concatenate | solution.py:308
  43.3 0.9 copy-done.5
  44.2 0.9 copy-done.7
  45.1 0.9 copy-done.9
  46.0 0.9 copy-done.11
  46.9 2.8 %shard_map.104 = (bf16[64,1024]{1,0:T(8,128)(2,1)S(1)}, bf16[64,1024]{1,0:T(8,128)(2,1)S(1)}, bf16[64,1024]{1,0:T(8,128)(2,1)S(1)}, bf16[64,1024]{1,0:T(8,128)(2...) custom-call(s32[1]{0:T(128)} %bitcast.3.place_ref, ...), custom_call_target="tpu_custom_call" | custom-call | flops 100663296 | bytes 2097152 | tf_op jit(solution)/shard_map/pallas_call | solution.py:77
  50.4 0.7 copy-done.15
  51.0 0.6 copy-done.16
  51.7 0.6 copy-done.17
  52.3 0.6 copy-done.18
  53.0 0.7 copy-done.19
  53.6 0.6 copy-done.20
  54.3 0.8 collective-permute-start.12
  55.3 3.6 %collective-permute-start.13 = (bf16[64,1024]{1,0:T(8,128)(2,1)}, bf16[64,1024]{1,0:T(8,128)(2,1)S(1)}, u32[]{:S(2)}, u32[]{:S(2)}) collective-permute-start(bf16[64,1024]{1,0:T(8,128)(2,1)} %copy-done.20), channel_id=1, source_target_pairs={{0,28},{4,24},{8,20},{12,16},{16,12},{20,8},{24,4},{28,0},{1,29},{... | collective-permute-start | bytes 393224 | tf_op jit(solution)/shard_map/ppermute | solution.py:261
  58.9 3.5 %collective-permute-done.12.refs_0_ = bf16[64,1024]{1,0:T(8,128)(2,1)S(1)} collective-permute-done((bf16[64,1024]{1,0:T(8,128)(2,1)}, bf16[64,1024]{1,0:T(8,128)(2,1)S(1)}, u32[]{:S(2)}, u32[]{:S(2)}) %collective-permute-start.12) | collective-permute-done | bytes 131104 | tf_op jit(solution)/shard_map/ppermute | solution.py:261
  62.4 0.8 collective-permute-start.11
  64.7 0.8 collective-permute-done.13.refs_1_
  65.5 9.3 %collective-permute-start.7 = (bf16[64,1024]{1,0:T(8,128)(2,1)}, bf16[64,1024]{1,0:T(8,128)(2,1)S(1)}, u32[]{:S(2)}, u32[]{:S(2)}) collective-permute-start(bf16[64,1024]{1,0:T(8,128)(2,1)} %copy-done.17), channel_id=1, source_target_pairs={{0,4},{4,0},{8,12},{12,8},{16,20},{20,16},{24,28},{28,24},{1,5},{5... | collective-permute-start | bytes 393224 | tf_op jit(solution)/shard_map/ppermute | solution.py:261
  75.6 1.7 %collective-permute-done.11.refs_1_ = bf16[64,1024]{1,0:T(8,128)(2,1)} collective-permute-done((bf16[64,1024]{1,0:T(8,128)(2,1)}, bf16[64,1024]{1,0:T(8,128)(2,1)}, u32[]{:S(2)}, u32[]{:S(2)}) %collective-permute-start.11) | collective-permute-done | bytes 131104 | tf_op jit(solution)/shard_map/ppermute | solution.py:261
  77.4 1.0 shard_map.107.refs_2_
  78.4 1.5 %shard_map.106.refs_1_ = bf16[128,1024]{1,0:T(8,128)(2,1)S(1)} custom-call(s32[2]{0:T(128)S(1)} %pad_add_fusion.2.place_ref, f32[2]{0:T(128)S(1)} %pad_maximum_fusion.4.scalar_ref, bf16[1024,1024]{1,0:T(8,128)(2,1)S(1)} %get-tuple-element.35.right_ref, bf16[2,512,512]{2,1,0:T(8,128)(2,1)S(1)} %bitcast.40, bf16[64,1024]{1,0:T(8,128)(2,1)} %collective-permute-done.10.refs_0_, ...), custom_call_target="tpu_custom_call" | custom-call | flops 268435456 | bytes 2097152 | tf_op jit(solution)/shard_map/pallas_call | solution.py:116
  79.9 1.4 %collective-permute-start.16 = (bf16[128,1024]{1,0:T(8,128)(2,1)S(1)}, bf16[128,1024]{1,0:T(8,128)(2,1)S(1)}, u32[]{:S(2)}, u32[]{:S(2)}) collective-permute-start(bf16[128,1024]{1,0:T(8,128)(2,1)S(1)} %shard_map.107.refs_2_), channel_id=1, source_target_pairs={{0,2},{1,3},{4,6},{5,7},{8,10},{9,11},{12,14},{13,15},{16,18},{17,... | collective-permute-start | bytes 786440 | tf_op jit(solution)/shard_map/ppermute | solution.py:266
  81.3 1.3 collective-permute-start.15
  82.7 1.0 collective-permute-done.9.refs_3_
  83.7 1.3 shard_map.105.refs_0_
  85.0 1.5 %collective-permute-start.14 = (bf16[256,1024]{1,0:T(8,128)(2,1)S(1)}, bf16[256,1024]{1,0:T(8,128)(2,1)S(1)}, u32[]{:S(2)}, u32[]{:S(2)}) collective-permute-start(bf16[256,1024]{1,0:T(8,128)(2,1)S(1)} %shard_map.105.refs_0_), channel_id=1, source_target_pairs={{0,2},{1,3},{4,6},{5,7},{8,10},{9,11},{12,14},{13,15},{16,18},{17,... | collective-permute-start | bytes 1572872 | tf_op jit(solution)/shard_map/ppermute | solution.py:266
  86.5 1.4 %broadcast_select_fusion.1 = (bf16[1024,512]{1,0:T(8,128)(2,1)S(1)}, bf16[1024,512]{1,0:T(8,128)(2,1)S(1)}) fusion(bf16[1024,512]{1,0:T(8,128)(2,1)} %collective-permute-done.17, pred[]{:T(512)S(6)} %eq.2, bf16[1,2,512,512]{3,2,1,0:T(8,128)(2,1)S(1)} %copy-done), kind=kLoop, calls=%fused_computation.7 | loop fusion | flops 1048576 | bytes 4194305 | tf_op jit(solution)/shard_map/jit(_where)/select_n | solution.py:300
  87.9 4.6 %shard_map.108 = (bf16[1024,512]{1,0:T(8,128)(2,1)S(1)}, bf16[1024,1024]{1,0:T(8,128)(2,1)}, bf16[1024,1024]{1,0:T(8,128)(2,1)}) custom-call(s32[1]{0:T(128)} %bitcast.18.core_ref, bf16[1024,512]{1,0:T(8,128)(2,1)S(1)} %get-tuple-element.33.low_ref, bf16[1024,512]{1,0:T(8,128)(2,1)S(1)} %get-tuple-element.32.high_ref, bf16[1024,512]{1,0:T(8,128)(2,1)S(1)} %bitcast.42, ...), custom_call_target="tpu_custom_call" | custom-call | flops 2147483648 | bytes 7340032 | tf_op jit(solution)/shard_map/pallas_call | solution.py:144
  92.4 1.3 broadcast_select_fusion.far_high_ref
  93.8 1.6 %copy-done.21 = bf16[1024,1024]{1,0:T(8,128)(2,1)S(1)} copy-done((bf16[1024,1024]{1,0:T(8,128)(2,1)S(1)}, bf16[1024,1024]{1,0:T(8,128)(2,1)}, u32[]{:S(2)}) %copy-start.21) | copy-done | bytes 2097176
  95.4 9.1 %shard_map.109 = (bf16[2,1024,1024]{2,1,0:T(8,128)(2,1)}, bf16[2,1024,1024]{2,1,0:T(8,128)(2,1)}) custom-call(s32[1]{0:T(128)} %bitcast.18.core_ref, bf16[1024,512]{1,0:T(8,128)(2,1)S(1)} %get-tuple-element.25.chain_ref, bf16[1024,512]{1,0:T(8,128)(2,1)S(1)} %broadcast_select_fusion.far_high_ref, bf16[1024,512]{1,0:T(8,128)(2,1)} %collective-permute-done.18.far_self_ref, ...), custom_call_target="tpu_custom_call" | custom-call | flops 4831838208 | bytes 7340032 | tf_op jit(solution)/shard_map/pallas_call | solution.py:179
  104.5 8.7 %shard_map.111 = bf16[1024,512]{1,0:T(8,128)(2,1)S(1)} custom-call(s32[3]{0:T(128)S(1)} %pad_add_fusion.bases_ref, bf16[256,1024]{1,0:T(8,128)(2,1)S(1)} %shard_map.105.refs_0_, bf16[128,1024]{1,0:T(8,128)(2,1)S(1)} %shard_map.106.refs_1_, bf16[128,1024]{1,0:T(8,128)(2,1)S(1)} %shard_map.107.refs_2_, bf16[1024,1024]{1,0:T(8,128)(2,1)S(1)} %copy-done.22, ...), custom_call_target="tpu_custom_call" | custom-call | flops 4294967296 | bytes 8388608 | tf_op jit(solution)/shard_map/pallas_call | solution.py:229
  113.9 7.7 %shard_map.110.own_ref = f32[1024,512]{1,0:T(8,128)S(1)} custom-call(s32[3]{0:T(128)S(1)} %pad_add_fusion.bases_ref, bf16[256,1024]{1,0:T(8,128)(2,1)S(1)} %shard_map.105.refs_0_, bf16[128,1024]{1,0:T(8,128)(2,1)S(1)} %shard_map.106.refs_1_, bf16[128,1024]{1,0:T(8,128)(2,1)S(1)} %shard_map.107.refs_2_, bf16[1024,1024]{1,0:T(8,128)(2,1)} %get-tuple-element.34.refs_3_, ...), custom_call_target="tpu_custom_call" | custom-call | flops 4294967296 | bytes 8388608 | tf_op jit(solution)/shard_map/pallas_call | solution.py:229
  121.6 1.1 shard_map.112
  122.7 11.2 %all_to_all.5 = f32[8,1,512]{2,1,0:T(1,128)S(1)} all-to-all(f32[8,1,512]{2,1,0:T(1,128)S(1)} %broadcast_in_dim.14), channel_id=1, replica_groups=mesh['energy'=8,'slab'=4] {'energy'}, dimensions={0} | all-to-all | bytes 32768 | tf_op jit(solution)/shard_map/all_to_all | solution.py:373
  (63 shorter events, 4.0 us)
Async XLA Ops:
  0.6 16.2 %copy-start = (bf16[1,2,512,512]{3,2,1,0:T(8,128)(2,1)S(1)}, bf16[1,2,512,512]{3,2,1,0:T(8,128)(2,1)}, u32[]{:S(2)}) copy-start(bf16[1,2,512,512]{3,2,1,0:T(8,128)(2,1)} %param.10) | copy-start | bytes 3145732
  0.6 85.8 %collective-permute-start.17 = (bf16[1024,512]{1,0:T(8,128)(2,1)}, bf16[1024,512]{1,0:T(8,128)(2,1)}, u32[]{:S(2)}, u32[]{:S(2)}) collective-permute-start(bf16[1024,512]{1,0:T(8,128)(2,1)} %bitcast.37), channel_id=1, source_target_pairs={{0,1},{1,0},{2,3},{3,2},{4,5},{5,4},{6,7},{7,6},{8,9},{9,8},{10,11... | collective-permute-start | bytes 3145736 | tf_op jit(solution)/shard_map/ppermute | solution.py:261
  1.2 54.0 %collective-permute-start.18 = (bf16[1024,512]{1,0:T(8,128)(2,1)}, bf16[1024,512]{1,0:T(8,128)(2,1)}, u32[]{:S(2)}, u32[]{:S(2)}) collective-permute-start(bf16[1024,512]{1,0:T(8,128)(2,1)} %bitcast.38), channel_id=1, source_target_pairs={{0,2},{1,3},{4,6},{5,7},{8,10},{9,11},{12,14},{13,15},{16,18},{17,... | collective-permute-start | bytes 3145736 | tf_op jit(solution)/shard_map/ppermute | solution.py:266
  8.8 5.5 %collective-permute-start = (bf16[2,64,512]{2,1,0:T(8,128)(2,1)S(1)}, bf16[2,64,512]{2,1,0:T(8,128)(2,1)S(1)}, u32[]{:S(2)}, u32[]{:S(2)}) collective-permute-start(bf16[2,64,512]{2,1,0:T(8,128)(2,1)S(1)} %get-tuple-element.41), channel_id=1, source_target_pairs={{0,4},{4,0},{8,12},{12,8},{16,20},{20,16},{24,28},{28,24},{1,5},{5... | collective-permute-start | bytes 393224 | tf_op jit(solution)/shard_map/ppermute | solution.py:261
  10.3 6.6 %collective-permute-start.1 = (bf16[2,64,512]{2,1,0:T(8,128)(2,1)S(1)}, bf16[2,64,512]{2,1,0:T(8,128)(2,1)S(1)}, u32[]{:S(2)}, u32[]{:S(2)}) collective-permute-start(bf16[2,64,512]{2,1,0:T(8,128)(2,1)S(1)} %get-tuple-element.40), channel_id=1, source_target_pairs={{0,8},{4,12},{8,0},{12,4},{16,24},{20,28},{24,16},{28,20},{1,9},{5... | collective-permute-start | bytes 393224 | tf_op jit(solution)/shard_map/ppermute | solution.py:261
  11.9 31.4 %copy-start.1 = (bf16[4,64,512]{2,1,0:T(8,128)(2,1)S(1)}, bf16[4,64,512]{2,1,0:T(8,128)(2,1)}, u32[]{:S(2)}) copy-start(bf16[4,64,512]{2,1,0:T(8,128)(2,1)} %phonon_ref.1) | copy-start | bytes 786436
  11.9 31.4 %copy-start.12 = (s32[8,6]{1,0:T(8,128)S(1)}, s32[8,6]{1,0:T(8,128)}, u32[]{:S(2)}) copy-start(s32[8,6]{1,0:T(8,128)} %source_ref.1) | copy-start | bytes 580
  11.9 31.4 %copy-start.13 = (s32[8,6]{1,0:T(8,128)S(1)}, s32[8,6]{1,0:T(8,128)}, u32[]{:S(2)}) copy-start(s32[8,6]{1,0:T(8,128)} %mode_ref.1) | copy-start | bytes 580
  11.9 7.8 %collective-permute-start.2 = (bf16[2,64,512]{2,1,0:T(8,128)(2,1)S(1)}, bf16[2,64,512]{2,1,0:T(8,128)(2,1)S(1)}, u32[]{:S(2)}, u32[]{:S(2)}) collective-permute-start(bf16[2,64,512]{2,1,0:T(8,128)(2,1)S(1)} %get-tuple-element.39), channel_id=1, source_target_pairs={{0,12},{4,8},{8,4},{12,0},{16,28},{20,24},{24,20},{28,16},{1,13},{... | collective-permute-start | bytes 393224 | tf_op jit(solution)/shard_map/ppermute | solution.py:261
  14.3 19.4 %copy-start.4 = (bf16[2,64,512]{2,1,0:T(8,128)(2,1)}, bf16[2,64,512]{2,1,0:T(8,128)(2,1)S(1)}, u32[]{:S(2)}) copy-start(bf16[2,64,512]{2,1,0:T(8,128)(2,1)S(1)} %collective-permute-done.refs_1_) | copy-start | bytes 393220
  14.3 8.9 %collective-permute-start.3 = (bf16[2,64,512]{2,1,0:T(8,128)(2,1)S(1)}, bf16[2,64,512]{2,1,0:T(8,128)(2,1)S(1)}, u32[]{:S(2)}, u32[]{:S(2)}) collective-permute-start(bf16[2,64,512]{2,1,0:T(8,128)(2,1)S(1)} %get-tuple-element.38), channel_id=1, source_target_pairs={{0,16},{4,20},{8,24},{12,28},{16,0},{20,4},{24,8},{28,12},{1,17},{... | collective-permute-start | bytes 393224 | tf_op jit(solution)/shard_map/ppermute | solution.py:261
  16.9 0.7 copy-start.6
  17.6 25.7 %collective-permute-start.4 = (bf16[2,64,512]{2,1,0:T(8,128)(2,1)}, bf16[2,64,512]{2,1,0:T(8,128)(2,1)}, u32[]{:S(2)}, u32[]{:S(2)}) collective-permute-start(bf16[2,64,512]{2,1,0:T(8,128)(2,1)} %get-tuple-element.37), channel_id=1, source_target_pairs={{0,20},{4,16},{8,28},{12,24},{16,4},{20,0},{24,12},{28,8},{1,21},{... | collective-permute-start | bytes 393224 | tf_op jit(solution)/shard_map/ppermute | solution.py:261
  19.7 0.7 copy-start.8
  20.3 23.0 %collective-permute-start.5 = (bf16[2,64,512]{2,1,0:T(8,128)(2,1)}, bf16[2,64,512]{2,1,0:T(8,128)(2,1)}, u32[]{:S(2)}, u32[]{:S(2)}) collective-permute-start(bf16[2,64,512]{2,1,0:T(8,128)(2,1)} %get-tuple-element.43), channel_id=1, source_target_pairs={{0,24},{4,28},{8,16},{12,20},{16,8},{20,12},{24,0},{28,4},{1,25},{... | collective-permute-start | bytes 393224 | tf_op jit(solution)/shard_map/ppermute | solution.py:261
  23.1 0.7 copy-start.10
  23.8 19.5 %collective-permute-start.6 = (bf16[2,64,512]{2,1,0:T(8,128)(2,1)}, bf16[2,64,512]{2,1,0:T(8,128)(2,1)}, u32[]{:S(2)}, u32[]{:S(2)}) collective-permute-start(bf16[2,64,512]{2,1,0:T(8,128)(2,1)} %get-tuple-element.36), channel_id=1, source_target_pairs={{0,28},{4,24},{8,20},{12,16},{16,12},{20,8},{24,4},{28,0},{1,29},{... | collective-permute-start | bytes 393224 | tf_op jit(solution)/shard_map/ppermute | solution.py:261
  43.3 0.9 copy-start.5
  44.2 0.9 copy-start.7
  45.1 0.9 copy-start.9
  46.0 0.9 copy-start.11
  49.7 0.6 copy-start.2
  50.4 0.7 copy-start.15
  51.0 0.6 copy-start.16
  51.7 0.6 copy-start.17
  52.3 0.6 copy-start.18
  53.0 0.7 copy-start.19
  53.6 0.6 copy-start.20
  54.3 29.4 %copy-start.3 = (bf16[64,1024]{1,0:T(8,128)(2,1)S(1)}, bf16[64,1024]{1,0:T(8,128)(2,1)}, u32[]{:S(2)}) copy-start(bf16[64,1024]{1,0:T(8,128)(2,1)} %copy-done.2) | copy-start | bytes 393220
  54.3 8.1 %collective-permute-start.12 = (bf16[64,1024]{1,0:T(8,128)(2,1)}, bf16[64,1024]{1,0:T(8,128)(2,1)S(1)}, u32[]{:S(2)}, u32[]{:S(2)}) collective-permute-start(bf16[64,1024]{1,0:T(8,128)(2,1)} %get-tuple-element.23), channel_id=1, source_target_pairs={{0,24},{4,28},{8,16},{12,20},{16,8},{20,12},{24,0},{28,4},{1,25},{... | collective-permute-start | bytes 393224 | tf_op jit(solution)/shard_map/ppermute | solution.py:261
  55.2 37.3 %collective-permute-start.19 = (bf16[1024,512]{1,0:T(8,128)(2,1)}, bf16[1024,512]{1,0:T(8,128)(2,1)}, u32[]{:S(2)}, u32[]{:S(2)}) collective-permute-start(bf16[1024,512]{1,0:T(8,128)(2,1)} %collective-permute-done.18.far_self_ref), channel_id=1, source_target_pairs={{0,1},{1,0},{2,3},{3,2},{4,5},{5,4},{6,7},{7,6},{8,9},{9,8},{10,11... | collective-permute-start | bytes 3145736 | tf_op jit(solution)/shard_map/ppermute | solution.py:261
  55.3 10.2 %collective-permute-start.13 = (bf16[64,1024]{1,0:T(8,128)(2,1)}, bf16[64,1024]{1,0:T(8,128)(2,1)S(1)}, u32[]{:S(2)}, u32[]{:S(2)}) collective-permute-start(bf16[64,1024]{1,0:T(8,128)(2,1)} %copy-done.20), channel_id=1, source_target_pairs={{0,28},{4,24},{8,20},{12,16},{16,12},{20,8},{24,4},{28,0},{1,29},{... | collective-permute-start | bytes 393224 | tf_op jit(solution)/shard_map/ppermute | solution.py:261
  58.9 16.3 %collective-permute-start.10 = (bf16[64,1024]{1,0:T(8,128)(2,1)}, bf16[64,1024]{1,0:T(8,128)(2,1)}, u32[]{:S(2)}, u32[]{:S(2)}) collective-permute-start(bf16[64,1024]{1,0:T(8,128)(2,1)} %copy-done.19), channel_id=1, source_target_pairs={{0,16},{4,20},{8,24},{12,28},{16,0},{20,4},{24,8},{28,12},{1,17},{... | collective-permute-start | bytes 393224 | tf_op jit(solution)/shard_map/ppermute | solution.py:261
  62.4 14.9 %collective-permute-start.11 = (bf16[64,1024]{1,0:T(8,128)(2,1)}, bf16[64,1024]{1,0:T(8,128)(2,1)}, u32[]{:S(2)}, u32[]{:S(2)}) collective-permute-start(bf16[64,1024]{1,0:T(8,128)(2,1)} %copy-done.18), channel_id=1, source_target_pairs={{0,20},{4,16},{8,28},{12,24},{16,4},{20,0},{24,12},{28,8},{1,21},{... | collective-permute-start | bytes 393224 | tf_op jit(solution)/shard_map/ppermute | solution.py:261
  65.5 14.4 %collective-permute-start.7 = (bf16[64,1024]{1,0:T(8,128)(2,1)}, bf16[64,1024]{1,0:T(8,128)(2,1)S(1)}, u32[]{:S(2)}, u32[]{:S(2)}) collective-permute-start(bf16[64,1024]{1,0:T(8,128)(2,1)} %copy-done.17), channel_id=1, source_target_pairs={{0,4},{4,0},{8,12},{12,8},{16,20},{20,16},{24,28},{28,24},{1,5},{5... | collective-permute-start | bytes 393224 | tf_op jit(solution)/shard_map/ppermute | solution.py:261
  75.2 6.1 %collective-permute-start.8 = (bf16[64,1024]{1,0:T(8,128)(2,1)}, bf16[64,1024]{1,0:T(8,128)(2,1)S(1)}, u32[]{:S(2)}, u32[]{:S(2)}) collective-permute-start(bf16[64,1024]{1,0:T(8,128)(2,1)} %copy-done.16), channel_id=1, source_target_pairs={{0,8},{4,12},{8,0},{12,4},{16,24},{20,28},{24,16},{28,20},{1,9},{5... | collective-permute-start | bytes 393224 | tf_op jit(solution)/shard_map/ppermute | solution.py:261
  77.3 6.4 %collective-permute-start.9 = (bf16[64,1024]{1,0:T(8,128)(2,1)}, bf16[64,1024]{1,0:T(8,128)(2,1)S(1)}, u32[]{:S(2)}, u32[]{:S(2)}) collective-permute-start(bf16[64,1024]{1,0:T(8,128)(2,1)} %copy-done.15), channel_id=1, source_target_pairs={{0,12},{4,8},{8,4},{12,0},{16,28},{20,24},{24,20},{28,16},{1,13},{... | collective-permute-start | bytes 393224 | tf_op jit(solution)/shard_map/ppermute | solution.py:261
  79.9 24.6 %collective-permute-start.16 = (bf16[128,1024]{1,0:T(8,128)(2,1)S(1)}, bf16[128,1024]{1,0:T(8,128)(2,1)S(1)}, u32[]{:S(2)}, u32[]{:S(2)}) collective-permute-start(bf16[128,1024]{1,0:T(8,128)(2,1)S(1)} %shard_map.107.refs_2_), channel_id=1, source_target_pairs={{0,2},{1,3},{4,6},{5,7},{8,10},{9,11},{12,14},{13,15},{16,18},{17,... | collective-permute-start | bytes 786440 | tf_op jit(solution)/shard_map/ppermute | solution.py:266
  81.3 23.1 %collective-permute-start.15 = (bf16[128,1024]{1,0:T(8,128)(2,1)S(1)}, bf16[128,1024]{1,0:T(8,128)(2,1)S(1)}, u32[]{:S(2)}, u32[]{:S(2)}) collective-permute-start(bf16[128,1024]{1,0:T(8,128)(2,1)S(1)} %shard_map.106.refs_1_), channel_id=1, source_target_pairs={{0,2},{1,3},{4,6},{5,7},{8,10},{9,11},{12,14},{13,15},{16,18},{17,... | collective-permute-start | bytes 786440 | tf_op jit(solution)/shard_map/ppermute | solution.py:266
  83.7 4.2 %copy-start.14 = (bf16[512,512]{1,0:T(8,128)(2,1)S(1)}, bf16[512,512]{1,0:T(8,128)(2,1)}, u32[]{:S(2)}) copy-start(bf16[512,512]{1,0:T(8,128)(2,1)} %coupling_ref.3) | copy-start | bytes 1572868
  85.0 19.5 %collective-permute-start.14 = (bf16[256,1024]{1,0:T(8,128)(2,1)S(1)}, bf16[256,1024]{1,0:T(8,128)(2,1)S(1)}, u32[]{:S(2)}, u32[]{:S(2)}) collective-permute-start(bf16[256,1024]{1,0:T(8,128)(2,1)S(1)} %shard_map.105.refs_0_), channel_id=1, source_target_pairs={{0,2},{1,3},{4,6},{5,7},{8,10},{9,11},{12,14},{13,15},{16,18},{17,... | collective-permute-start | bytes 1572872 | tf_op jit(solution)/shard_map/ppermute | solution.py:266
  93.8 1.6 %copy-start.21 = (bf16[1024,1024]{1,0:T(8,128)(2,1)S(1)}, bf16[1024,1024]{1,0:T(8,128)(2,1)}, u32[]{:S(2)}) copy-start(bf16[1024,1024]{1,0:T(8,128)(2,1)} %get-tuple-element.26.high_embed.refs_3_) | copy-start | bytes 6291460
  95.4 9.1 %copy-start.22 = (bf16[1024,1024]{1,0:T(8,128)(2,1)S(1)}, bf16[1024,1024]{1,0:T(8,128)(2,1)}, u32[]{:S(2)}) copy-start(bf16[1024,1024]{1,0:T(8,128)(2,1)} %get-tuple-element.26.high_embed.refs_3_) | copy-start | bytes 6291460
  113.2 8.4 %collective-permute-start.20 = (bf16[1024,512]{1,0:T(8,128)(2,1)S(1)}, bf16[1024,512]{1,0:T(8,128)(2,1)S(1)}, u32[]{:S(2)}, u32[]{:S(2)}) collective-permute-start(bf16[1024,512]{1,0:T(8,128)(2,1)S(1)} %shard_map.111), channel_id=1, source_target_pairs={{0,1},{1,0},{2,3},{3,2},{4,5},{5,4},{6,7},{7,6},{8,9},{9,8},{10,11... | collective-permute-start | bytes 3145736 | tf_op jit(solution)/shard_map/ppermute | solution.py:261

commit v2 on v0

v2 whole, which is shorter than its diff:
```python
import functools

import jax
import jax.numpy as jnp
from jax import lax
from jax.experimental import pallas as pl
from jax.experimental.pallas import tpu as pltpu
from jax.sharding import PartitionSpec as P

BF16 = jnp.bfloat16
F32 = jnp.float32
VMEM = pl.BlockSpec(memory_space=pltpu.VMEM)
SMEM = pl.BlockSpec(memory_space=pltpu.SMEM)


def mxu(first, second):
    return jnp.dot(first, second, preferred_element_type=F32)


def mxu_nt(first, second):
    return lax.dot_general(first, second, (((1,), (1,)), ((), ())), preferred_element_type=F32)


def call(kernel, out_shape, in_specs, scratch=(), out_specs=None, flops=0, bytes_accessed=0, vmem=16):
    return pl.pallas_call(
        kernel,
        out_shape=out_shape,
        in_specs=in_specs,
        out_specs=jax.tree.map(lambda _: VMEM, out_shape) if out_specs is None else out_specs,
        scratch_shapes=list(scratch),
        compiler_params=pltpu.CompilerParams(vmem_limit_bytes=vmem * 2**20),
        cost_estimate=pl.CostEstimate(flops=flops, bytes_accessed=bytes_accessed, transcendentals=0),
    )


def complex_of(by_real, by_imag):
    rows = by_real.shape[0] // 2
    return by_real[:rows] - by_imag[rows:], by_real[rows:] + by_imag[:rows]


def product(first, second):
    rows = second.shape[0] // 2
    return complex_of(mxu(first, second[:rows]), mxu(first, second[rows:]))


def store(ref, parts):
    rows = parts[0].shape[0]
    for index, part in enumerate(parts):
        ref[index * rows : (index + 1) * rows, :] = part.astype(ref.dtype)


def mix_kernel(place_ref, source_ref, mode_ref, phonon_ref, *refs):
    energies = (len(refs) - 2) // 2
    pieces, outs = refs[:energies], refs[energies : 2 * energies]
    green, phonon = refs[2 * energies :]
    place = place_ref[0]
    pairs = source_ref.shape[1]
    rows, n = phonon_ref.shape[1:]
    phonon[...] = phonon_ref[...].astype(F32)
    for distance in range(energies):
        green[distance] = pieces[distance][...].astype(F32)
    step = 16

    @pl.loop(0, rows // step)
    def _(block):
        at = pl.ds(pl.multiple_of(block * step, step), step)
        for distance in range(energies):
            energy = place ^ distance
            real = jnp.zeros((step, n), F32)
            imag = jnp.zeros((step, n), F32)
            for pair in range(pairs):
                origin = source_ref[energy, pair] ^ place
                factor = phonon[mode_ref[energy, pair], at, :]
                real = real + factor * green[origin, 0, at, :]
                imag = imag + factor * green[origin, 1, at, :]
            outs[distance][0, at, :] = real.astype(BF16)
            outs[distance][1, at, :] = imag.astype(BF16)


def mix(place, source, mode, phonon, pieces):
    energies = len(pieces)
    _, rows, n = pieces[0].shape
    return call(
        mix_kernel,
        [jax.ShapeDtypeStruct((2, rows, n), BF16)] * energies,
        [SMEM] * 3 + [VMEM] * (energies + 1),
        [pltpu.VMEM((energies, 2, rows, n), F32), pltpu.VMEM(phonon.shape, F32)],
        flops=energies * 24 * rows * n * 16,
        bytes_accessed=energies * rows * n * 8,
        vmem=12,
    )(place, source, mode, phonon, *pieces)


def right_kernel(place_ref, slab_ref, active_ref, offset_ref, inverse_ref, *refs, first):
    pieces, out_ref, rows_ref = refs[:-2], refs[-2], refs[-1]
    count = len(pieces)
    place = place_ref[0] ^ first
    rows, n = pieces[0].shape[1:]
    total = count * rows
    for index, piece in enumerate(pieces):
        at = (place ^ index) & (count - 1)
        for part in range(2):
            rows_ref[pl.ds(pl.multiple_of(part * total + at * rows, rows), rows), :] = piece[part]
    mask = jnp.where(slab_ref[0] < active_ref[0], 1.0, 0.0)
    offset = offset_ref[0]
    start = pl.multiple_of(place // count * total, total)
    eye = (
        lax.broadcasted_iota(jnp.int32, (total, n), 0) + start
        == lax.broadcasted_iota(jnp.int32, (total, n), 1)
    ).astype(F32)
    real, imag = product(rows_ref[...], inverse_ref[...])
    own_real = inverse_ref[pl.ds(start, total), :].astype(F32)
    own_imag = inverse_ref[pl.ds(pl.multiple_of(n + start, total), total), :].astype(F32)
    store(out_ref, (mask * real + offset * own_real + eye, mask * imag + offset * own_imag))


def right_rows(scalars, inverse, pieces, first):
    _, rows, n = pieces[0].shape
    total = rows * len(pieces)
    return call(
        functools.partial(right_kernel, first=first),
        jax.ShapeDtypeStruct((2 * total, n), BF16),
        [SMEM] * 4 + [VMEM] * (1 + len(pieces)),
        [pltpu.VMEM((2 * total, n), BF16)],
        flops=8 * total * n * n,
        bytes_accessed=8 * n * n,
        vmem=12,
    )(*scalars, inverse, *pieces)


def own_matrices_kernel(slab_ref, self_ref, partner_ref, coupling_ref, low_ref, high_ref, factor_ref, both):
    core = slab_ref[0] & 1
    both[core] = self_ref[...]
    both[1 - core] = partner_ref[...]
    coupling = coupling_ref[...]
    low_ref[...] = mxu(both[0], coupling).astype(BF16)
    high_ref[...] = mxu(both[1], coupling).astype(BF16)

    @pl.when(core == 0)
    def _():
        store(factor_ref, product(high_ref[...], self_ref[...]))

    @pl.when(core != 0)
    def _():
        factor_ref[...] = jnp.zeros_like(factor_ref)


def own_matrices(slab, own, partner, coupling):
    n = coupling.shape[0]
    matrix = jax.ShapeDtypeStruct((2 * n, n), BF16)
    return call(
        own_matrices_kernel,
        [matrix, matrix, matrix],
        [SMEM] + [VMEM] * 3,
        [pltpu.VMEM((2, 2 * n, n), BF16)],
        flops=16 * n**3,
        bytes_accessed=14 * n * n,
        vmem=20,
    )(slab, own, partner, coupling)


def far_matrices_kernel(slab_ref, chain_ref, self_ref, partner_ref, coupling_ref, high_ref, moves, factors):
    core = slab_ref[0] & 1
    low, high = core, 1 - core

    @pl.when(core == 0)
    def _():
        far_high = mxu(partner_ref[...], coupling_ref[...]).astype(BF16)
        store(moves.at[low], product(chain_ref[...], far_high))

    @pl.when(core != 0)
    def _():
        moves[low] = chain_ref[...]

    store(moves.at[high], product(high_ref[...], moves[low]))
    for place in range(2):
        store(factors.at[place], product(moves[place], self_ref[...]))


def far_matrices(slab, chain, far_self, far_partner, coupling, high):
    n = coupling.shape[0]
    pair = jax.ShapeDtypeStruct((2, 2 * n, n), BF16)
    return call(
        far_matrices_kernel,
        [pair, pair],
        [SMEM] + [VMEM] * 5,
        flops=36 * n**3,
        bytes_accessed=20 * n * n,
        vmem=20,
    )(slab, chain, far_self, far_partner, coupling, high)


def block_of(place, first, size, n, energies):
    return (place ^ first) // (size * energies // n)


def moved_term(rows, move, factor):
    n = move.shape[0] // 2
    moved = complex_of(mxu_nt(rows, move[:n]), mxu_nt(rows, move[n:]))
    moved = [part.astype(BF16) for part in moved]
    return complex_of(mxu(factor, moved[0]), mxu(factor, moved[1]))


def own_terms_kernel(place_ref, high_ref, own_ref, factor_ref, *refs, firsts, energies):
    chunks, (self_ref, partner_ref, rows_ref) = refs[:-3], refs[-3:]
    n = self_ref.shape[1]
    for index, chunk in enumerate(chunks):
        size = chunk.shape[0] // 2
        for part in range(2):
            start = pl.multiple_of(part * n + block_of(place_ref[0], firsts[index], size, n, energies) * size, size)
            rows_ref[pl.ds(start, size), :] = chunk[part * size : (part + 1) * size, :]
    store(partner_ref, moved_term(rows_ref[...], high_ref[...], factor_ref[...]))
    store(self_ref, product(own_ref[...], rows_ref[...]))


def own_terms(place, high, own, factor, chunks, firsts, energies):
    n = own.shape[1]
    total = jax.ShapeDtypeStruct((2 * n, n), F32)
    return call(
        functools.partial(own_terms_kernel, firsts=tuple(firsts), energies=energies),
        [total, total],
        [SMEM] + [VMEM] * (3 + len(chunks)),
        [pltpu.VMEM((2 * n, n), BF16)],
        flops=24 * n**3,
        bytes_accessed=28 * n * n,
        vmem=20,
    )(place, high, own, factor, *chunks)


def far_terms_kernel(place_ref, total_ref, *refs, target, firsts, energies):
    count = len(firsts)
    out_ref, refs = refs[-1], refs[:-1]
    n = total_ref.shape[1]
    total = [total_ref[:n, :], total_ref[n:, :]]
    for term in range(len(refs) // (count + 2)):
        group = refs[term * (count + 2) : (term + 1) * (count + 2)]
        moves, factors = group[count].at[target], group[count + 1].at[target]
        for index in range(count):
            block = group[index]
            size = block.shape[0] // 2
            start = pl.multiple_of(block_of(place_ref[0], firsts[index], size, n, energies) * size, size)
            parts = moved_term(block[...], moves[...], factors[:, pl.ds(start, size)])
            total = [a + b for a, b in zip(total, parts)]
    store(out_ref, total)


def far_terms(place, total, terms, firsts, target, dtype, energies):
    n = total.shape[1]
    arrays = [array for chunks, moves, factors in terms for array in (*chunks, moves, factors)]
    rows = sum(chunk.shape[0] // 2 for chunk in terms[0][0])
    return call(
        functools.partial(far_terms_kernel, target=target, firsts=tuple(firsts), energies=energies),
        jax.ShapeDtypeStruct((2 * n, n), dtype),
        [SMEM] + [VMEM] * (1 + len(arrays)),
        flops=16 * n**2 * rows * len(terms),
        bytes_accessed=16 * n * n * len(terms),
        vmem=20 + 5 * (len(terms) - 1),
    )(place, total, *arrays)


def finish_kernel(scalar_ref, own_ref, partner_ref, green_ref, density_ref):
    n = own_ref.shape[1]
    green = (own_ref[...] + partner_ref[...].astype(F32)).astype(BF16)
    green_ref[...] = green
    eye = lax.broadcasted_iota(jnp.int32, (n, n), 0) == lax.broadcasted_iota(jnp.int32, (n, n), 1)
    diagonal = jnp.sum(jnp.where(eye, green[n:].astype(F32), 0.0), axis=0, keepdims=True)
    density_ref[...] = -scalar_ref[0] * diagonal


def finish(scalars, own, partner):
    n = own.shape[1]
    return call(
        finish_kernel,
        [jax.ShapeDtypeStruct((2 * n, n), BF16), jax.ShapeDtypeStruct((1, n), F32)],
        [SMEM, VMEM, VMEM],
        flops=8 * n * n,
        bytes_accessed=16 * n * n,
    )(scalars, own, partner)


def exchange(x, axis, distance):
    size = lax.axis_size(axis)
    return lax.ppermute(x, axis, [(i, i ^ distance) for i in range(size)])


def shift(x, axis, by):
    size = lax.axis_size(axis)
    return lax.ppermute(x, axis, [(i, i + by) for i in range(size - by)])


def after(x, *others):
    return lax.optimization_barrier((x, *others))[0]


def exchange_all(pieces, window):
    received = [pieces[0]]
    for distance in range(1, len(pieces)):
        piece = pieces[distance]
        if distance > window:
            piece = after(piece, received[distance - window])
        received.append(exchange(piece, "energy", distance))
    return received


def complex_columns(first, second, n):
    real, imag = first[:n], first[n:]
    dot = functools.partial(jnp.dot, preferred_element_type=F32)
    return jnp.concatenate(
        (
            dot(real, second[:n]) - dot(imag, second[n:]),
            dot(real, second[n:]) + dot(imag, second[:n]),
        ),
        axis=0,
    ).astype(BF16)


def local(
    green_prev,
    slab_inverse,
    coupling_block,
    phonon_coupling,
    offset,
    occupation,
    pair_source,
    pair_mode,
    active_slabs,
):
    energies = pair_source.shape[0]
    n = coupling_block.shape[0]
    rows = n // energies
    slabs = lax.axis_size("slab")
    place = lax.axis_index("energy").astype(jnp.int32)
    slab = lax.axis_index("slab").astype(jnp.int32)
    core = slab & 1
    place_one = place[None]
    slab_one = slab[None]
    column = slab_inverse[0].reshape(2 * n, n)
    green = green_prev[0, 0]

    sent = [
        lax.dynamic_slice_in_dim(green, (place ^ distance) * rows, rows, axis=1)
        for distance in range(energies)
    ]
    pieces = exchange_all(sent, 4)

    partner = exchange(column, "slab", 1)
    low_move, high_move, own_factor = own_matrices(slab_one, column, partner, coupling_block)
    far_selves = [shift(column, "slab", back) for back in range(2, slabs, 2)]

    pieces[-1] = after(pieces[-1], high_move)
    mixed = mix(place_one, pair_source, pair_mode, phonon_coupling, pieces)
    back = exchange_all(mixed, 4)

    far_blocks = []
    for far_self in far_selves:
        far_self = after(far_self, mixed[1])
        far_blocks.append((far_self, exchange(far_self, "slab", 1)))
    far = []
    chain = after(low_move, back[2])
    for far_self, far_partner in far_blocks:
        if far:
            far_self_old, far_partner_old = far_blocks[len(far) - 1]
            high = jnp.where(core == 0, far_partner_old, far_self_old)
            low = jnp.where(core == 0, far_self_old, far_partner_old)
            for block in (high, low):
                step = jnp.dot(block, coupling_block, preferred_element_type=F32).astype(BF16)
                chain = complex_columns(chain, step, n)
        far.append(far_matrices(slab_one, chain, far_self, far_partner, coupling_block, high_move))

    scalars = (place_one, slab_one, active_slabs, offset)
    groups = [(0, energies // 2), (energies // 2, 3 * energies // 4), (3 * energies // 4, energies)]
    firsts = [first for first, _ in groups]
    if far:
        back[-1] = after(back[-1], far[-1][0])
    own_chunks = [right_rows(scalars, column, back[first:last], first) for first, last in groups]
    far_chunks = [
        [shift(chunk, "slab", 2 * (index + 1)) for chunk in own_chunks] for index in range(len(far))
    ]
    for_self, for_partner = own_terms(place_one, high_move, column, own_factor, own_chunks, firsts, energies)
    for first, last in ((0, 1), (1, 3)):
        terms = [(chunks[first:last], *matrices) for chunks, matrices in zip(far_chunks, far)]
        if terms:
            far_of = functools.partial(far_terms, place_one, terms=terms, firsts=firsts[first:last], energies=energies)
            for_partner = far_of(total=for_partner, target=1, dtype=F32 if first == 0 else BF16)
            for_self = far_of(total=for_self, target=0, dtype=F32)
    from_partner = exchange(for_partner.astype(BF16), "slab", 1)
    current, terms = finish(occupation, for_self, from_partner)
    spread = jnp.broadcast_to(terms[None], (energies, 1, n))
    density = jnp.sum(lax.all_to_all(spread, "energy", 0, 0, tiled=True), axis=0)
    return (current.reshape(1, 1, 2, n, n), density)


def solution(mesh):
    in_specs = (
        P("energy", "slab", None, None, None),
        P("slab", None, None, None),
        P(),
        P(None, "energy", None),
        P("energy"),
        P("energy"),
        P(),
        P(),
        P("energy"),
    )
    out_specs = (P("energy", "slab", None, None, None), P("slab", None))
    return jax.shard_map(local, mesh=mesh, in_specs=in_specs, out_specs=out_specs, check_vma=False)
```

time: 166 us -> 103 us (0.62)
  the two profiles are of different devices: /device:TPU:2 before, /device:TPU:0 now
where the time goes in v2:
time: 103 us; the launch traced here: 102 us
  starting transfers between devices  38.9 us (38%)
  Pallas kernels  24.4 us (24%)
  waiting for transfers between devices  23.9 us (23%)
  blocking collectives  9.59 us (9%)
  between operations  2.89 us (3%)
  local copies, waits for them, and re-layouts  2.17 us (2%)
    ppermute x17, starting transfers between devices, exchange(): return lax.ppermute(x, axis, [(i, i ^ distance) for i in range(size)])  29.1 us
    ppermute x17, waiting for transfers between devices, exchange(): return lax.ppermute(x, axis, [(i, i ^ distance) for i in range(size)])  21 us
    ppermute x4, starting transfers between devices, shift(): return lax.ppermute(x, axis, [(i, i + by) for i in range(size - by)])  9.76 us
    all_to_all x1, blocking collectives, local(): lax.all_to_all(spread, 'energy', 0, 0, tiled=True)  9.59 us
    pallas_call x4, Pallas kernels, far_terms(): call(functools.partial(far_terms_kernel, target=target, firsts=tuple(firs...  7.15 us
    pallas_call x1, Pallas kernels, far_matrices(): call(far_matrices_kernel, [pair, pair], [SMEM] + [VMEM] * 5, flops=36 * n...  5.23 us
    pallas_call x1, Pallas kernels, own_matrices(): call(own_matrices_kernel, [matrix, matrix, matrix], [SMEM] + [VMEM] * 3,...  3.81 us
    pallas_call x1, Pallas kernels, own_terms(): call(functools.partial(own_terms_kernel, firsts=tuple(firsts), energies=e...  3.54 us
  transfers between devices with their start and end apart: 21, of which 6 were waited for; matrix products, arithmetic and copies ran while one was open for 2% of the time, Pallas kernels for 21%

profile of v2, /device:TPU:0, one launch (start us, length us, event | category | flops | bytes accessed | tf_op | source)
XLA Modules:
  0.0 102.3 jit_solution(13932098416560541457)
XLA Ops:
  0.6 0.5 collective-permute-start
  1.2 4.6 %collective-permute-start.15 = (bf16[1024,512]{1,0:T(8,128)(2,1)}, bf16[1024,512]{1,0:T(8,128)(2,1)S(1)}, u32[]{:S(2)}, u32[]{:S(2)}) collective-permute-start(bf16[1024,512]{1,0:T(8,128)(2,1)} %bitcast.23), channel_id=1, source_target_pairs={{0,2},{1,3},{4,6},{5,7},{8,10},{9,11},{12,14},{13,15},{16,18},{17,... | collective-permute-start | bytes 3145736 | tf_op jit(solution)/shard_map/ppermute | solution.py:288
  5.8 2.1 %dynamic-slice_bitcast_fusion = (bf16[2,64,512]{2,1,0:T(8,128)(2,1)}, bf16[2,64,512]{2,1,0:T(8,128)(2,1)S(1)}, bf16[2,64,512]{2,1,0:T(8,128)(2,1)S(1)}, bf16[2,6...) fusion(bf16[1,1,2,512,512]{4,3,2,1,0:T(8,128)(2,1)} %param.9, ...), kind=kLoop, calls=%fused_computation | loop fusion | bytes 2097184 | tf_op jit(solution)/shard_map/dynamic_slice | solution.py:341
  8.0 2.5 %collective-permute-start.3 = (bf16[2,64,512]{2,1,0:T(8,128)(2,1)}, bf16[2,64,512]{2,1,0:T(8,128)(2,1)S(1)}, u32[]{:S(2)}, u32[]{:S(2)}) collective-permute-start(bf16[2,64,512]{2,1,0:T(8,128)(2,1)} %get-tuple-element.59), channel_id=1, source_target_pairs={{0,12},{4,8},{8,4},{12,0},{16,28},{20,24},{24,20},{28,16},{1,13},{... | collective-permute-start | bytes 393224 | tf_op jit(solution)/shard_map/ppermute | solution.py:283
  10.5 0.5 collective-permute-start.1
  11.0 0.4 collective-permute-start.2
  11.4 3.3 %collective-permute-done.3.refs_3_ = bf16[2,64,512]{2,1,0:T(8,128)(2,1)S(1)} collective-permute-done((bf16[2,64,512]{2,1,0:T(8,128)(2,1)}, bf16[2,64,512]{2,1,0:T(8,128)(2,1)S(1)}, u32[]{:S(2)}, u32[]{:S(2)}) %collective-permute-start.3) | collective-permute-done | bytes 131104 | tf_op jit(solution)/shard_map/ppermute | solution.py:283
  14.7 2.6 %collective-permute-start.4 = (bf16[2,64,512]{2,1,0:T(8,128)(2,1)S(1)}, bf16[2,64,512]{2,1,0:T(8,128)(2,1)S(1)}, u32[]{:S(2)}, u32[]{:S(2)}) collective-permute-start(bf16[2,64,512]{2,1,0:T(8,128)(2,1)S(1)} %get-tuple-element.58), channel_id=1, source_target_pairs={{0,16},{4,20},{8,24},{12,28},{16,0},{20,4},{24,8},{28,12},{1,17},{... | collective-permute-start | bytes 393224 | tf_op jit(solution)/shard_map/ppermute | solution.py:283
  17.3 0.0 collective-permute-done.1.refs_1_
  17.3 3.8 %collective-permute-start.7 = (bf16[2,64,512]{2,1,0:T(8,128)(2,1)}, bf16[2,64,512]{2,1,0:T(8,128)(2,1)S(1)}, u32[]{:S(2)}, u32[]{:S(2)}) collective-permute-start(bf16[2,64,512]{2,1,0:T(8,128)(2,1)} %get-tuple-element.33), channel_id=1, source_target_pairs={{0,28},{4,24},{8,20},{12,16},{16,12},{20,8},{24,4},{28,0},{1,29},{... | collective-permute-start | bytes 393224 | tf_op jit(solution)/shard_map/ppermute | solution.py:283
  21.1 0.0 collective-permute-done.2.refs_2_
  21.1 0.9 collective-permute-start.5
  22.0 0.0 collective-permute-done.partner_ref
  22.0 1.8 %collective-permute-start.6 = (bf16[2,64,512]{2,1,0:T(8,128)(2,1)S(1)}, bf16[2,64,512]{2,1,0:T(8,128)(2,1)S(1)}, u32[]{:S(2)}, u32[]{:S(2)}) collective-permute-start(bf16[2,64,512]{2,1,0:T(8,128)(2,1)S(1)} %get-tuple-element.32), channel_id=1, source_target_pairs={{0,24},{4,28},{8,16},{12,20},{16,8},{20,12},{24,0},{28,4},{1,25},{... | collective-permute-start | bytes 393224 | tf_op jit(solution)/shard_map/ppermute | solution.py:283
  23.8 0.0 copy-start.3
  23.8 3.8 %shard_map.104 = (bf16[1024,512]{1,0:T(8,128)(2,1)S(1)}, bf16[1024,512]{1,0:T(8,128)(2,1)S(1)}, bf16[1024,512]{1,0:T(8,128)(2,1)S(1)}) custom-call(s32[1]{0:T(128)} %bitcast.1.slab_ref, bf16[1024,512]{1,0:T(8,128)(2,1)S(1)} %bitcast.24, bf16[1024,512]{1,0:T(8,128)(2,1)} %collective-permute-done.partner_ref, bf16[512,512]{1,0:T(8,128)(2,1)S(1)} %copy-done.4), custom_call_target="tpu_custom_call" | custom-call | flops 2147483648 | bytes 3670016 | tf_op jit(solution)/shard_map/pallas_call | solution.py:151
  27.6 0.0 collective-permute-done.7.refs_7_
  27.6 4.6 %collective-permute-done.4.refs_4_ = bf16[2,64,512]{2,1,0:T(8,128)(2,1)S(1)} collective-permute-done((bf16[2,64,512]{2,1,0:T(8,128)(2,1)S(1)}, bf16[2,64,512]{2,1,0:T(8,128)(2,1)S(1)}, u32[]{:S(2)}, u32[]{:S(2)}) %collective-permute-start.4) | collective-permute-done | bytes 131104 | tf_op jit(solution)/shard_map/ppermute | solution.py:283
  32.2 6.1 %collective-permute-done.5.refs_5_ = bf16[2,64,512]{2,1,0:T(8,128)(2,1)S(1)} collective-permute-done((bf16[2,64,512]{2,1,0:T(8,128)(2,1)S(1)}, bf16[2,64,512]{2,1,0:T(8,128)(2,1)S(1)}, u32[]{:S(2)}, u32[]{:S(2)}) %collective-permute-start.5) | collective-permute-done | bytes 131104 | tf_op jit(solution)/shard_map/ppermute | solution.py:283
  38.3 1.8 %shard_map.105 = (bf16[2,64,512]{2,1,0:T(8,128)(2,1)S(1)}, bf16[2,64,512]{2,1,0:T(8,128)(2,1)S(1)}, bf16[2,64,512]{2,1,0:T(8,128)(2,1)S(1)}, bf16[2,64,512]{2,1,...) custom-call(s32[1]{0:T(128)} %bitcast.place_ref, ...), custom_call_target="tpu_custom_call" | custom-call | flops 100663296 | bytes 2097152 | tf_op jit(solution)/shard_map/pallas_call | solution.py:83
  40.1 0.1 collective-permute-start.16
  40.2 1.0 %collective-permute-start.8 = (bf16[2,64,512]{2,1,0:T(8,128)(2,1)S(1)}, bf16[2,64,512]{2,1,0:T(8,128)(2,1)S(1)}, u32[]{:S(2)}, u32[]{:S(2)}) collective-permute-start(bf16[2,64,512]{2,1,0:T(8,128)(2,1)S(1)} %get-tuple-element.36), channel_id=1, source_target_pairs={{0,4},{4,0},{8,12},{12,8},{16,20},{20,16},{24,28},{28,24},{1,5},{5... | collective-permute-start | bytes 393224 | tf_op jit(solution)/shard_map/ppermute | solution.py:283
  41.3 2.6 %collective-permute-start.9 = (bf16[2,64,512]{2,1,0:T(8,128)(2,1)S(1)}, bf16[2,64,512]{2,1,0:T(8,128)(2,1)S(1)}, u32[]{:S(2)}, u32[]{:S(2)}) collective-permute-start(bf16[2,64,512]{2,1,0:T(8,128)(2,1)S(1)} %get-tuple-element.37), channel_id=1, source_target_pairs={{0,8},{4,12},{8,0},{12,4},{16,24},{20,28},{24,16},{28,20},{1,9},{5... | collective-permute-start | bytes 393224 | tf_op jit(solution)/shard_map/ppermute | solution.py:283
  43.9 0.1 collective-permute-start.10
  43.9 3.9 %collective-permute-start.11 = (bf16[2,64,512]{2,1,0:T(8,128)(2,1)S(1)}, bf16[2,64,512]{2,1,0:T(8,128)(2,1)S(1)}, u32[]{:S(2)}, u32[]{:S(2)}) collective-permute-start(bf16[2,64,512]{2,1,0:T(8,128)(2,1)S(1)} %get-tuple-element.39), channel_id=1, source_target_pairs={{0,16},{4,20},{8,24},{12,28},{16,0},{20,4},{24,8},{28,12},{1,17},{... | collective-permute-start | bytes 393224 | tf_op jit(solution)/shard_map/ppermute | solution.py:283
  47.9 3.2 %collective-permute-start.12 = (bf16[2,64,512]{2,1,0:T(8,128)(2,1)S(1)}, bf16[2,64,512]{2,1,0:T(8,128)(2,1)S(1)}, u32[]{:S(2)}, u32[]{:S(2)}) collective-permute-start(bf16[2,64,512]{2,1,0:T(8,128)(2,1)S(1)} %get-tuple-element.41), channel_id=1, source_target_pairs={{0,20},{4,16},{8,28},{12,24},{16,4},{20,0},{24,12},{28,8},{1,21},{... | collective-permute-start | bytes 393224 | tf_op jit(solution)/shard_map/ppermute | solution.py:283
  52.4 2.7 %collective-permute-done.10.refs_3_ = bf16[2,64,512]{2,1,0:T(8,128)(2,1)S(1)} collective-permute-done((bf16[2,64,512]{2,1,0:T(8,128)(2,1)S(1)}, bf16[2,64,512]{2,1,0:T(8,128)(2,1)S(1)}, u32[]{:S(2)}, u32[]{:S(2)}) %collective-permute-start.10) | collective-permute-done | bytes 131104 | tf_op jit(solution)/shard_map/ppermute | solution.py:283
  55.1 2.5 %collective-permute-start.14 = (bf16[2,64,512]{2,1,0:T(8,128)(2,1)S(1)}, bf16[2,64,512]{2,1,0:T(8,128)(2,1)S(1)}, u32[]{:S(2)}, u32[]{:S(2)}) collective-permute-start(bf16[2,64,512]{2,1,0:T(8,128)(2,1)S(1)} %get-tuple-element.45), channel_id=1, source_target_pairs={{0,28},{4,24},{8,20},{12,16},{16,12},{20,8},{24,4},{28,0},{1,29},{... | collective-permute-start | bytes 393224 | tf_op jit(solution)/shard_map/ppermute | solution.py:283
  57.6 2.5 %collective-permute-start.13 = (bf16[2,64,512]{2,1,0:T(8,128)(2,1)S(1)}, bf16[2,64,512]{2,1,0:T(8,128)(2,1)S(1)}, u32[]{:S(2)}, u32[]{:S(2)}) collective-permute-start(bf16[2,64,512]{2,1,0:T(8,128)(2,1)S(1)} %get-tuple-element.43), channel_id=1, source_target_pairs={{0,24},{4,28},{8,16},{12,20},{16,8},{20,12},{24,0},{28,4},{1,25},{... | collective-permute-start | bytes 393224 | tf_op jit(solution)/shard_map/ppermute | solution.py:283
  60.2 0.8 shard_map.106.refs_0_
  61.0 0.0 collective-permute-done.11.refs_0_
  61.0 1.9 %collective-permute-start.17 = (bf16[512,512]{1,0:T(8,128)(2,1)S(1)}, bf16[512,512]{1,0:T(8,128)(2,1)S(1)}, u32[]{:S(2)}, u32[]{:S(2)}) collective-permute-start(bf16[512,512]{1,0:T(8,128)(2,1)S(1)} %shard_map.106.refs_0_), channel_id=1, source_target_pairs={{0,2},{1,3},{4,6},{5,7},{8,10},{9,11},{12,14},{13,15},{16,18},{17,... | collective-permute-start | bytes 1572872 | tf_op jit(solution)/shard_map/ppermute | solution.py:288
  62.9 4.3 %collective-permute-done.12.refs_1_ = bf16[2,64,512]{2,1,0:T(8,128)(2,1)S(1)} collective-permute-done((bf16[2,64,512]{2,1,0:T(8,128)(2,1)S(1)}, bf16[2,64,512]{2,1,0:T(8,128)(2,1)S(1)}, u32[]{:S(2)}, u32[]{:S(2)}) %collective-permute-start.12) | collective-permute-done | bytes 131104 | tf_op jit(solution)/shard_map/ppermute | solution.py:283
  67.1 0.4 shard_map.107.refs_1_
  67.6 1.8 %collective-permute-start.18 = (bf16[256,512]{1,0:T(8,128)(2,1)S(1)}, bf16[256,512]{1,0:T(8,128)(2,1)S(1)}, u32[]{:S(2)}, u32[]{:S(2)}) collective-permute-start(bf16[256,512]{1,0:T(8,128)(2,1)S(1)} %shard_map.107.refs_1_), channel_id=1, source_target_pairs={{0,2},{1,3},{4,6},{5,7},{8,10},{9,11},{12,14},{13,15},{16,18},{17,... | collective-permute-start | bytes 786440 | tf_op jit(solution)/shard_map/ppermute | solution.py:288
  69.4 5.2 %shard_map.108 = (bf16[2,1024,512]{2,1,0:T(8,128)(2,1)S(1)}, bf16[2,1024,512]{2,1,0:T(8,128)(2,1)S(1)}) custom-call(s32[1]{0:T(128)} %bitcast.1.slab_ref, bf16[1024,512]{1,0:T(8,128)(2,1)S(1)} %get-tuple-element.47.chain_ref, bf16[1024,512]{1,0:T(8,128)(2,1)S(1)} %collective-permute-done.15.self_ref, ...), custom_call_target="tpu_custom_call" | custom-call | flops 4831838208 | bytes 5242880 | tf_op jit(solution)/shard_map/pallas_call | solution.py:183
  74.6 0.5 shard_map.109.refs_2_
  75.1 1.5 %collective-permute-start.19 = (bf16[256,512]{1,0:T(8,128)(2,1)S(1)}, bf16[256,512]{1,0:T(8,128)(2,1)S(1)}, u32[]{:S(2)}, u32[]{:S(2)}) collective-permute-start(bf16[256,512]{1,0:T(8,128)(2,1)S(1)} %shard_map.109.refs_2_), channel_id=1, source_target_pairs={{0,2},{1,3},{4,6},{5,7},{8,10},{9,11},{12,14},{13,15},{16,18},{17,... | collective-permute-start | bytes 786440 | tf_op jit(solution)/shard_map/ppermute | solution.py:288
  76.6 3.5 %shard_map.110 = (f32[1024,512]{1,0:T(8,128)S(1)}, f32[1024,512]{1,0:T(8,128)S(1)}) custom-call(s32[1]{0:T(128)} %bitcast.place_ref, bf16[1024,512]{1,0:T(8,128)(2,1)S(1)} %get-tuple-element.29.high_ref, bf16[1024,512]{1,0:T(8,128)(2,1)S(1)} %bitcast.28, bf16[1024,512]{1,0:T(8,128)(2,1)S(1)} %get-tuple-element.30.factor_ref, ...), custom_call_target="tpu_custom_call" | custom-call | flops 3221225472 | bytes 7340032 | tf_op jit(solution)/shard_map/pallas_call | solution.py:219
  80.2 1.4 %shard_map.113.total_ref = f32[1024,512]{1,0:T(8,128)S(1)} custom-call(s32[1]{0:T(128)} %bitcast.place_ref, f32[1024,512]{1,0:T(8,128)S(1)} %get-tuple-element.53.total_ref, bf16[512,512]{1,0:T(8,128)(2,1)S(1)} %collective-permute-done.17.refs_0_, bf16[2,1024,512]{2,1,0:T(8,128)(2,1)S(1)} %get-tuple-element.49.refs_1_.refs_2_, ...), custom_call_target="tpu_custom_call" | custom-call | flops 1073741824 | bytes 4194304 | tf_op jit(solution)/shard_map/pallas_call | solution.py:251
  81.6 2.9 %collective-permute-done.19.refs_1_ = bf16[256,512]{1,0:T(8,128)(2,1)S(1)} collective-permute-done((bf16[256,512]{1,0:T(8,128)(2,1)S(1)}, bf16[256,512]{1,0:T(8,128)(2,1)S(1)}, u32[]{:S(2)}, u32[]{:S(2)}) %collective-permute-start.19) | collective-permute-done | bytes 262176 | tf_op jit(solution)/shard_map/ppermute | solution.py:288
  84.5 2.1 %shard_map.114 = bf16[1024,512]{1,0:T(8,128)(2,1)S(1)} custom-call(s32[1]{0:T(128)} %bitcast.place_ref, f32[1024,512]{1,0:T(8,128)S(1)} %shard_map.113.total_ref, bf16[256,512]{1,0:T(8,128)(2,1)S(1)} %collective-permute-done.18.refs_0_, bf16[256,512]{1,0:T(8,128)(2,1)S(1)} %collective-permute-done.19.refs_1_, ...), custom_call_target="tpu_custom_call" | custom-call | flops 1073741824 | bytes 4194304 | tf_op jit(solution)/shard_map/pallas_call | solution.py:251
  86.6 0.1 collective-permute-start.20
  87.4 1.4 %shard_map.111.total_ref = f32[1024,512]{1,0:T(8,128)S(1)} custom-call(s32[1]{0:T(128)} %bitcast.place_ref, f32[1024,512]{1,0:T(8,128)S(1)} %get-tuple-element.51.total_ref, bf16[512,512]{1,0:T(8,128)(2,1)S(1)} %collective-permute-done.17.refs_0_, bf16[2,1024,512]{2,1,0:T(8,128)(2,1)S(1)} %get-tuple-element.49.refs_1_.refs_2_, ...), custom_call_target="tpu_custom_call" | custom-call | flops 1073741824 | bytes 4194304 | tf_op jit(solution)/shard_map/pallas_call | solution.py:251
  88.8 2.2 %shard_map.112.own_ref = f32[1024,512]{1,0:T(8,128)S(1)} custom-call(s32[1]{0:T(128)} %bitcast.place_ref, f32[1024,512]{1,0:T(8,128)S(1)} %shard_map.111.total_ref, bf16[256,512]{1,0:T(8,128)(2,1)S(1)} %collective-permute-done.18.refs_0_, bf16[256,512]{1,0:T(8,128)(2,1)S(1)} %collective-permute-done.19.refs_1_, ...), custom_call_target="tpu_custom_call" | custom-call | flops 1073741824 | bytes 4194304 | tf_op jit(solution)/shard_map/pallas_call | solution.py:251
  91.0 1.1 %shard_map.115 = (bf16[1024,512]{1,0:T(8,128)(2,1)}, f32[1,512]{1,0:T(1,128)S(1)}) custom-call(f32[1]{0:T(128)S(6)} %copy.14.scalar_ref, f32[1024,512]{1,0:T(8,128)S(1)} %shard_map.112.own_ref, bf16[1024,512]{1,0:T(8,128)(2,1)S(1)} %collective-permute-done.20.partner_ref), custom_call_target="tpu_custom_call" | custom-call | flops 2097152 | bytes 4194304 | tf_op jit(solution)/shard_map/pallas_call | solution.py:272
  92.1 9.6 %all_to_all.5 = f32[8,1,512]{2,1,0:T(1,128)S(1)} all-to-all(f32[8,1,512]{2,1,0:T(1,128)S(1)} %broadcast_in_dim.17), channel_id=1, replica_groups=mesh['energy'=8,'slab'=4] {'energy'}, dimensions={0} | all-to-all | bytes 32768 | tf_op jit(solution)/shard_map/all_to_all | solution.py:389
  101.7 0.6 reduce_sum.11
  (20 shorter events, 0.1 us)
Async XLA Ops:
  0.6 23.1 %copy-start = (bf16[1,2,512,512]{3,2,1,0:T(8,128)(2,1)S(1)}, bf16[1,2,512,512]{3,2,1,0:T(8,128)(2,1)}, u32[]{:S(2)}) copy-start(bf16[1,2,512,512]{3,2,1,0:T(8,128)(2,1)} %param.10) | copy-start | bytes 3145732
  0.6 23.1 %copy-start.4 = (bf16[512,512]{1,0:T(8,128)(2,1)S(1)}, bf16[512,512]{1,0:T(8,128)(2,1)}, u32[]{:S(2)}) copy-start(bf16[512,512]{1,0:T(8,128)(2,1)} %coupling_ref.3) | copy-start | bytes 1572868
  0.6 21.3 %collective-permute-start = (bf16[1024,512]{1,0:T(8,128)(2,1)}, bf16[1024,512]{1,0:T(8,128)(2,1)}, u32[]{:S(2)}, u32[]{:S(2)}) collective-permute-start(bf16[1024,512]{1,0:T(8,128)(2,1)} %bitcast.22), channel_id=1, source_target_pairs={{0,1},{1,0},{2,3},{3,2},{4,5},{5,4},{6,7},{7,6},{8,9},{9,8},{10,11... | collective-permute-start | bytes 3145736 | tf_op jit(solution)/shard_map/ppermute | solution.py:283
  1.2 39.0 %collective-permute-start.15 = (bf16[1024,512]{1,0:T(8,128)(2,1)}, bf16[1024,512]{1,0:T(8,128)(2,1)S(1)}, u32[]{:S(2)}, u32[]{:S(2)}) collective-permute-start(bf16[1024,512]{1,0:T(8,128)(2,1)} %bitcast.23), channel_id=1, source_target_pairs={{0,2},{1,3},{4,6},{5,7},{8,10},{9,11},{12,14},{13,15},{16,18},{17,... | collective-permute-start | bytes 3145736 | tf_op jit(solution)/shard_map/ppermute | solution.py:288
  8.0 6.8 %collective-permute-start.3 = (bf16[2,64,512]{2,1,0:T(8,128)(2,1)}, bf16[2,64,512]{2,1,0:T(8,128)(2,1)S(1)}, u32[]{:S(2)}, u32[]{:S(2)}) collective-permute-start(bf16[2,64,512]{2,1,0:T(8,128)(2,1)} %get-tuple-element.59), channel_id=1, source_target_pairs={{0,12},{4,8},{8,4},{12,0},{16,28},{20,24},{24,20},{28,16},{1,13},{... | collective-permute-start | bytes 393224 | tf_op jit(solution)/shard_map/ppermute | solution.py:283
  10.5 6.9 %collective-permute-start.1 = (bf16[2,64,512]{2,1,0:T(8,128)(2,1)}, bf16[2,64,512]{2,1,0:T(8,128)(2,1)S(1)}, u32[]{:S(2)}, u32[]{:S(2)}) collective-permute-start(bf16[2,64,512]{2,1,0:T(8,128)(2,1)} %get-tuple-element.61), channel_id=1, source_target_pairs={{0,4},{4,0},{8,12},{12,8},{16,20},{20,16},{24,28},{28,24},{1,5},{5... | collective-permute-start | bytes 393224 | tf_op jit(solution)/shard_map/ppermute | solution.py:283
  11.0 10.1 %collective-permute-start.2 = (bf16[2,64,512]{2,1,0:T(8,128)(2,1)}, bf16[2,64,512]{2,1,0:T(8,128)(2,1)S(1)}, u32[]{:S(2)}, u32[]{:S(2)}) collective-permute-start(bf16[2,64,512]{2,1,0:T(8,128)(2,1)} %get-tuple-element.60), channel_id=1, source_target_pairs={{0,8},{4,12},{8,0},{12,4},{16,24},{20,28},{24,16},{28,20},{1,9},{5... | collective-permute-start | bytes 393224 | tf_op jit(solution)/shard_map/ppermute | solution.py:283
  14.7 17.5 %collective-permute-start.4 = (bf16[2,64,512]{2,1,0:T(8,128)(2,1)S(1)}, bf16[2,64,512]{2,1,0:T(8,128)(2,1)S(1)}, u32[]{:S(2)}, u32[]{:S(2)}) collective-permute-start(bf16[2,64,512]{2,1,0:T(8,128)(2,1)S(1)} %get-tuple-element.58), channel_id=1, source_target_pairs={{0,16},{4,20},{8,24},{12,28},{16,0},{20,4},{24,8},{28,12},{1,17},{... | collective-permute-start | bytes 393224 | tf_op jit(solution)/shard_map/ppermute | solution.py:283
  17.3 10.3 %collective-permute-start.7 = (bf16[2,64,512]{2,1,0:T(8,128)(2,1)}, bf16[2,64,512]{2,1,0:T(8,128)(2,1)S(1)}, u32[]{:S(2)}, u32[]{:S(2)}) collective-permute-start(bf16[2,64,512]{2,1,0:T(8,128)(2,1)} %get-tuple-element.33), channel_id=1, source_target_pairs={{0,28},{4,24},{8,20},{12,16},{16,12},{20,8},{24,4},{28,0},{1,29},{... | collective-permute-start | bytes 393224 | tf_op jit(solution)/shard_map/ppermute | solution.py:283
  21.1 17.2 %collective-permute-start.5 = (bf16[2,64,512]{2,1,0:T(8,128)(2,1)S(1)}, bf16[2,64,512]{2,1,0:T(8,128)(2,1)S(1)}, u32[]{:S(2)}, u32[]{:S(2)}) collective-permute-start(bf16[2,64,512]{2,1,0:T(8,128)(2,1)S(1)} %get-tuple-element.31), channel_id=1, source_target_pairs={{0,20},{4,16},{8,28},{12,24},{16,4},{20,0},{24,12},{28,8},{1,21},{... | collective-permute-start | bytes 393224 | tf_op jit(solution)/shard_map/ppermute | solution.py:283
  22.0 16.3 %collective-permute-start.6 = (bf16[2,64,512]{2,1,0:T(8,128)(2,1)S(1)}, bf16[2,64,512]{2,1,0:T(8,128)(2,1)S(1)}, u32[]{:S(2)}, u32[]{:S(2)}) collective-permute-start(bf16[2,64,512]{2,1,0:T(8,128)(2,1)S(1)} %get-tuple-element.32), channel_id=1, source_target_pairs={{0,24},{4,28},{8,16},{12,20},{16,8},{20,12},{24,0},{28,4},{1,25},{... | collective-permute-start | bytes 393224 | tf_op jit(solution)/shard_map/ppermute | solution.py:283
  23.8 14.5 %copy-start.1 = (bf16[4,64,512]{2,1,0:T(8,128)(2,1)S(1)}, bf16[4,64,512]{2,1,0:T(8,128)(2,1)}, u32[]{:S(2)}) copy-start(bf16[4,64,512]{2,1,0:T(8,128)(2,1)} %phonon_ref.1) | copy-start | bytes 786436
  23.8 14.5 %copy-start.2 = (s32[8,6]{1,0:T(8,128)S(1)}, s32[8,6]{1,0:T(8,128)}, u32[]{:S(2)}) copy-start(s32[8,6]{1,0:T(8,128)} %source_ref.1) | copy-start | bytes 580
  23.8 14.5 %copy-start.3 = (s32[8,6]{1,0:T(8,128)S(1)}, s32[8,6]{1,0:T(8,128)}, u32[]{:S(2)}) copy-start(s32[8,6]{1,0:T(8,128)} %mode_ref.1) | copy-start | bytes 580
  40.1 29.2 %collective-permute-start.16 = (bf16[1024,512]{1,0:T(8,128)(2,1)S(1)}, bf16[1024,512]{1,0:T(8,128)(2,1)S(1)}, u32[]{:S(2)}, u32[]{:S(2)}) collective-permute-start(bf16[1024,512]{1,0:T(8,128)(2,1)S(1)} %collective-permute-done.15.self_ref), channel_id=1, source_target_pairs={{0,1},{1,0},{2,3},{3,2},{4,5},{5,4},{6,7},{7,6},{8,9},{9,8},{10,11... | collective-permute-start | bytes 3145736 | tf_op jit(solution)/shard_map/ppermute | solution.py:283
  40.2 7.6 %collective-permute-start.8 = (bf16[2,64,512]{2,1,0:T(8,128)(2,1)S(1)}, bf16[2,64,512]{2,1,0:T(8,128)(2,1)S(1)}, u32[]{:S(2)}, u32[]{:S(2)}) collective-permute-start(bf16[2,64,512]{2,1,0:T(8,128)(2,1)S(1)} %get-tuple-element.36), channel_id=1, source_target_pairs={{0,4},{4,0},{8,12},{12,8},{16,20},{20,16},{24,28},{28,24},{1,5},{5... | collective-permute-start | bytes 393224 | tf_op jit(solution)/shard_map/ppermute | solution.py:283
  41.3 11.1 %collective-permute-start.9 = (bf16[2,64,512]{2,1,0:T(8,128)(2,1)S(1)}, bf16[2,64,512]{2,1,0:T(8,128)(2,1)S(1)}, u32[]{:S(2)}, u32[]{:S(2)}) collective-permute-start(bf16[2,64,512]{2,1,0:T(8,128)(2,1)S(1)} %get-tuple-element.37), channel_id=1, source_target_pairs={{0,8},{4,12},{8,0},{12,4},{16,24},{20,28},{24,16},{28,20},{1,9},{5... | collective-permute-start | bytes 393224 | tf_op jit(solution)/shard_map/ppermute | solution.py:283
  43.9 11.2 %collective-permute-start.10 = (bf16[2,64,512]{2,1,0:T(8,128)(2,1)S(1)}, bf16[2,64,512]{2,1,0:T(8,128)(2,1)S(1)}, u32[]{:S(2)}, u32[]{:S(2)}) collective-permute-start(bf16[2,64,512]{2,1,0:T(8,128)(2,1)S(1)} %get-tuple-element.38), channel_id=1, source_target_pairs={{0,12},{4,8},{8,4},{12,0},{16,28},{20,24},{24,20},{28,16},{1,13},{... | collective-permute-start | bytes 393224 | tf_op jit(solution)/shard_map/ppermute | solution.py:283
  43.9 17.0 %collective-permute-start.11 = (bf16[2,64,512]{2,1,0:T(8,128)(2,1)S(1)}, bf16[2,64,512]{2,1,0:T(8,128)(2,1)S(1)}, u32[]{:S(2)}, u32[]{:S(2)}) collective-permute-start(bf16[2,64,512]{2,1,0:T(8,128)(2,1)S(1)} %get-tuple-element.39), channel_id=1, source_target_pairs={{0,16},{4,20},{8,24},{12,28},{16,0},{20,4},{24,8},{28,12},{1,17},{... | collective-permute-start | bytes 393224 | tf_op jit(solution)/shard_map/ppermute | solution.py:283
  47.9 19.3 %collective-permute-start.12 = (bf16[2,64,512]{2,1,0:T(8,128)(2,1)S(1)}, bf16[2,64,512]{2,1,0:T(8,128)(2,1)S(1)}, u32[]{:S(2)}, u32[]{:S(2)}) collective-permute-start(bf16[2,64,512]{2,1,0:T(8,128)(2,1)S(1)} %get-tuple-element.41), channel_id=1, source_target_pairs={{0,20},{4,16},{8,28},{12,24},{16,4},{20,0},{24,12},{28,8},{1,21},{... | collective-permute-start | bytes 393224 | tf_op jit(solution)/shard_map/ppermute | solution.py:283
  55.1 19.6 %collective-permute-start.14 = (bf16[2,64,512]{2,1,0:T(8,128)(2,1)S(1)}, bf16[2,64,512]{2,1,0:T(8,128)(2,1)S(1)}, u32[]{:S(2)}, u32[]{:S(2)}) collective-permute-start(bf16[2,64,512]{2,1,0:T(8,128)(2,1)S(1)} %get-tuple-element.45), channel_id=1, source_target_pairs={{0,28},{4,24},{8,20},{12,16},{16,12},{20,8},{24,4},{28,0},{1,29},{... | collective-permute-start | bytes 393224 | tf_op jit(solution)/shard_map/ppermute | solution.py:283
  57.6 17.0 %collective-permute-start.13 = (bf16[2,64,512]{2,1,0:T(8,128)(2,1)S(1)}, bf16[2,64,512]{2,1,0:T(8,128)(2,1)S(1)}, u32[]{:S(2)}, u32[]{:S(2)}) collective-permute-start(bf16[2,64,512]{2,1,0:T(8,128)(2,1)S(1)} %get-tuple-element.43), channel_id=1, source_target_pairs={{0,24},{4,28},{8,16},{12,20},{16,8},{20,12},{24,0},{28,4},{1,25},{... | collective-permute-start | bytes 393224 | tf_op jit(solution)/shard_map/ppermute | solution.py:283
  61.0 19.2 %collective-permute-start.17 = (bf16[512,512]{1,0:T(8,128)(2,1)S(1)}, bf16[512,512]{1,0:T(8,128)(2,1)S(1)}, u32[]{:S(2)}, u32[]{:S(2)}) collective-permute-start(bf16[512,512]{1,0:T(8,128)(2,1)S(1)} %shard_map.106.refs_0_), channel_id=1, source_target_pairs={{0,2},{1,3},{4,6},{5,7},{8,10},{9,11},{12,14},{13,15},{16,18},{17,... | collective-permute-start | bytes 1572872 | tf_op jit(solution)/shard_map/ppermute | solution.py:288
  67.6 14.0 %collective-permute-start.18 = (bf16[256,512]{1,0:T(8,128)(2,1)S(1)}, bf16[256,512]{1,0:T(8,128)(2,1)S(1)}, u32[]{:S(2)}, u32[]{:S(2)}) collective-permute-start(bf16[256,512]{1,0:T(8,128)(2,1)S(1)} %shard_map.107.refs_1_), channel_id=1, source_target_pairs={{0,2},{1,3},{4,6},{5,7},{8,10},{9,11},{12,14},{13,15},{16,18},{17,... | collective-permute-start | bytes 786440 | tf_op jit(solution)/shard_map/ppermute | solution.py:288
  75.1 9.4 %collective-permute-start.19 = (bf16[256,512]{1,0:T(8,128)(2,1)S(1)}, bf16[256,512]{1,0:T(8,128)(2,1)S(1)}, u32[]{:S(2)}, u32[]{:S(2)}) collective-permute-start(bf16[256,512]{1,0:T(8,128)(2,1)S(1)} %shard_map.109.refs_2_), channel_id=1, source_target_pairs={{0,2},{1,3},{4,6},{5,7},{8,10},{9,11},{12,14},{13,15},{16,18},{17,... | collective-permute-start | bytes 786440 | tf_op jit(solution)/shard_map/ppermute | solution.py:288
  86.6 4.3 %collective-permute-start.20 = (bf16[1024,512]{1,0:T(8,128)(2,1)S(1)}, bf16[1024,512]{1,0:T(8,128)(2,1)S(1)}, u32[]{:S(2)}, u32[]{:S(2)}) collective-permute-start(bf16[1024,512]{1,0:T(8,128)(2,1)S(1)} %shard_map.114), channel_id=1, source_target_pairs={{0,1},{1,0},{2,3},{3,2},{4,5},{5,4},{6,7},{7,6},{8,9},{9,8},{10,11... | collective-permute-start | bytes 3145736 | tf_op jit(solution)/shard_map/ppermute | solution.py:283

commit v3 on v2

--- a/solution.py
+++ b/solution.py
@@ -9,6 +9,7 @@
 
 BF16 = jnp.bfloat16
 F32 = jnp.float32
+MICROSECOND = 3_300_000
 VMEM = pl.BlockSpec(memory_space=pltpu.VMEM)
 SMEM = pl.BlockSpec(memory_space=pltpu.SMEM)
 
@@ -21,15 +22,17 @@
     return lax.dot_general(first, second, (((1,), (1,)), ((), ())), preferred_element_type=F32)
 
 
-def call(kernel, out_shape, in_specs, scratch=(), out_specs=None, flops=0, bytes_accessed=0, vmem=16):
+def call(kernel, out_shape, in_specs, scratch=(), vmem=16, cost=0.0):
     return pl.pallas_call(
         kernel,
         out_shape=out_shape,
         in_specs=in_specs,
-        out_specs=jax.tree.map(lambda _: VMEM, out_shape) if out_specs is None else out_specs,
+        out_specs=jax.tree.map(lambda _: VMEM, out_shape),
         scratch_shapes=list(scratch),
         compiler_params=pltpu.CompilerParams(vmem_limit_bytes=vmem * 2**20),
-        cost_estimate=pl.CostEstimate(flops=flops, bytes_accessed=bytes_accessed, transcendentals=0),
+        cost_estimate=pl.CostEstimate(
+            flops=1024, bytes_accessed=1024 + int(cost * MICROSECOND), transcendentals=0
+        ),
     )
 
 
@@ -58,7 +61,7 @@
     rows, n = phonon_ref.shape[1:]
     phonon[...] = phonon_ref[...].astype(F32)
     for distance in range(energies):
-        green[distance] = pieces[distance][...].astype(F32)
+        green[place ^ distance] = pieces[distance][...].astype(F32)
     step = 16
 
     @pl.loop(0, rows // step)
@@ -69,7 +72,7 @@
             real = jnp.zeros((step, n), F32)
             imag = jnp.zeros((step, n), F32)
             for pair in range(pairs):
-                origin = source_ref[energy, pair] ^ place
+                origin = source_ref[energy, pair]
                 factor = phonon[mode_ref[energy, pair], at, :]
                 real = real + factor * green[origin, 0, at, :]
                 imag = imag + factor * green[origin, 1, at, :]
@@ -85,10 +88,20 @@
         [jax.ShapeDtypeStruct((2, rows, n), BF16)] * energies,
         [SMEM] * 3 + [VMEM] * (energies + 1),
         [pltpu.VMEM((energies, 2, rows, n), F32), pltpu.VMEM(phonon.shape, F32)],
-        flops=energies * 24 * rows * n * 16,
-        bytes_accessed=energies * rows * n * 8,
         vmem=12,
+        cost=2.0,
     )(place, source, mode, phonon, *pieces)
+
+
+def arrived_kernel(*refs):
+    refs[-1][...] = jnp.zeros_like(refs[-1])
+
+
+def arrived(*arrays):
+    anywhere = pl.BlockSpec(memory_space=pl.ANY)
+    return call(
+        arrived_kernel, jax.ShapeDtypeStruct((8, 128), F32), [anywhere] * len(arrays), vmem=1, cost=60.0
+    )(*arrays)
 
 
 def right_kernel(place_ref, slab_ref, active_ref, offset_ref, inverse_ref, *refs, first):
@@ -114,7 +127,7 @@
     store(out_ref, (mask * real + offset * own_real + eye, mask * imag + offset * own_imag))
 
 
-def right_rows(scalars, inverse, pieces, first):
+def right_rows(scalars, inverse, pieces, first, cost=0.8):
     _, rows, n = pieces[0].shape
     total = rows * len(pieces)
     return call(
@@ -122,9 +135,8 @@
         jax.ShapeDtypeStruct((2 * total, n), BF16),
         [SMEM] * 4 + [VMEM] * (1 + len(pieces)),
         [pltpu.VMEM((2 * total, n), BF16)],
-        flops=8 * total * n * n,
-        bytes_accessed=8 * n * n,
         vmem=12,
+        cost=cost,
     )(*scalars, inverse, *pieces)
 
 
@@ -153,40 +165,50 @@
         [matrix, matrix, matrix],
         [SMEM] + [VMEM] * 3,
         [pltpu.VMEM((2, 2 * n, n), BF16)],
-        flops=16 * n**3,
-        bytes_accessed=14 * n * n,
         vmem=20,
+        cost=3.0,
     )(slab, own, partner, coupling)
 
 
-def far_matrices_kernel(slab_ref, chain_ref, self_ref, partner_ref, coupling_ref, high_ref, moves, factors):
+def far_matrices_kernel(slab_ref, chain_ref, self_ref, partner_ref, coupling_ref, high_ref, moves, factors, *more):
     core = slab_ref[0] & 1
     low, high = core, 1 - core
 
+    def chain_and_high(high_inverse):
+        step = mxu(high_inverse, coupling_ref[...]).astype(BF16)
+        store(moves.at[high], product(chain_ref[...], step))
+
     @pl.when(core == 0)
     def _():
-        far_high = mxu(partner_ref[...], coupling_ref[...]).astype(BF16)
-        store(moves.at[low], product(chain_ref[...], far_high))
+        chain_and_high(partner_ref[...])
+        moves[low] = moves[high]
+        for chain in more:
+            step = mxu(self_ref[...], coupling_ref[...]).astype(BF16)
+            store(chain, product(moves[high], step))
 
     @pl.when(core != 0)
     def _():
         moves[low] = chain_ref[...]
+        for chain in more:
+            chain_and_high(self_ref[...])
+            step = mxu(partner_ref[...], coupling_ref[...]).astype(BF16)
+            store(chain, product(moves[high], step))
 
     store(moves.at[high], product(high_ref[...], moves[low]))
     for place in range(2):
         store(factors.at[place], product(moves[place], self_ref[...]))
 
 
-def far_matrices(slab, chain, far_self, far_partner, coupling, high):
+def far_matrices(slab, chain, far_self, far_partner, coupling, high, goes_on):
     n = coupling.shape[0]
+    matrix = jax.ShapeDtypeStruct((2 * n, n), BF16)
     pair = jax.ShapeDtypeStruct((2, 2 * n, n), BF16)
     return call(
         far_matrices_kernel,
-        [pair, pair],
+        [pair, pair] + [matrix] * goes_on,
         [SMEM] + [VMEM] * 5,
-        flops=36 * n**3,
-        bytes_accessed=20 * n * n,
-        vmem=20,
+        vmem=24,
+        cost=5.2,
     )(slab, chain, far_self, far_partner, coupling, high)
 
 
@@ -221,9 +243,8 @@
         [total, total],
         [SMEM] + [VMEM] * (3 + len(chunks)),
         [pltpu.VMEM((2 * n, n), BF16)],
-        flops=24 * n**3,
-        bytes_accessed=28 * n * n,
         vmem=20,
+        cost=3.6,
     )(place, high, own, factor, *chunks)
 
 
@@ -252,9 +273,8 @@
         functools.partial(far_terms_kernel, target=target, firsts=tuple(firsts), energies=energies),
         jax.ShapeDtypeStruct((2 * n, n), dtype),
         [SMEM] + [VMEM] * (1 + len(arrays)),
-        flops=16 * n**2 * rows * len(terms),
-        bytes_accessed=16 * n * n * len(terms),
         vmem=20 + 5 * (len(terms) - 1),
+        cost=1.8,
     )(place, total, *arrays)
 
 
@@ -273,8 +293,6 @@
         finish_kernel,
         [jax.ShapeDtypeStruct((2 * n, n), BF16), jax.ShapeDtypeStruct((1, n), F32)],
         [SMEM, VMEM, VMEM],
-        flops=8 * n * n,
-        bytes_accessed=16 * n * n,
     )(scalars, own, partner)
 
 
@@ -292,26 +310,14 @@
     return lax.optimization_barrier((x, *others))[0]
 
 
-def exchange_all(pieces, window):
-    received = [pieces[0]]
-    for distance in range(1, len(pieces)):
+def exchange_all(pieces, order, window):
+    received = list(pieces)
+    for at, distance in enumerate(order):
         piece = pieces[distance]
-        if distance > window:
-            piece = after(piece, received[distance - window])
-        received.append(exchange(piece, "energy", distance))
+        if at >= window:
+            piece = after(piece, received[order[at - window]])
+        received[distance] = exchange(piece, "energy", distance)
     return received
-
-
-def complex_columns(first, second, n):
-    real, imag = first[:n], first[n:]
-    dot = functools.partial(jnp.dot, preferred_element_type=F32)
-    return jnp.concatenate(
-        (
-            dot(real, second[:n]) - dot(imag, second[n:]),
-            dot(real, second[n:]) + dot(imag, second[:n]),
-        ),
-        axis=0,
-    ).astype(BF16)
 
 
 def local(
@@ -337,52 +343,55 @@
     column = slab_inverse[0].reshape(2 * n, n)
     green = green_prev[0, 0]
 
+    half = energies // 2
+    partner = exchange(column, "slab", 1)
+    far_selves = [shift(column, "slab", behind) for behind in range(2, slabs, 2)]
     sent = [
         lax.dynamic_slice_in_dim(green, (place ^ distance) * rows, rows, axis=1)
         for distance in range(energies)
     ]
-    pieces = exchange_all(sent, 4)
-
-    partner = exchange(column, "slab", 1)
-    low_move, high_move, own_factor = own_matrices(slab_one, column, partner, coupling_block)
-    far_selves = [shift(column, "slab", back) for back in range(2, slabs, 2)]
-
-    pieces[-1] = after(pieces[-1], high_move)
+    sent[1] = after(sent[1], partner)
+    pieces = exchange_all(sent, range(1, energies), energies)
     mixed = mix(place_one, pair_source, pair_mode, phonon_coupling, pieces)
-    back = exchange_all(mixed, 4)
-
-    far_blocks = []
-    for far_self in far_selves:
-        far_self = after(far_self, mixed[1])
-        far_blocks.append((far_self, exchange(far_self, "slab", 1)))
+    far_partners = [exchange(after(far_self, mixed[1]), "slab", 1) for far_self in far_selves]
+    back = exchange_all(mixed, range(1, energies), energies)
+    back[1] = after(back[1], *far_partners)
+
+    scalars = (place_one, slab_one, active_slabs, offset)
+    groups = [(0, half), (half, energies)]
+    firsts = [first for first, _ in groups]
+    own_chunks = [right_rows(scalars, column, back[:half], 0)]
+
+    chain, high_move, own_factor = own_matrices(
+        slab_one, column, after(partner, own_chunks[0]), coupling_block
+    )
     far = []
-    chain = after(low_move, back[2])
-    for far_self, far_partner in far_blocks:
-        if far:
-            far_self_old, far_partner_old = far_blocks[len(far) - 1]
-            high = jnp.where(core == 0, far_partner_old, far_self_old)
-            low = jnp.where(core == 0, far_self_old, far_partner_old)
-            for block in (high, low):
-                step = jnp.dot(block, coupling_block, preferred_element_type=F32).astype(BF16)
-                chain = complex_columns(chain, step, n)
-        far.append(far_matrices(slab_one, chain, far_self, far_partner, coupling_block, high_move))
-
-    scalars = (place_one, slab_one, active_slabs, offset)
-    groups = [(0, energies // 2), (energies // 2, 3 * energies // 4), (3 * energies // 4, energies)]
-    firsts = [first for first, _ in groups]
+    for index, (far_self, far_partner) in enumerate(zip(far_selves, far_partners)):
+        moves, factors, *chain = far_matrices(
+            slab_one,
+            chain if index == 0 else chain[0],
+            far_self,
+            far_partner,
+            coupling_block,
+            high_move,
+            index + 1 < len(far_selves),
+        )
+        far.append((moves, factors))
     if far:
-        back[-1] = after(back[-1], far[-1][0])
-    own_chunks = [right_rows(scalars, column, back[first:last], first) for first, last in groups]
+        back[half] = after(back[half], far[-1][0])
+    own_chunks += [right_rows(scalars, column, back[first:last], first, 30.0) for first, last in groups[1:]]
     far_chunks = [
         [shift(chunk, "slab", 2 * (index + 1)) for chunk in own_chunks] for index in range(len(far))
     ]
     for_self, for_partner = own_terms(place_one, high_move, column, own_factor, own_chunks, firsts, energies)
-    for first, last in ((0, 1), (1, 3)):
+    for first, last in ((0, 1), (1, 2)):
         terms = [(chunks[first:last], *matrices) for chunks, matrices in zip(far_chunks, far)]
         if terms:
-            far_of = functools.partial(far_terms, place_one, terms=terms, firsts=firsts[first:last], energies=energies)
-            for_partner = far_of(total=for_partner, target=1, dtype=F32 if first == 0 else BF16)
-            for_self = far_of(total=for_self, target=0, dtype=F32)
+            if first > 0:
+                terms[-1][0][-1] = after(terms[-1][0][-1], for_self, for_partner)
+            far_of = functools.partial(far_terms, place_one, firsts=firsts[first:last], energies=energies)
+            for_partner = far_of(terms=terms, total=for_partner, target=1, dtype=F32 if first == 0 else BF16)
+            for_self = far_of(terms=terms, total=for_self, target=0, dtype=F32)
     from_partner = exchange(for_partner.astype(BF16), "slab", 1)
     current, terms = finish(occupation, for_self, from_partner)
     spread = jnp.broadcast_to(terms[None], (energies, 1, n))

time: 103 us -> 97 us (0.942)
  waiting for transfers between devices: 23.9 us -> 14 us
  blocking collectives: 9.59 us -> 11.8 us
  starting transfers between devices: 38.9 us -> 40.2 us
    ppermute x17, waiting for transfers between devices: 21 us -> 10.4 us  [exchange(): return lax.ppermute(x, axis, [(i, i ^ distance) for i in range(size)])]
    ppermute x17, starting transfers between devices: 29.1 us -> 32.6 us  [exchange(): return lax.ppermute(x, axis, [(i, i ^ distance) for i in range(size)])]
    all_to_all x1, blocking collectives: 9.59 us -> 11.8 us  [local(): lax.all_to_all(spread, 'energy', 0, 0, tiled=True)]
    ppermute x4 -> x3, starting transfers between devices: 9.76 us -> 7.64 us  [shift(): return lax.ppermute(x, axis, [(i, i + by) for i in range(size - by)])]
    pallas_call x4, Pallas kernels: 7.15 us -> 5.76 us  [far_terms(): call(functools.partial(far_terms_kernel, target=target, firsts=tuple(firs...]
    pallas_call x3 -> x2, Pallas kernels: 1.69 us -> 2.59 us  [right_rows(): call(functools.partial(right_kernel, first=first), jax.ShapeDtypeStruct((...]
    ppermute x4 -> x3, waiting for transfers between devices: 2.9 us -> 3.59 us  [shift(): return lax.ppermute(x, axis, [(i, i + by) for i in range(size - by)])]
  transfers between devices with their start and end apart: 21 -> 20, of which waited for: 6 -> 5; matrix products, arithmetic and copies ran while one was open for 2% -> 1% of each run, Pallas kernels for 21% -> 23%
where the time goes in v3:
time: 97 us; the launch traced here: 96.7 us
  starting transfers between devices  40.2 us (41%)
  Pallas kernels  24.7 us (25%)
  waiting for transfers between devices  14 us (14%)
  blocking collectives  11.8 us (12%)
  between operations  2.9 us (3%)
  local copies, waits for them, and re-layouts  2.41 us (2%)
    ppermute x17, starting transfers between devices, exchange(): return lax.ppermute(x, axis, [(i, i ^ distance) for i in range(size)])  32.6 us
    all_to_all x1, blocking collectives, local(): lax.all_to_all(spread, 'energy', 0, 0, tiled=True)  11.8 us
    ppermute x17, waiting for transfers between devices, exchange(): return lax.ppermute(x, axis, [(i, i ^ distance) for i in range(size)])  10.4 us
    ppermute x3, starting transfers between devices, shift(): return lax.ppermute(x, axis, [(i, i + by) for i in range(size - by)])  7.64 us
    pallas_call x4, Pallas kernels, far_terms(): call(functools.partial(far_terms_kernel, target=target, firsts=tuple(firs...  5.76 us
    pallas_call x1, Pallas kernels, far_matrices(): call(far_matrices_kernel, [pair, pair] + [matrix] * goes_on, [SMEM] + [VM...  5.23 us
    pallas_call x1, Pallas kernels, own_matrices(): call(own_matrices_kernel, [matrix, matrix, matrix], [SMEM] + [VMEM] * 3,...  3.77 us
    ppermute x3, waiting for transfers between devices, shift(): return lax.ppermute(x, axis, [(i, i + by) for i in range(size - by)])  3.59 us
  transfers between devices with their start and end apart: 20, of which 5 were waited for; matrix products, arithmetic and copies ran while one was open for 1% of the time, Pallas kernels for 23%

profile of v3, /device:TPU:0, one launch (start us, length us, event | category | flops | bytes accessed | tf_op | source)
XLA Modules:
  0.0 96.7 jit_solution(528733759852130761)
XLA Ops:
  0.7 0.5 collective-permute-start
  1.2 4.6 %collective-permute-start.9 = (bf16[1024,512]{1,0:T(8,128)(2,1)}, bf16[1024,512]{1,0:T(8,128)(2,1)S(1)}, u32[]{:S(2)}, u32[]{:S(2)}) collective-permute-start(bf16[1024,512]{1,0:T(8,128)(2,1)} %bitcast.23), channel_id=1, source_target_pairs={{0,2},{1,3},{4,6},{5,7},{8,10},{9,11},{12,14},{13,15},{16,18},{17,... | collective-permute-start | bytes 3145736 | tf_op jit(solution)/shard_map/ppermute | solution.py:306
  5.8 1.4 %dynamic-slice_bitcast_fusion = (bf16[2,64,512]{2,1,0:T(8,128)(2,1)S(1)}, bf16[2,64,512]{2,1,0:T(8,128)(2,1)S(1)}, bf16[2,64,512]{2,1,0:T(8,128)(2,1)S(1)}, bf16...) fusion(bf16[1,1,2,512,512]{4,3,2,1,0:T(8,128)(2,1)} %param.9, ...), kind=kLoop, calls=%fused_computation | loop fusion | bytes 2097184 | tf_op jit(solution)/shard_map/dynamic_slice | solution.py:350
  7.3 0.0 copy-start.1
  7.3 1.6 %collective-permute-start.2 = (bf16[2,64,512]{2,1,0:T(8,128)(2,1)S(1)}, bf16[2,64,512]{2,1,0:T(8,128)(2,1)S(1)}, u32[]{:S(2)}, u32[]{:S(2)}) collective-permute-start(bf16[2,64,512]{2,1,0:T(8,128)(2,1)S(1)} %get-tuple-element.52), channel_id=1, source_target_pairs={{0,8},{4,12},{8,0},{12,4},{16,24},{20,28},{24,16},{28,20},{1,9},{5... | collective-permute-start | bytes 393224 | tf_op jit(solution)/shard_map/ppermute | solution.py:301
  8.9 1.4 %collective-permute-start.3 = (bf16[2,64,512]{2,1,0:T(8,128)(2,1)S(1)}, bf16[2,64,512]{2,1,0:T(8,128)(2,1)S(1)}, u32[]{:S(2)}, u32[]{:S(2)}) collective-permute-start(bf16[2,64,512]{2,1,0:T(8,128)(2,1)S(1)} %get-tuple-element.51), channel_id=1, source_target_pairs={{0,12},{4,8},{8,4},{12,0},{16,28},{20,24},{24,20},{28,16},{1,13},{... | collective-permute-start | bytes 393224 | tf_op jit(solution)/shard_map/ppermute | solution.py:301
  10.3 2.6 %collective-permute-start.4 = (bf16[2,64,512]{2,1,0:T(8,128)(2,1)S(1)}, bf16[2,64,512]{2,1,0:T(8,128)(2,1)S(1)}, u32[]{:S(2)}, u32[]{:S(2)}) collective-permute-start(bf16[2,64,512]{2,1,0:T(8,128)(2,1)S(1)} %get-tuple-element.50), channel_id=1, source_target_pairs={{0,16},{4,20},{8,24},{12,28},{16,0},{20,4},{24,8},{28,12},{1,17},{... | collective-permute-start | bytes 393224 | tf_op jit(solution)/shard_map/ppermute | solution.py:301
  12.9 0.0 collective-permute-done.partner_ref
  12.9 0.3 collective-permute-start.5
  13.2 0.1 collective-permute-done.2.refs_2_
  13.3 5.4 %collective-permute-start.6 = (bf16[2,64,512]{2,1,0:T(8,128)(2,1)S(1)}, bf16[2,64,512]{2,1,0:T(8,128)(2,1)S(1)}, u32[]{:S(2)}, u32[]{:S(2)}) collective-permute-start(bf16[2,64,512]{2,1,0:T(8,128)(2,1)S(1)} %get-tuple-element.55), channel_id=1, source_target_pairs={{0,24},{4,28},{8,16},{12,20},{16,8},{20,12},{24,0},{28,4},{1,25},{... | collective-permute-start | bytes 393224 | tf_op jit(solution)/shard_map/ppermute | solution.py:301
  18.7 2.4 %collective-permute-done.3.refs_3_ = bf16[2,64,512]{2,1,0:T(8,128)(2,1)S(1)} collective-permute-done((bf16[2,64,512]{2,1,0:T(8,128)(2,1)S(1)}, bf16[2,64,512]{2,1,0:T(8,128)(2,1)S(1)}, u32[]{:S(2)}, u32[]{:S(2)}) %collective-permute-start.3) | collective-permute-done | bytes 131104 | tf_op jit(solution)/shard_map/ppermute | solution.py:301
  21.1 1.7 %collective-permute-start.7 = (bf16[2,64,512]{2,1,0:T(8,128)(2,1)S(1)}, bf16[2,64,512]{2,1,0:T(8,128)(2,1)S(1)}, u32[]{:S(2)}, u32[]{:S(2)}) collective-permute-start(bf16[2,64,512]{2,1,0:T(8,128)(2,1)S(1)} %get-tuple-element.48), channel_id=1, source_target_pairs={{0,28},{4,24},{8,20},{12,16},{16,12},{20,8},{24,4},{28,0},{1,29},{... | collective-permute-start | bytes 393224 | tf_op jit(solution)/shard_map/ppermute | solution.py:301
  22.8 1.9 %collective-permute-start.1 = (bf16[2,64,512]{2,1,0:T(8,128)(2,1)S(1)}, bf16[2,64,512]{2,1,0:T(8,128)(2,1)S(1)}, u32[]{:S(2)}, u32[]{:S(2)}) collective-permute-start(bf16[2,64,512]{2,1,0:T(8,128)(2,1)S(1)} %get-tuple-element.25), channel_id=1, source_target_pairs={{0,4},{4,0},{8,12},{12,8},{16,20},{20,16},{24,28},{28,24},{1,5},{5... | collective-permute-start | bytes 393224 | tf_op jit(solution)/shard_map/ppermute | solution.py:301
  24.8 7.3 %collective-permute-done.5.refs_5_ = bf16[2,64,512]{2,1,0:T(8,128)(2,1)S(1)} collective-permute-done((bf16[2,64,512]{2,1,0:T(8,128)(2,1)S(1)}, bf16[2,64,512]{2,1,0:T(8,128)(2,1)S(1)}, u32[]{:S(2)}, u32[]{:S(2)}) %collective-permute-start.5) | collective-permute-done | bytes 131104 | tf_op jit(solution)/shard_map/ppermute | solution.py:301
  32.1 0.0 collective-permute-done.6.refs_6_
  32.1 0.0 collective-permute-done.7.refs_7_
  32.1 2.7 %shard_map.104 = (bf16[2,64,512]{2,1,0:T(8,128)(2,1)S(1)}, bf16[2,64,512]{2,1,0:T(8,128)(2,1)S(1)}, bf16[2,64,512]{2,1,0:T(8,128)(2,1)S(1)}, bf16[2,64,512]{2,1,...) custom-call(s32[1]{0:T(128)} %bitcast.place_ref, ...), custom_call_target="tpu_custom_call" | custom-call | flops 1024 | bytes 6601024 | tf_op jit(solution)/shard_map/pallas_call | solution.py:86
  34.8 0.0 collective-permute-done.9.self_ref
  34.8 0.0 collective-permute-start.10
  34.8 1.1 %collective-permute-start.8 = (bf16[2,64,512]{2,1,0:T(8,128)(2,1)S(1)}, bf16[2,64,512]{2,1,0:T(8,128)(2,1)S(1)}, u32[]{:S(2)}, u32[]{:S(2)}) collective-permute-start(bf16[2,64,512]{2,1,0:T(8,128)(2,1)S(1)} %get-tuple-element.27), channel_id=1, source_target_pairs={{0,4},{4,0},{8,12},{12,8},{16,20},{20,16},{24,28},{28,24},{1,5},{5... | collective-permute-start | bytes 393224 | tf_op jit(solution)/shard_map/ppermute | solution.py:301
  36.0 4.8 %collective-permute-start.11 = (bf16[2,64,512]{2,1,0:T(8,128)(2,1)S(1)}, bf16[2,64,512]{2,1,0:T(8,128)(2,1)S(1)}, u32[]{:S(2)}, u32[]{:S(2)}) collective-permute-start(bf16[2,64,512]{2,1,0:T(8,128)(2,1)S(1)} %get-tuple-element.30), channel_id=1, source_target_pairs={{0,8},{4,12},{8,0},{12,4},{16,24},{20,28},{24,16},{28,20},{1,9},{5... | collective-permute-start | bytes 393224 | tf_op jit(solution)/shard_map/ppermute | solution.py:301
  40.7 0.5 collective-permute-start.12
  41.2 3.5 %collective-permute-start.13 = (bf16[2,64,512]{2,1,0:T(8,128)(2,1)}, bf16[2,64,512]{2,1,0:T(8,128)(2,1)S(1)}, u32[]{:S(2)}, u32[]{:S(2)}) collective-permute-start(bf16[2,64,512]{2,1,0:T(8,128)(2,1)} %get-tuple-element.35), channel_id=1, source_target_pairs={{0,16},{4,20},{8,24},{12,28},{16,0},{20,4},{24,8},{28,12},{1,17},{... | collective-permute-start | bytes 393224 | tf_op jit(solution)/shard_map/ppermute | solution.py:301
  44.7 0.0 collective-permute-done.8.refs_1_
  44.7 3.3 %collective-permute-start.14 = (bf16[2,64,512]{2,1,0:T(8,128)(2,1)}, bf16[2,64,512]{2,1,0:T(8,128)(2,1)S(1)}, u32[]{:S(2)}, u32[]{:S(2)}) collective-permute-start(bf16[2,64,512]{2,1,0:T(8,128)(2,1)} %get-tuple-element.39), channel_id=1, source_target_pairs={{0,20},{4,16},{8,28},{12,24},{16,4},{20,0},{24,12},{28,8},{1,21},{... | collective-permute-start | bytes 393224 | tf_op jit(solution)/shard_map/ppermute | solution.py:301
  48.1 0.0 collective-permute-done.11.refs_2_
  48.1 3.3 %collective-permute-start.15 = (bf16[2,64,512]{2,1,0:T(8,128)(2,1)}, bf16[2,64,512]{2,1,0:T(8,128)(2,1)S(1)}, u32[]{:S(2)}, u32[]{:S(2)}) collective-permute-start(bf16[2,64,512]{2,1,0:T(8,128)(2,1)} %get-tuple-element.40), channel_id=1, source_target_pairs={{0,24},{4,28},{8,16},{12,20},{16,8},{20,12},{24,0},{28,4},{1,25},{... | collective-permute-start | bytes 393224 | tf_op jit(solution)/shard_map/ppermute | solution.py:301
  51.4 0.0 collective-permute-done.10.partner_ref
  51.4 1.0 %copy-done.2 = bf16[1024,512]{1,0:T(8,128)(2,1)} copy-done((bf16[1024,512]{1,0:T(8,128)(2,1)}, bf16[1024,512]{1,0:T(8,128)(2,1)S(1)}, u32[]{:S(2)}) %copy-start.2) | copy-done | bytes 1048600
  52.4 0.4 collective-permute-start.16
  54.1 1.8 %shard_map.105.refs_0_ = bf16[512,512]{1,0:T(8,128)(2,1)S(1)} custom-call(s32[1]{0:T(128)} %bitcast.place_ref, s32[1]{0:T(128)} %bitcast.1.slab_ref, s32[1]{0:T(128)S(6)} %copy.15.active_ref, f32[1]{0:T(128)S(6)} %copy.13.offset_ref, bf16[1024,512]{1,0:T(8,128)(2,1)S(1)} %bitcast.24, bf16[2,64,512]{2,1,0:T(8,128)(2,1)S(1)} %get-tuple-element.26.refs_0_, ...), custom_call_target="tpu_custom_call" | custom-call | flops 1024 | bytes 2641024 | tf_op jit(solution)/shard_map/pallas_call | solution.py:133
  55.9 1.5 %collective-permute-start.17 = (bf16[512,512]{1,0:T(8,128)(2,1)S(1)}, bf16[512,512]{1,0:T(8,128)(2,1)S(1)}, u32[]{:S(2)}, u32[]{:S(2)}) collective-permute-start(bf16[512,512]{1,0:T(8,128)(2,1)S(1)} %shard_map.105.refs_0_), channel_id=1, source_target_pairs={{0,2},{1,3},{4,6},{5,7},{8,10},{9,11},{12,14},{13,15},{16,18},{17,... | collective-permute-start | bytes 1572872 | tf_op jit(solution)/shard_map/ppermute | solution.py:306
  57.5 3.8 %shard_map.106 = (bf16[1024,512]{1,0:T(8,128)(2,1)S(1)}, bf16[1024,512]{1,0:T(8,128)(2,1)S(1)}, bf16[1024,512]{1,0:T(8,128)(2,1)S(1)}) custom-call(s32[1]{0:T(128)} %bitcast.1.slab_ref, bf16[1024,512]{1,0:T(8,128)(2,1)S(1)} %bitcast.25, bf16[1024,512]{1,0:T(8,128)(2,1)} %collective-permute-done.partner_ref, bf16[512,512]{1,0:T(8,128)(2,1)S(1)} %copy-done.1), custom_call_target="tpu_custom_call" | custom-call | flops 1024 | bytes 9901024 | tf_op jit(solution)/shard_map/pallas_call | solution.py:163
  61.3 5.2 %shard_map.107 = (bf16[2,1024,512]{2,1,0:T(8,128)(2,1)S(1)}, bf16[2,1024,512]{2,1,0:T(8,128)(2,1)S(1)}) custom-call(s32[1]{0:T(128)} %bitcast.1.slab_ref, bf16[1024,512]{1,0:T(8,128)(2,1)S(1)} %get-tuple-element.36.chain_ref, bf16[1024,512]{1,0:T(8,128)(2,1)S(1)} %collective-permute-done.9.self_ref, bf16[1024,512]{1,0:T(8,128)(2,1)S(1)} %copy-done.3, ...), custom_call_target="tpu_custom_call" | custom-call | flops 1024 | bytes 17161024 | tf_op jit(solution)/shard_map/pallas_call | solution.py:206
  66.5 0.8 shard_map.108.refs_1_
  67.4 1.5 %collective-permute-start.18 = (bf16[512,512]{1,0:T(8,128)(2,1)S(1)}, bf16[512,512]{1,0:T(8,128)(2,1)S(1)}, u32[]{:S(2)}, u32[]{:S(2)}) collective-permute-start(bf16[512,512]{1,0:T(8,128)(2,1)S(1)} %shard_map.108.refs_1_), channel_id=1, source_target_pairs={{0,2},{1,3},{4,6},{5,7},{8,10},{9,11},{12,14},{13,15},{16,18},{17,... | collective-permute-start | bytes 1572872 | tf_op jit(solution)/shard_map/ppermute | solution.py:306
  68.9 3.5 %shard_map.109 = (f32[1024,512]{1,0:T(8,128)S(1)}, f32[1024,512]{1,0:T(8,128)S(1)}) custom-call(s32[1]{0:T(128)} %bitcast.place_ref, bf16[1024,512]{1,0:T(8,128)(2,1)S(1)} %get-tuple-element.33.high_ref, bf16[1024,512]{1,0:T(8,128)(2,1)S(1)} %bitcast.27, bf16[1024,512]{1,0:T(8,128)(2,1)S(1)} %get-tuple-element.34.factor_ref, ...), custom_call_target="tpu_custom_call" | custom-call | flops 1024 | bytes 11881024 | tf_op jit(solution)/shard_map/pallas_call | solution.py:241
  72.4 1.4 %shard_map.111.total_ref = f32[1024,512]{1,0:T(8,128)S(1)} custom-call(s32[1]{0:T(128)} %bitcast.place_ref, f32[1024,512]{1,0:T(8,128)S(1)} %get-tuple-element.44.total_ref, bf16[512,512]{1,0:T(8,128)(2,1)S(1)} %collective-permute-done.17.refs_0_, bf16[2,1024,512]{2,1,0:T(8,128)(2,1)S(1)} %get-tuple-element.37.refs_1_, ...), custom_call_target="tpu_custom_call" | custom-call | flops 1024 | bytes 5941024 | tf_op jit(solution)/shard_map/pallas_call | solution.py:272
  73.9 1.4 %shard_map.110.total_ref = f32[1024,512]{1,0:T(8,128)S(1)} custom-call(s32[1]{0:T(128)} %bitcast.place_ref, f32[1024,512]{1,0:T(8,128)S(1)} %get-tuple-element.42.total_ref, bf16[512,512]{1,0:T(8,128)(2,1)S(1)} %collective-permute-done.17.refs_0_, bf16[2,1024,512]{2,1,0:T(8,128)(2,1)S(1)} %get-tuple-element.37.refs_1_, ...), custom_call_target="tpu_custom_call" | custom-call | flops 1024 | bytes 5941024 | tf_op jit(solution)/shard_map/pallas_call | solution.py:272
  75.3 3.6 %collective-permute-done.18.refs_0_ = bf16[512,512]{1,0:T(8,128)(2,1)S(1)} collective-permute-done((bf16[512,512]{1,0:T(8,128)(2,1)S(1)}, bf16[512,512]{1,0:T(8,128)(2,1)S(1)}, u32[]{:S(2)}, u32[]{:S(2)}) %collective-permute-start.18) | collective-permute-done | bytes 524320 | tf_op jit(solution)/shard_map/ppermute | solution.py:306
  78.9 1.5 %shard_map.113 = bf16[1024,512]{1,0:T(8,128)(2,1)S(1)} custom-call(s32[1]{0:T(128)} %bitcast.place_ref, f32[1024,512]{1,0:T(8,128)S(1)} %shard_map.111.total_ref, bf16[512,512]{1,0:T(8,128)(2,1)S(1)} %collective-permute-done.18.refs_0_, bf16[2,1024,512]{2,1,0:T(8,128)(2,1)S(1)} %get-tuple-element.37.refs_1_, bf16[2,1024,512]{2,1,0:T(8,128)(2,1)S(1)} %get-tuple-element.43.refs_2_), custom_call_target="tpu_custom_call" | custom-call | flops 1024 | bytes 5941024 | tf_op jit(solution)/shard_map/pallas_call | solution.py:272
  80.3 0.1 collective-permute-start.19
  81.1 1.5 %shard_map.112.own_ref = f32[1024,512]{1,0:T(8,128)S(1)} custom-call(s32[1]{0:T(128)} %bitcast.place_ref, f32[1024,512]{1,0:T(8,128)S(1)} %shard_map.110.total_ref, bf16[512,512]{1,0:T(8,128)(2,1)S(1)} %collective-permute-done.18.refs_0_, bf16[2,1024,512]{2,1,0:T(8,128)(2,1)S(1)} %get-tuple-element.37.refs_1_, ...), custom_call_target="tpu_custom_call" | custom-call | flops 1024 | bytes 5941024 | tf_op jit(solution)/shard_map/pallas_call | solution.py:272
  82.5 0.5 collective-permute-done.19.partner_ref
  83.1 1.1 %shard_map.114 = (bf16[1024,512]{1,0:T(8,128)(2,1)}, f32[1,512]{1,0:T(1,128)S(1)}) custom-call(f32[1]{0:T(128)S(6)} %copy.14.scalar_ref, f32[1024,512]{1,0:T(8,128)S(1)} %shard_map.112.own_ref, bf16[1024,512]{1,0:T(8,128)(2,1)S(1)} %collective-permute-done.19.partner_ref), custom_call_target="tpu_custom_call" | custom-call | flops 1024 | bytes 1024 | tf_op jit(solution)/shard_map/pallas_call | solution.py:292
  84.2 11.8 %all_to_all.5 = f32[8,1,512]{2,1,0:T(1,128)S(1)} all-to-all(f32[8,1,512]{2,1,0:T(1,128)S(1)} %broadcast_in_dim.17), channel_id=1, replica_groups=mesh['energy'=8,'slab'=4] {'energy'}, dimensions={0} | all-to-all | bytes 32768 | tf_op jit(solution)/shard_map/all_to_all | solution.py:398
  96.1 0.6 reduce_sum.11
  (21 shorter events, 0.1 us)
Async XLA Ops:
  0.6 53.5 %copy-start = (bf16[1,2,512,512]{3,2,1,0:T(8,128)(2,1)S(1)}, bf16[1,2,512,512]{3,2,1,0:T(8,128)(2,1)}, u32[]{:S(2)}) copy-start(bf16[1,2,512,512]{3,2,1,0:T(8,128)(2,1)} %param.10) | copy-start | bytes 3145732
  0.6 31.5 %copy-start.4 = (bf16[4,64,512]{2,1,0:T(8,128)(2,1)S(1)}, bf16[4,64,512]{2,1,0:T(8,128)(2,1)}, u32[]{:S(2)}) copy-start(bf16[4,64,512]{2,1,0:T(8,128)(2,1)} %phonon_ref.1) | copy-start | bytes 786436
  0.7 31.5 %copy-start.5 = (s32[8,6]{1,0:T(8,128)S(1)}, s32[8,6]{1,0:T(8,128)}, u32[]{:S(2)}) copy-start(s32[8,6]{1,0:T(8,128)} %source_ref.1) | copy-start | bytes 580
  0.7 31.5 %copy-start.6 = (s32[8,6]{1,0:T(8,128)S(1)}, s32[8,6]{1,0:T(8,128)}, u32[]{:S(2)}) copy-start(s32[8,6]{1,0:T(8,128)} %mode_ref.1) | copy-start | bytes 580
  0.7 12.2 %collective-permute-start = (bf16[1024,512]{1,0:T(8,128)(2,1)}, bf16[1024,512]{1,0:T(8,128)(2,1)}, u32[]{:S(2)}, u32[]{:S(2)}) collective-permute-start(bf16[1024,512]{1,0:T(8,128)(2,1)} %bitcast.22), channel_id=1, source_target_pairs={{0,1},{1,0},{2,3},{3,2},{4,5},{5,4},{6,7},{7,6},{8,9},{9,8},{10,11... | collective-permute-start | bytes 3145736 | tf_op jit(solution)/shard_map/ppermute | solution.py:301
  1.2 33.6 %collective-permute-start.9 = (bf16[1024,512]{1,0:T(8,128)(2,1)}, bf16[1024,512]{1,0:T(8,128)(2,1)S(1)}, u32[]{:S(2)}, u32[]{:S(2)}) collective-permute-start(bf16[1024,512]{1,0:T(8,128)(2,1)} %bitcast.23), channel_id=1, source_target_pairs={{0,2},{1,3},{4,6},{5,7},{8,10},{9,11},{12,14},{13,15},{16,18},{17,... | collective-permute-start | bytes 3145736 | tf_op jit(solution)/shard_map/ppermute | solution.py:306
  7.3 50.2 %copy-start.1 = (bf16[512,512]{1,0:T(8,128)(2,1)S(1)}, bf16[512,512]{1,0:T(8,128)(2,1)}, u32[]{:S(2)}) copy-start(bf16[512,512]{1,0:T(8,128)(2,1)} %coupling_ref.3) | copy-start | bytes 1572868
  7.3 6.0 %collective-permute-start.2 = (bf16[2,64,512]{2,1,0:T(8,128)(2,1)S(1)}, bf16[2,64,512]{2,1,0:T(8,128)(2,1)S(1)}, u32[]{:S(2)}, u32[]{:S(2)}) collective-permute-start(bf16[2,64,512]{2,1,0:T(8,128)(2,1)S(1)} %get-tuple-element.52), channel_id=1, source_target_pairs={{0,8},{4,12},{8,0},{12,4},{16,24},{20,28},{24,16},{28,20},{1,9},{5... | collective-permute-start | bytes 393224 | tf_op jit(solution)/shard_map/ppermute | solution.py:301
  8.9 12.2 %collective-permute-start.3 = (bf16[2,64,512]{2,1,0:T(8,128)(2,1)S(1)}, bf16[2,64,512]{2,1,0:T(8,128)(2,1)S(1)}, u32[]{:S(2)}, u32[]{:S(2)}) collective-permute-start(bf16[2,64,512]{2,1,0:T(8,128)(2,1)S(1)} %get-tuple-element.51), channel_id=1, source_target_pairs={{0,12},{4,8},{8,4},{12,0},{16,28},{20,24},{24,20},{28,16},{1,13},{... | collective-permute-start | bytes 393224 | tf_op jit(solution)/shard_map/ppermute | solution.py:301
  10.3 12.5 %collective-permute-start.4 = (bf16[2,64,512]{2,1,0:T(8,128)(2,1)S(1)}, bf16[2,64,512]{2,1,0:T(8,128)(2,1)S(1)}, u32[]{:S(2)}, u32[]{:S(2)}) collective-permute-start(bf16[2,64,512]{2,1,0:T(8,128)(2,1)S(1)} %get-tuple-element.50), channel_id=1, source_target_pairs={{0,16},{4,20},{8,24},{12,28},{16,0},{20,4},{24,8},{28,12},{1,17},{... | collective-permute-start | bytes 393224 | tf_op jit(solution)/shard_map/ppermute | solution.py:301
  12.9 19.2 %collective-permute-start.5 = (bf16[2,64,512]{2,1,0:T(8,128)(2,1)S(1)}, bf16[2,64,512]{2,1,0:T(8,128)(2,1)S(1)}, u32[]{:S(2)}, u32[]{:S(2)}) collective-permute-start(bf16[2,64,512]{2,1,0:T(8,128)(2,1)S(1)} %get-tuple-element.49), channel_id=1, source_target_pairs={{0,20},{4,16},{8,28},{12,24},{16,4},{20,0},{24,12},{28,8},{1,21},{... | collective-permute-start | bytes 393224 | tf_op jit(solution)/shard_map/ppermute | solution.py:301
  13.3 18.8 %collective-permute-start.6 = (bf16[2,64,512]{2,1,0:T(8,128)(2,1)S(1)}, bf16[2,64,512]{2,1,0:T(8,128)(2,1)S(1)}, u32[]{:S(2)}, u32[]{:S(2)}) collective-permute-start(bf16[2,64,512]{2,1,0:T(8,128)(2,1)S(1)} %get-tuple-element.55), channel_id=1, source_target_pairs={{0,24},{4,28},{8,16},{12,20},{16,8},{20,12},{24,0},{28,4},{1,25},{... | collective-permute-start | bytes 393224 | tf_op jit(solution)/shard_map/ppermute | solution.py:301
  21.1 11.0 %collective-permute-start.7 = (bf16[2,64,512]{2,1,0:T(8,128)(2,1)S(1)}, bf16[2,64,512]{2,1,0:T(8,128)(2,1)S(1)}, u32[]{:S(2)}, u32[]{:S(2)}) collective-permute-start(bf16[2,64,512]{2,1,0:T(8,128)(2,1)S(1)} %get-tuple-element.48), channel_id=1, source_target_pairs={{0,28},{4,24},{8,20},{12,16},{16,12},{20,8},{24,4},{28,0},{1,29},{... | collective-permute-start | bytes 393224 | tf_op jit(solution)/shard_map/ppermute | solution.py:301
  22.8 9.3 %collective-permute-start.1 = (bf16[2,64,512]{2,1,0:T(8,128)(2,1)S(1)}, bf16[2,64,512]{2,1,0:T(8,128)(2,1)S(1)}, u32[]{:S(2)}, u32[]{:S(2)}) collective-permute-start(bf16[2,64,512]{2,1,0:T(8,128)(2,1)S(1)} %get-tuple-element.25), channel_id=1, source_target_pairs={{0,4},{4,0},{8,12},{12,8},{16,20},{20,16},{24,28},{28,24},{1,5},{5... | collective-permute-start | bytes 393224 | tf_op jit(solution)/shard_map/ppermute | solution.py:301
  34.8 16.6 %collective-permute-start.10 = (bf16[1024,512]{1,0:T(8,128)(2,1)S(1)}, bf16[1024,512]{1,0:T(8,128)(2,1)S(1)}, u32[]{:S(2)}, u32[]{:S(2)}) collective-permute-start(bf16[1024,512]{1,0:T(8,128)(2,1)S(1)} %collective-permute-done.9.self_ref), channel_id=1, source_target_pairs={{0,1},{1,0},{2,3},{3,2},{4,5},{5,4},{6,7},{7,6},{8,9},{9,8},{10,11... | collective-permute-start | bytes 3145736 | tf_op jit(solution)/shard_map/ppermute | solution.py:301
  34.8 9.9 %collective-permute-start.8 = (bf16[2,64,512]{2,1,0:T(8,128)(2,1)S(1)}, bf16[2,64,512]{2,1,0:T(8,128)(2,1)S(1)}, u32[]{:S(2)}, u32[]{:S(2)}) collective-permute-start(bf16[2,64,512]{2,1,0:T(8,128)(2,1)S(1)} %get-tuple-element.27), channel_id=1, source_target_pairs={{0,4},{4,0},{8,12},{12,8},{16,20},{20,16},{24,28},{28,24},{1,5},{5... | collective-permute-start | bytes 393224 | tf_op jit(solution)/shard_map/ppermute | solution.py:301
  36.0 12.1 %collective-permute-start.11 = (bf16[2,64,512]{2,1,0:T(8,128)(2,1)S(1)}, bf16[2,64,512]{2,1,0:T(8,128)(2,1)S(1)}, u32[]{:S(2)}, u32[]{:S(2)}) collective-permute-start(bf16[2,64,512]{2,1,0:T(8,128)(2,1)S(1)} %get-tuple-element.30), channel_id=1, source_target_pairs={{0,8},{4,12},{8,0},{12,4},{16,24},{20,28},{24,16},{28,20},{1,9},{5... | collective-permute-start | bytes 393224 | tf_op jit(solution)/shard_map/ppermute | solution.py:301
  40.7 13.4 %collective-permute-start.12 = (bf16[2,64,512]{2,1,0:T(8,128)(2,1)}, bf16[2,64,512]{2,1,0:T(8,128)(2,1)}, u32[]{:S(2)}, u32[]{:S(2)}) collective-permute-start(bf16[2,64,512]{2,1,0:T(8,128)(2,1)} %get-tuple-element.31), channel_id=1, source_target_pairs={{0,12},{4,8},{8,4},{12,0},{16,28},{20,24},{24,20},{28,16},{1,13},{... | collective-permute-start | bytes 393224 | tf_op jit(solution)/shard_map/ppermute | solution.py:301
  41.2 25.3 %collective-permute-start.13 = (bf16[2,64,512]{2,1,0:T(8,128)(2,1)}, bf16[2,64,512]{2,1,0:T(8,128)(2,1)S(1)}, u32[]{:S(2)}, u32[]{:S(2)}) collective-permute-start(bf16[2,64,512]{2,1,0:T(8,128)(2,1)} %get-tuple-element.35), channel_id=1, source_target_pairs={{0,16},{4,20},{8,24},{12,28},{16,0},{20,4},{24,8},{28,12},{1,17},{... | collective-permute-start | bytes 393224 | tf_op jit(solution)/shard_map/ppermute | solution.py:301
  44.7 21.8 %collective-permute-start.14 = (bf16[2,64,512]{2,1,0:T(8,128)(2,1)}, bf16[2,64,512]{2,1,0:T(8,128)(2,1)S(1)}, u32[]{:S(2)}, u32[]{:S(2)}) collective-permute-start(bf16[2,64,512]{2,1,0:T(8,128)(2,1)} %get-tuple-element.39), channel_id=1, source_target_pairs={{0,20},{4,16},{8,28},{12,24},{16,4},{20,0},{24,12},{28,8},{1,21},{... | collective-permute-start | bytes 393224 | tf_op jit(solution)/shard_map/ppermute | solution.py:301
  48.1 18.5 %collective-permute-start.15 = (bf16[2,64,512]{2,1,0:T(8,128)(2,1)}, bf16[2,64,512]{2,1,0:T(8,128)(2,1)S(1)}, u32[]{:S(2)}, u32[]{:S(2)}) collective-permute-start(bf16[2,64,512]{2,1,0:T(8,128)(2,1)} %get-tuple-element.40), channel_id=1, source_target_pairs={{0,24},{4,28},{8,16},{12,20},{16,8},{20,12},{24,0},{28,4},{1,25},{... | collective-permute-start | bytes 393224 | tf_op jit(solution)/shard_map/ppermute | solution.py:301
  51.4 1.0 %copy-start.2 = (bf16[1024,512]{1,0:T(8,128)(2,1)}, bf16[1024,512]{1,0:T(8,128)(2,1)S(1)}, u32[]{:S(2)}) copy-start(bf16[1024,512]{1,0:T(8,128)(2,1)S(1)} %collective-permute-done.10.partner_ref) | copy-start | bytes 3145732
  52.4 14.2 %collective-permute-start.16 = (bf16[2,64,512]{2,1,0:T(8,128)(2,1)}, bf16[2,64,512]{2,1,0:T(8,128)(2,1)S(1)}, u32[]{:S(2)}, u32[]{:S(2)}) collective-permute-start(bf16[2,64,512]{2,1,0:T(8,128)(2,1)} %get-tuple-element.41), channel_id=1, source_target_pairs={{0,28},{4,24},{8,20},{12,16},{16,12},{20,8},{24,4},{28,0},{1,29},{... | collective-permute-start | bytes 393224 | tf_op jit(solution)/shard_map/ppermute | solution.py:301
  54.1 7.1 %copy-start.3 = (bf16[1024,512]{1,0:T(8,128)(2,1)S(1)}, bf16[1024,512]{1,0:T(8,128)(2,1)}, u32[]{:S(2)}) copy-start(bf16[1024,512]{1,0:T(8,128)(2,1)} %copy-done.2) | copy-start | bytes 3145732
  55.9 16.5 %collective-permute-start.17 = (bf16[512,512]{1,0:T(8,128)(2,1)S(1)}, bf16[512,512]{1,0:T(8,128)(2,1)S(1)}, u32[]{:S(2)}, u32[]{:S(2)}) collective-permute-start(bf16[512,512]{1,0:T(8,128)(2,1)S(1)} %shard_map.105.refs_0_), channel_id=1, source_target_pairs={{0,2},{1,3},{4,6},{5,7},{8,10},{9,11},{12,14},{13,15},{16,18},{17,... | collective-permute-start | bytes 1572872 | tf_op jit(solution)/shard_map/ppermute | solution.py:306
  67.4 11.5 %collective-permute-start.18 = (bf16[512,512]{1,0:T(8,128)(2,1)S(1)}, bf16[512,512]{1,0:T(8,128)(2,1)S(1)}, u32[]{:S(2)}, u32[]{:S(2)}) collective-permute-start(bf16[512,512]{1,0:T(8,128)(2,1)S(1)} %shard_map.108.refs_1_), channel_id=1, source_target_pairs={{0,2},{1,3},{4,6},{5,7},{8,10},{9,11},{12,14},{13,15},{16,18},{17,... | collective-permute-start | bytes 1572872 | tf_op jit(solution)/shard_map/ppermute | solution.py:306
  80.3 2.7 %collective-permute-start.19 = (bf16[1024,512]{1,0:T(8,128)(2,1)S(1)}, bf16[1024,512]{1,0:T(8,128)(2,1)S(1)}, u32[]{:S(2)}, u32[]{:S(2)}) collective-permute-start(bf16[1024,512]{1,0:T(8,128)(2,1)S(1)} %shard_map.113), channel_id=1, source_target_pairs={{0,1},{1,0},{2,3},{3,2},{4,5},{5,4},{6,7},{7,6},{8,9},{9,8},{10,11... | collective-permute-start | bytes 3145736 | tf_op jit(solution)/shard_map/ppermute | solution.py:301

commit v4 on v3

v4 whole, which is shorter than its diff:
```python
import functools

import jax
import jax.numpy as jnp
from jax import lax
from jax.experimental import pallas as pl
from jax.experimental.pallas import tpu as pltpu
from jax.sharding import PartitionSpec as P

BF16 = jnp.bfloat16
F32 = jnp.float32
LANES = 128
MICROSECOND = 3_300_000
VMEM = pl.BlockSpec(memory_space=pltpu.VMEM)
SMEM = pl.BlockSpec(memory_space=pltpu.SMEM)


def mxu(first, second):
    return jnp.dot(first, second, preferred_element_type=F32)


def mxu_nt(first, second):
    return lax.dot_general(first, second, (((1,), (1,)), ((), ())), preferred_element_type=F32)


def call(kernel, out_shape, in_specs, scratch=(), vmem=16, cost=0.0):
    return pl.pallas_call(
        kernel,
        out_shape=out_shape,
        in_specs=in_specs,
        out_specs=jax.tree.map(lambda _: VMEM, out_shape),
        scratch_shapes=list(scratch),
        compiler_params=pltpu.CompilerParams(vmem_limit_bytes=vmem * 2**20),
        cost_estimate=pl.CostEstimate(
            flops=1024, bytes_accessed=1024 + int(cost * MICROSECOND), transcendentals=0
        ),
    )


def complex_of(by_real, by_imag):
    rows = by_real.shape[0] // 2
    return by_real[:rows] - by_imag[rows:], by_real[rows:] + by_imag[:rows]


def product(first, second):
    rows = second.shape[0] // 2
    return complex_of(mxu(first, second[:rows]), mxu(first, second[rows:]))


def store(ref, parts):
    rows = parts[0].shape[0]
    for index, part in enumerate(parts):
        ref[index * rows : (index + 1) * rows, :] = part.astype(ref.dtype)


def weight_kernel(slab_ref, active_ref, occupation_ref, offset_ref, out_ref):
    shape = out_ref.shape
    row = lax.broadcasted_iota(jnp.int32, shape, 0)
    lane = lax.broadcasted_iota(jnp.int32, shape, 1)
    weight = occupation_ref[0]
    active = jnp.where(slab_ref[0] < active_ref[0], weight, 0.0)
    rest = jnp.where(lane < 2 * LANES, weight, weight * offset_ref[0])
    rest = jnp.where(lane < LANES, active, rest)
    out = jnp.zeros(shape, F32)
    for index in range(3):
        part = rest.astype(BF16).astype(F32)
        out = jnp.where(row == index, part, out)
        rest = rest - part
    out_ref[...] = out.astype(BF16)


def weight_rows(slab, active, occupation, offset, n):
    shape = jax.ShapeDtypeStruct((8, n), BF16)
    return call(weight_kernel, shape, [SMEM] * 4, vmem=4)(slab, active, occupation, offset)


def wide(row, n):
    return jnp.concatenate([row[:, :LANES]] * (n // LANES), axis=1)


def mix_kernel(place_ref, source_ref, mode_ref, phonon_ref, *refs):
    energies = (len(refs) - 5) // 2
    pieces, outs = refs[:energies], refs[energies : 2 * energies]
    weighted_ref, totals_ref, green, phonon, weights = refs[2 * energies :]
    place = place_ref[0]
    pairs = source_ref.shape[1]
    rows, n = phonon_ref.shape[1:]
    phonon[...] = phonon_ref[...].astype(F32)
    totals = jnp.zeros((1, n), F32)
    for distance in range(energies):
        piece = pieces[distance]
        for part in range(2):
            green[place ^ distance, part] = piece[part * rows : (part + 1) * rows, :].astype(F32)
        parts = piece[2 * rows :, :].astype(F32)
        row = parts[0:1] + parts[1:2] + parts[2:3]
        totals = totals + row
        weights[place ^ distance] = jnp.broadcast_to(wide(row, n), (8, n))
    totals_ref[...] = jnp.broadcast_to(totals, totals_ref.shape)
    step = 16

    @pl.loop(0, rows // step)
    def _(block):
        at = pl.ds(pl.multiple_of(block * step, step), step)
        weighted_real = jnp.zeros((step, n), F32)
        weighted_imag = jnp.zeros((step, n), F32)
        for distance in range(energies):
            energy = place ^ distance
            real = jnp.zeros((step, n), F32)
            imag = jnp.zeros((step, n), F32)
            for pair in range(pairs):
                origin = source_ref[energy, pair]
                factor = phonon[mode_ref[energy, pair], at, :]
                real = real + factor * green[origin, 0, at, :]
                imag = imag + factor * green[origin, 1, at, :]
            outs[distance][0, at, :] = real.astype(BF16)
            outs[distance][1, at, :] = imag.astype(BF16)
            weight = weights[energy, 0:1, :]
            weighted_real = weighted_real + weight * real
            weighted_imag = weighted_imag + weight * imag
        weighted_ref[0, at, :] = weighted_real.astype(BF16)
        weighted_ref[1, at, :] = weighted_imag.astype(BF16)


def mix(place, source, mode, phonon, pieces):
    energies = len(pieces)
    _, rows, n = phonon.shape
    block = jax.ShapeDtypeStruct((2, rows, n), BF16)
    return call(
        mix_kernel,
        [block] * (energies + 1) + [jax.ShapeDtypeStruct((8, n), F32)],
        [SMEM] * 3 + [VMEM] * (energies + 1),
        [
            pltpu.VMEM((energies, 2, rows, n), F32),
            pltpu.VMEM(phonon.shape, F32),
            pltpu.VMEM((energies, 8, n), F32),
        ],
        vmem=12,
        cost=2.0,
    )(place, source, mode, phonon, *pieces)


def finished_rows(sigma, inverse_ref, start, mask, offset, one):
    size, n = sigma.shape[0] // 2, sigma.shape[1]
    eye = (
        lax.broadcasted_iota(jnp.int32, (size, n), 0) + start
        == lax.broadcasted_iota(jnp.int32, (size, n), 1)
    ).astype(F32)
    real, imag = product(sigma, inverse_ref[...])
    own_real = inverse_ref[pl.ds(start, size), :].astype(F32)
    own_imag = inverse_ref[pl.ds(pl.multiple_of(n + start, size), size), :].astype(F32)
    return mask * real + offset * own_real + one * eye, mask * imag + offset * own_imag


def right_kernel(place_ref, slab_ref, active_ref, offset_ref, inverse_ref, *refs, first):
    pieces, out_ref, rows_ref = refs[:-2], refs[-2], refs[-1]
    count = len(pieces)
    place = place_ref[0] ^ first
    rows = pieces[0].shape[1]
    total = count * rows
    for index, piece in enumerate(pieces):
        at = (place ^ index) & (count - 1)
        for part in range(2):
            rows_ref[pl.ds(pl.multiple_of(part * total + at * rows, rows), rows), :] = piece[part]
    mask = jnp.where(slab_ref[0] < active_ref[0], 1.0, 0.0)
    start = pl.multiple_of(place // count * total, total)
    store(out_ref, finished_rows(rows_ref[...], inverse_ref, start, mask, offset_ref[0], 1.0))


def right_rows(scalars, inverse, pieces, first):
    _, rows, n = pieces[0].shape
    total = rows * len(pieces)
    return call(
        functools.partial(right_kernel, first=first),
        jax.ShapeDtypeStruct((2 * total, n), BF16),
        [SMEM] * 4 + [VMEM] * (1 + len(pieces)),
        [pltpu.VMEM((2 * total, n), BF16)],
        vmem=12,
        cost=0.8,
    )(*scalars, inverse, *pieces)


def weighted_kernel(place_ref, inverse_ref, sigma_ref, totals_ref, out_ref):
    _, rows, n = sigma_ref.shape
    start = pl.multiple_of(place_ref[0] * rows, rows)
    one = wide(totals_ref[0:1, LANES : 2 * LANES], n)
    offset = wide(totals_ref[0:1, 2 * LANES : 3 * LANES], n)
    sigma = sigma_ref[...].reshape(2 * rows, n)
    store(out_ref, finished_rows(sigma, inverse_ref, start, 1.0, offset, one))


def weighted_rows(place, inverse, sigma, totals):
    _, rows, n = sigma.shape
    return call(
        weighted_kernel,
        jax.ShapeDtypeStruct((2 * rows, n), BF16),
        [SMEM] + [VMEM] * 3,
        vmem=8,
        cost=0.3,
    )(place, inverse, sigma, totals)


def own_matrices_kernel(slab_ref, self_ref, partner_ref, coupling_ref, low_ref, high_ref, factor_ref, both):
    core = slab_ref[0] & 1
    both[core] = self_ref[...]
    both[1 - core] = partner_ref[...]
    coupling = coupling_ref[...]
    low_ref[...] = mxu(both[0], coupling).astype(BF16)
    high_ref[...] = mxu(both[1], coupling).astype(BF16)

    @pl.when(core == 0)
    def _():
        store(factor_ref, product(high_ref[...], self_ref[...]))

    @pl.when(core != 0)
    def _():
        factor_ref[...] = jnp.zeros_like(factor_ref)


def own_matrices(slab, own, partner, coupling):
    n = coupling.shape[0]
    matrix = jax.ShapeDtypeStruct((2 * n, n), BF16)
    return call(
        own_matrices_kernel,
        [matrix, matrix, matrix],
        [SMEM] + [VMEM] * 3,
        [pltpu.VMEM((2, 2 * n, n), BF16)],
        vmem=20,
        cost=0.0,
    )(slab, own, partner, coupling)


def far_matrices_kernel(slab_ref, chain_ref, self_ref, partner_ref, coupling_ref, high_ref, moves, factors, *more):
    core = slab_ref[0] & 1
    low, high = core, 1 - core

    def chain_and_high(high_inverse):
        step = mxu(high_inverse, coupling_ref[...]).astype(BF16)
        store(moves.at[high], product(chain_ref[...], step))

    @pl.when(core == 0)
    def _():
        chain_and_high(partner_ref[...])
        moves[low] = moves[high]
        for chain in more:
            step = mxu(self_ref[...], coupling_ref[...]).astype(BF16)
            store(chain, product(moves[high], step))

    @pl.when(core != 0)
    def _():
        moves[low] = chain_ref[...]
        for chain in more:
            chain_and_high(self_ref[...])
            step = mxu(partner_ref[...], coupling_ref[...]).astype(BF16)
            store(chain, product(moves[high], step))

    store(moves.at[high], product(high_ref[...], moves[low]))
    for place in range(2):
        store(factors.at[place], product(moves[place], self_ref[...]))


def far_matrices(slab, chain, far_self, far_partner, coupling, high, goes_on):
    n = coupling.shape[0]
    matrix = jax.ShapeDtypeStruct((2 * n, n), BF16)
    pair = jax.ShapeDtypeStruct((2, 2 * n, n), BF16)
    return call(
        far_matrices_kernel,
        [pair, pair] + [matrix] * goes_on,
        [SMEM] + [VMEM] * 5,
        vmem=24,
        cost=5.2,
    )(slab, chain, far_self, far_partner, coupling, high)


def block_start(place, group, n, energies):
    first, last = group
    size = n * (last - first) // energies
    return size, pl.multiple_of((place ^ first) // (last - first) * size, size)


def moved_rows(rows, move):
    n = move.shape[0] // 2
    return complex_of(mxu_nt(rows, move[:n]), mxu_nt(rows, move[n:]))


def moved_term(rows, move, factor):
    moved = [part.astype(BF16) for part in moved_rows(rows, move)]
    return complex_of(mxu(factor, moved[0]), mxu(factor, moved[1]))


def own_terms_kernel(place_ref, high_ref, own_ref, factor_ref, *refs, groups, energies):
    chunks, (self_ref, partner_ref, rows_ref) = refs[:-3], refs[-3:]
    n = self_ref.shape[1]
    for group, chunk in zip(groups, chunks):
        size, start = block_start(place_ref[0], group, n, energies)
        for part in range(2):
            at = pl.ds(pl.multiple_of(part * n + start, size), size)
            rows_ref[at, :] = chunk[part * size : (part + 1) * size, :]
    store(partner_ref, moved_term(rows_ref[...], high_ref[...], factor_ref[...]))
    store(self_ref, product(own_ref[...], rows_ref[...]))


def own_terms(place, high, own, factor, chunks, groups, energies):
    n = own.shape[1]
    total = jax.ShapeDtypeStruct((2 * n, n), F32)
    return call(
        functools.partial(own_terms_kernel, groups=groups, energies=energies),
        [total, total],
        [SMEM] + [VMEM] * (3 + len(chunks)),
        [pltpu.VMEM((2 * n, n), BF16)],
        vmem=20,
        cost=3.6,
    )(place, high, own, factor, *chunks)


def far_terms_kernel(place_ref, total_ref, *refs, target, group, energies):
    out_ref, refs = refs[-1], refs[:-1]
    n = total_ref.shape[1]
    total = [total_ref[:n, :], total_ref[n:, :]]
    size, start = block_start(place_ref[0], group, n, energies)
    for term in range(len(refs) // 3):
        block, moves, factors = refs[3 * term : 3 * term + 3]
        factor = factors.at[target]
        parts = moved_term(block[: 2 * size, :], moves[target], factor[:, pl.ds(start, size)])
        total = [a + b for a, b in zip(total, parts)]
    store(out_ref, total)


def far_terms(place, total, terms, group, target, dtype, energies):
    n = total.shape[1]
    arrays = [array for term in terms for array in term]
    return call(
        functools.partial(far_terms_kernel, target=target, group=group, energies=energies),
        jax.ShapeDtypeStruct((2 * n, n), dtype),
        [SMEM] + [VMEM] * (1 + len(arrays)),
        vmem=20 + 5 * (len(terms) - 1),
        cost=1.8,
    )(place, total, *arrays)


def diagonal_kernel(place_ref, inverse_ref, high_ref, factor_ref, rows_ref, *refs, rows):
    out_ref, refs = refs[-1], refs[:-1]
    n = rows_ref.shape[1]
    pick = (
        lax.broadcasted_iota(jnp.int32, (rows, n), 0) + place_ref[0] * rows
        == lax.broadcasted_iota(jnp.int32, (rows, n), 1)
    ).astype(BF16)

    def part(first, second):
        real, imag = mxu_nt(pick, first[:n]), mxu_nt(pick, first[n:])
        return jnp.sum(real * second[1] + imag * second[0], axis=0, keepdims=True)

    block = rows_ref[...]
    sums = [
        part(inverse_ref[...], (block[:rows].astype(F32), block[rows:].astype(F32))),
        part(factor_ref[...], moved_rows(block, high_ref[...])),
    ]
    for far in range(len(refs) // 3):
        far_ref, moves, factors = refs[3 * far : 3 * far + 3]
        block = far_ref[...]
        for target in range(2):
            sums[target] += part(factors[target], moved_rows(block, moves[target]))
    for target in range(2):
        out_ref[target : target + 1, :] = sums[target]


def diagonal_sums(place, inverse, high, factor, rows, far, energies):
    n = inverse.shape[1]
    arrays = [array for term in far for array in term]
    return call(
        functools.partial(diagonal_kernel, rows=n // energies),
        jax.ShapeDtypeStruct((2, n), F32),
        [SMEM] + [VMEM] * (4 + len(arrays)),
        vmem=20 + 5 * (len(far) - 1),
        cost=2.4,
    )(place, inverse, high, factor, rows, *arrays)


def add_kernel(first_ref, second_ref, out_ref):
    out_ref[...] = first_ref[...] + second_ref[...]


def add(first, second):
    shape = jax.ShapeDtypeStruct(first.shape, first.dtype)
    return call(add_kernel, shape, [VMEM] * 2, vmem=4)(first, second)


def finish_kernel(own_ref, partner_ref, own_density_ref, partner_density_ref, green_ref, density_ref):
    green_ref[...] = (own_ref[...] + partner_ref[...].astype(F32)).astype(BF16)
    density_ref[...] = -(own_density_ref[0:1, :] + partner_density_ref[1:2, :])


def finish(own, partner, own_density, partner_density):
    n = own.shape[1]
    return call(
        finish_kernel,
        [jax.ShapeDtypeStruct((2 * n, n), BF16), jax.ShapeDtypeStruct((1, n), F32)],
        [VMEM] * 4,
        cost=1.2,
    )(own, partner, own_density, partner_density)


def exchange(x, axis, distance):
    size = lax.axis_size(axis)
    return lax.ppermute(x, axis, [(i, i ^ distance) for i in range(size)])


def shift(x, axis, by):
    size = lax.axis_size(axis)
    return lax.ppermute(x, axis, [(i, i + by) for i in range(size - by)])


def after(x, *others):
    return lax.optimization_barrier((x, *others))[0]


def exchange_all(pieces, order, window):
    received = list(pieces)
    for at, distance in enumerate(order):
        piece = pieces[distance]
        if at >= window:
            piece = after(piece, received[order[at - window]])
        received[distance] = exchange(piece, "energy", distance)
    return received


def local(
    green_prev,
    slab_inverse,
    coupling_block,
    phonon_coupling,
    offset,
    occupation,
    pair_source,
    pair_mode,
    active_slabs,
):
    energies = pair_source.shape[0]
    n = coupling_block.shape[0]
    rows = n // energies
    slabs = lax.axis_size("slab")
    place = lax.axis_index("energy").astype(jnp.int32)
    slab = lax.axis_index("slab").astype(jnp.int32)
    core = slab & 1
    place_one = place[None]
    slab_one = slab[None]
    column = slab_inverse[0].reshape(2 * n, n)
    green = green_prev[0, 0]

    half = energies // 2
    partner = exchange(column, "slab", 1)
    far_selves = [shift(column, "slab", behind) for behind in range(2, slabs, 2)]
    weights = weight_rows(slab_one, active_slabs, occupation, offset, n)
    sent = [
        jnp.concatenate(
            [lax.dynamic_slice_in_dim(part, (place ^ distance) * rows, rows) for part in green]
            + [weights]
        )
        for distance in range(energies)
    ]
    sent[1] = after(sent[1], partner)
    pieces = exchange_all(sent, range(1, energies), energies)
    low_move, high_move, own_factor = own_matrices(slab_one, column, partner, coupling_block)
    pieces[0] = after(pieces[0], high_move)
    *mixed, weighted, totals = mix(place_one, pair_source, pair_mode, phonon_coupling, pieces)
    far_partners = [exchange(after(far_self, mixed[1]), "slab", 1) for far_self in far_selves]
    back = exchange_all(mixed, range(1, energies), energies)
    back[1] = after(back[1], *far_partners)

    scalars = (place_one, slab_one, active_slabs, offset)
    near, cross = (0, half), (half, energies)
    own_weighted = weighted_rows(place_one, column, weighted, totals)
    far_weighted = [shift(own_weighted, "slab", behind) for behind in range(2, slabs, 2)]
    back[0] = after(back[0], own_weighted)
    own_near = right_rows(scalars, column, back[:half], 0)

    chain = after(low_move, own_near, *far_weighted)
    far = []
    for index, (far_self, far_partner) in enumerate(zip(far_selves, far_partners)):
        moves, factors, *chain = far_matrices(
            slab_one,
            chain if index == 0 else chain[0],
            far_self,
            far_partner,
            coupling_block,
            high_move,
            index + 1 < len(far_selves),
        )
        far.append((moves, factors))
    density = diagonal_sums(
        place_one,
        column,
        high_move,
        own_factor,
        own_weighted,
        [(rows, *matrices) for rows, matrices in zip(far_weighted, far)],
        energies,
    )

    back[half] = after(back[half], density)
    own_cross = right_rows(scalars, column, back[half:], half)
    far_near = [shift(own_near, "slab", behind) for behind in range(2, slabs, 2)]
    far_cross = [shift(own_cross, "slab", behind) for behind in range(2, slabs, 2)]

    for_self, for_partner = own_terms(
        place_one, high_move, column, own_factor, [own_near, own_cross], (near, cross), energies
    )
    near_terms = [(rows, *matrices) for rows, matrices in zip(far_near, far)]
    cross_terms = [(rows, *matrices) for rows, matrices in zip(far_cross, far)]
    def energy_step(density, distance):
        return add(density, exchange(density, "energy", distance))

    def far_sum(total, terms, group, target, dtype=F32):
        return far_terms(place_one, total, terms, group, target, dtype, energies) if terms else total

    distances = [1 << bit for bit in range(energies.bit_length() - 1)]
    density = energy_step(density, distances[0])
    for_partner = far_sum(for_partner, near_terms, near, 1)
    for_self = far_sum(after(for_self, density), near_terms, near, 0)
    density = energy_step(density, distances[1])
    for_partner = far_sum(after(for_partner, density, for_self), cross_terms, cross, 1, BF16).astype(BF16)
    for distance in distances[2:]:
        density = energy_step(density, distance)
    from_partner = exchange(for_partner, "slab", 1)
    density_partner = exchange(density, "slab", 1)
    for_self = far_sum(for_self, cross_terms, cross, 0)
    current, density = finish(for_self, from_partner, density, density_partner)
    return (current.reshape(1, 1, 2, n, n), density)


def solution(mesh):
    in_specs = (
        P("energy", "slab", None, None, None),
        P("slab", None, None, None),
        P(),
        P(None, "energy", None),
        P("energy"),
        P("energy"),
        P(),
        P(),
        P("energy"),
    )
    out_specs = (P("energy", "slab", None, None, None), P("slab", None))
    return jax.shard_map(local, mesh=mesh, in_specs=in_specs, out_specs=out_specs, check_vma=False)
```

time: 97 us -> 95.4 us (0.984)
  blocking collectives: 11.8 us -> 0 us
  starting transfers between devices: 40.2 us -> 46.9 us
  waiting for transfers between devices: 14 us -> 18.9 us
    all_to_all x1 -> x0, blocking collectives: 11.8 us -> none  [local(): lax.all_to_all(spread, 'energy', 0, 0, tiled=True)]
    ppermute x17 -> x21, waiting for transfers between devices: 10.4 us -> 18.9 us  [exchange(): return lax.ppermute(x, axis, [(i, i ^ distance) for i in range(size)])]
    ppermute x17 -> x21, starting transfers between devices: 32.6 us -> 37.7 us  [exchange(): return lax.ppermute(x, axis, [(i, i ^ distance) for i in range(size)])]
    ppermute x3 -> x4, waiting for transfers between devices: 3.59 us -> 0.01 us  [shift(): return lax.ppermute(x, axis, [(i, i + by) for i in range(size - by)])]
    pallas_call x6 -> x12, Pallas kernels: 12 us -> 14.2 us  [the longest x4 5.86 us: far_terms(): call(functools.partial(far_terms_kernel, target=target, group=group, ener...]
    ppermute x3 -> x4, starting transfers between devices: 7.64 us -> 9.24 us  [shift(): return lax.ppermute(x, axis, [(i, i + by) for i in range(size - by)])]
    another operation x0 -> x1, local copies, waits for them, and re-layouts: none -> 1.27 us  [local(): sent = [jnp.concatenate([lax.dynamic_slice_in_dim(part, (place ^ distance...]
    dynamic_slice x1, local copies, waits for them, and re-layouts: 1.4 us -> 0.15 us  [local(): lax.dynamic_slice_in_dim(part, (place ^ distance) * rows, rows)]
  transfers between devices with their start and end apart: 20 -> 25, of which waited for: 5 -> 5; matrix products, arithmetic and copies ran while one was open for 1% -> 2% of each run, Pallas kernels for 23% -> 23%
where the time goes in v4:
time: 95.4 us; the launch traced here: 95.1 us
  starting transfers between devices  46.9 us (49%)
  Pallas kernels  24.7 us (26%)
  waiting for transfers between devices  18.9 us (20%)
  between operations  2.96 us (3%)
  local copies, waits for them, and re-layouts  1.45 us (2%)
    ppermute x21, starting transfers between devices, exchange(): return lax.ppermute(x, axis, [(i, i ^ distance) for i in range(size)])  37.7 us
    ppermute x21, waiting for transfers between devices, exchange(): return lax.ppermute(x, axis, [(i, i ^ distance) for i in range(size)])  18.9 us
    ppermute x4, starting transfers between devices, shift(): return lax.ppermute(x, axis, [(i, i + by) for i in range(size - by)])  9.24 us
    pallas_call x4, Pallas kernels, far_terms(): call(functools.partial(far_terms_kernel, target=target, group=group, ener...  5.86 us
    pallas_call x1, Pallas kernels, far_matrices(): call(far_matrices_kernel, [pair, pair] + [matrix] * goes_on, [SMEM] + [VM...  5.25 us
    pallas_call x1, Pallas kernels, own_terms(): call(functools.partial(own_terms_kernel, groups=groups, energies=energies...  3.56 us
    pallas_call x1, Pallas kernels, own_matrices(): call(own_matrices_kernel, [matrix, matrix, matrix], [SMEM] + [VMEM] * 3,...  2.55 us
    pallas_call x1, Pallas kernels, diagonal_sums(): call(functools.partial(diagonal_kernel, rows=n // energies), jax.ShapeDty...  2.43 us
  transfers between devices with their start and end apart: 25, of which 5 were waited for; matrix products, arithmetic and copies ran while one was open for 2% of the time, Pallas kernels for 23%

profile of v4, /device:TPU:0, one launch (start us, length us, event | category | flops | bytes accessed | tf_op | source)
XLA Modules:
  0.0 95.1 jit_solution(3005894449582847813)
XLA Ops:
  0.6 0.5 collective-permute-start
  1.1 4.5 %collective-permute-start.9 = (bf16[1024,512]{1,0:T(8,128)(2,1)}, bf16[1024,512]{1,0:T(8,128)(2,1)S(1)}, u32[]{:S(2)}, u32[]{:S(2)}) collective-permute-start(bf16[1024,512]{1,0:T(8,128)(2,1)} %bitcast.37), channel_id=1, source_target_pairs={{0,2},{1,3},{4,6},{5,7},{8,10},{9,11},{12,14},{13,15},{16,18},{17,... | collective-permute-start | bytes 3145736 | tf_op jit(solution)/shard_map/ppermute | solution.py:409
  7.6 1.3 %fusion = (bf16[1,1,1,512,512]{4,3,2,1,0:T(8,128)(2,1)S(1)}, bf16[1,1,1,512,512]{4,3,2,1,0:T(8,128)(2,1)S(1)}) fusion(bf16[1,1,2,512,512]{4,3,2,1,0:T(8,128)(2,1)} %param.9), kind=kLoop, calls=%fused_computation.24 | loop fusion | bytes 2097152 | tf_op jit(solution)/shard_map/unstack | solution.py:455
  8.9 0.0 copy-start
  8.9 0.0 copy-start.1
  8.9 0.2 dynamic-slice_bitcast_fusion
  9.1 0.0 copy-start.2
  9.1 0.1 pad_maximum_fusion
  9.2 1.6 %collective-permute-start.2 = (bf16[136,512]{1,0:T(8,128)(2,1)S(1)}, bf16[136,512]{1,0:T(8,128)(2,1)S(1)}, u32[]{:S(2)}, u32[]{:S(2)}) collective-permute-start(bf16[136,512]{1,0:T(8,128)(2,1)S(1)} %get-tuple-element.78), channel_id=1, source_target_pairs={{0,8},{4,12},{8,0},{12,4},{16,24},{20,28},{24,16},{28,20},{1,9},{5... | collective-permute-start | bytes 417800 | tf_op jit(solution)/shard_map/ppermute | solution.py:404
  10.9 1.4 %collective-permute-start.3 = (bf16[136,512]{1,0:T(8,128)(2,1)S(1)}, bf16[136,512]{1,0:T(8,128)(2,1)S(1)}, u32[]{:S(2)}, u32[]{:S(2)}) collective-permute-start(bf16[136,512]{1,0:T(8,128)(2,1)S(1)} %get-tuple-element.79), channel_id=1, source_target_pairs={{0,12},{4,8},{8,4},{12,0},{16,28},{20,24},{24,20},{28,16},{1,13},{... | collective-permute-start | bytes 417800 | tf_op jit(solution)/shard_map/ppermute | solution.py:404
  12.3 2.6 %collective-permute-start.4 = (bf16[136,512]{1,0:T(8,128)(2,1)S(1)}, bf16[136,512]{1,0:T(8,128)(2,1)S(1)}, u32[]{:S(2)}, u32[]{:S(2)}) collective-permute-start(bf16[136,512]{1,0:T(8,128)(2,1)S(1)} %get-tuple-element.80), channel_id=1, source_target_pairs={{0,16},{4,20},{8,24},{12,28},{16,0},{20,4},{24,8},{28,12},{1,17},{... | collective-permute-start | bytes 417800 | tf_op jit(solution)/shard_map/ppermute | solution.py:404
  14.9 0.3 collective-permute-start.5
  15.2 4.7 %collective-permute-done.2.refs_2_ = bf16[136,512]{1,0:T(8,128)(2,1)S(1)} collective-permute-done((bf16[136,512]{1,0:T(8,128)(2,1)S(1)}, bf16[136,512]{1,0:T(8,128)(2,1)S(1)}, u32[]{:S(2)}, u32[]{:S(2)}) %collective-permute-start.2) | collective-permute-done | bytes 139296 | tf_op jit(solution)/shard_map/ppermute | solution.py:404
  20.0 3.9 %collective-permute-start.7 = (bf16[136,512]{1,0:T(8,128)(2,1)S(1)}, bf16[136,512]{1,0:T(8,128)(2,1)S(1)}, u32[]{:S(2)}, u32[]{:S(2)}) collective-permute-start(bf16[136,512]{1,0:T(8,128)(2,1)S(1)} %get-tuple-element.76), channel_id=1, source_target_pairs={{0,28},{4,24},{8,20},{12,16},{16,12},{20,8},{24,4},{28,0},{1,29},{... | collective-permute-start | bytes 417800 | tf_op jit(solution)/shard_map/ppermute | solution.py:404
  23.8 0.0 collective-permute-done.3.refs_3_
  23.9 2.2 %collective-permute-start.6 = (bf16[136,512]{1,0:T(8,128)(2,1)S(1)}, bf16[136,512]{1,0:T(8,128)(2,1)S(1)}, u32[]{:S(2)}, u32[]{:S(2)}) collective-permute-start(bf16[136,512]{1,0:T(8,128)(2,1)S(1)} %get-tuple-element.82), channel_id=1, source_target_pairs={{0,24},{4,28},{8,16},{12,20},{16,8},{20,12},{24,0},{28,4},{1,25},{... | collective-permute-start | bytes 417800 | tf_op jit(solution)/shard_map/ppermute | solution.py:404
  26.1 2.5 %shard_map.104 = (bf16[1024,512]{1,0:T(8,128)(2,1)S(1)}, bf16[1024,512]{1,0:T(8,128)(2,1)S(1)}, bf16[1024,512]{1,0:T(8,128)(2,1)S(1)}) custom-call(s32[1]{0:T(128)} %bitcast.1.slab_ref, bf16[1024,512]{1,0:T(8,128)(2,1)S(1)} %bitcast.38, bf16[1024,512]{1,0:T(8,128)(2,1)S(1)} %collective-permute-done.partner_ref, bf16[512,512]{1,0:T(8,128)(2,1)S(1)} %copy-done.1), custom_call_target="tpu_custom_call" | custom-call | flops 1024 | bytes 1024 | tf_op jit(solution)/shard_map/pallas_call | solution.py:222
  28.7 6.6 %collective-permute-done.5.refs_5_ = bf16[136,512]{1,0:T(8,128)(2,1)S(1)} collective-permute-done((bf16[136,512]{1,0:T(8,128)(2,1)S(1)}, bf16[136,512]{1,0:T(8,128)(2,1)S(1)}, u32[]{:S(2)}, u32[]{:S(2)}) %collective-permute-start.5) | collective-permute-done | bytes 139296 | tf_op jit(solution)/shard_map/ppermute | solution.py:404
  35.3 2.0 %shard_map.106 = (bf16[2,64,512]{2,1,0:T(8,128)(2,1)S(1)}, bf16[2,64,512]{2,1,0:T(8,128)(2,1)S(1)}, bf16[2,64,512]{2,1,0:T(8,128)(2,1)S(1)}, bf16[2,64,512]{2,1,...) custom-call(s32[1]{0:T(128)} %bitcast.place_ref, ...), custom_call_target="tpu_custom_call" | custom-call | flops 1024 | bytes 6601024 | tf_op jit(solution)/shard_map/pallas_call | solution.py:128
  37.4 0.1 collective-permute-start.10
  37.4 0.6 collective-permute-start.8
  38.0 4.9 %collective-permute-start.11 = (bf16[2,64,512]{2,1,0:T(8,128)(2,1)S(1)}, bf16[2,64,512]{2,1,0:T(8,128)(2,1)S(1)}, u32[]{:S(2)}, u32[]{:S(2)}) collective-permute-start(bf16[2,64,512]{2,1,0:T(8,128)(2,1)S(1)} %get-tuple-element.41), channel_id=1, source_target_pairs={{0,8},{4,12},{8,0},{12,4},{16,24},{20,28},{24,16},{28,20},{1,9},{5... | collective-permute-start | bytes 393224 | tf_op jit(solution)/shard_map/ppermute | solution.py:404
  42.9 0.8 collective-permute-start.12
  43.8 0.3 shard_map.107.rows_ref
  44.1 1.5 %collective-permute-start.14 = (bf16[128,512]{1,0:T(8,128)(2,1)S(1)}, bf16[128,512]{1,0:T(8,128)(2,1)S(1)}, u32[]{:S(2)}, u32[]{:S(2)}) collective-permute-start(bf16[128,512]{1,0:T(8,128)(2,1)S(1)} %shard_map.107.rows_ref), channel_id=1, source_target_pairs={{0,2},{1,3},{4,6},{5,7},{8,10},{9,11},{12,14},{13,15},{16,18},{17,... | collective-permute-start | bytes 393224 | tf_op jit(solution)/shard_map/ppermute | solution.py:409
  45.6 4.5 %collective-permute-start.13 = (bf16[2,64,512]{2,1,0:T(8,128)(2,1)S(1)}, bf16[2,64,512]{2,1,0:T(8,128)(2,1)S(1)}, u32[]{:S(2)}, u32[]{:S(2)}) collective-permute-start(bf16[2,64,512]{2,1,0:T(8,128)(2,1)S(1)} %get-tuple-element.43), channel_id=1, source_target_pairs={{0,16},{4,20},{8,24},{12,28},{16,0},{20,4},{24,8},{28,12},{1,17},{... | collective-permute-start | bytes 393224 | tf_op jit(solution)/shard_map/ppermute | solution.py:404
  50.1 2.0 %collective-permute-start.15 = (bf16[2,64,512]{2,1,0:T(8,128)(2,1)S(1)}, bf16[2,64,512]{2,1,0:T(8,128)(2,1)S(1)}, u32[]{:S(2)}, u32[]{:S(2)}) collective-permute-start(bf16[2,64,512]{2,1,0:T(8,128)(2,1)S(1)} %get-tuple-element.49), channel_id=1, source_target_pairs={{0,20},{4,16},{8,28},{12,24},{16,4},{20,0},{24,12},{28,8},{1,21},{... | collective-permute-start | bytes 393224 | tf_op jit(solution)/shard_map/ppermute | solution.py:404
  52.0 3.6 %collective-permute-start.16 = (bf16[2,64,512]{2,1,0:T(8,128)(2,1)S(1)}, bf16[2,64,512]{2,1,0:T(8,128)(2,1)S(1)}, u32[]{:S(2)}, u32[]{:S(2)}) collective-permute-start(bf16[2,64,512]{2,1,0:T(8,128)(2,1)S(1)} %get-tuple-element.50), channel_id=1, source_target_pairs={{0,24},{4,28},{8,16},{12,20},{16,8},{20,12},{24,0},{28,4},{1,25},{... | collective-permute-start | bytes 393224 | tf_op jit(solution)/shard_map/ppermute | solution.py:404
  55.7 0.1 collective-permute-start.17
  55.8 0.8 shard_map.108.refs_0_
  56.6 1.5 %collective-permute-start.19 = (bf16[512,512]{1,0:T(8,128)(2,1)S(1)}, bf16[512,512]{1,0:T(8,128)(2,1)S(1)}, u32[]{:S(2)}, u32[]{:S(2)}) collective-permute-start(bf16[512,512]{1,0:T(8,128)(2,1)S(1)} %shard_map.108.refs_0_), channel_id=1, source_target_pairs={{0,2},{1,3},{4,6},{5,7},{8,10},{9,11},{12,14},{13,15},{16,18},{17,... | collective-permute-start | bytes 1572872 | tf_op jit(solution)/shard_map/ppermute | solution.py:409
  58.2 5.2 %shard_map.109 = (bf16[2,1024,512]{2,1,0:T(8,128)(2,1)S(1)}, bf16[2,1024,512]{2,1,0:T(8,128)(2,1)S(1)}) custom-call(s32[1]{0:T(128)} %bitcast.1.slab_ref, bf16[1024,512]{1,0:T(8,128)(2,1)S(1)} %get-tuple-element.45.chain_ref, bf16[1024,512]{1,0:T(8,128)(2,1)S(1)} %collective-permute-done.9.self_ref, ...), custom_call_target="tpu_custom_call" | custom-call | flops 1024 | bytes 17161024 | tf_op jit(solution)/shard_map/pallas_call | solution.py:265
  63.4 2.4 %shard_map.110.first_ref = f32[2,512]{1,0:T(2,128)S(1)} custom-call(s32[1]{0:T(128)} %bitcast.place_ref, bf16[1024,512]{1,0:T(8,128)(2,1)S(1)} %bitcast.41, bf16[1024,512]{1,0:T(8,128)(2,1)S(1)} %get-tuple-element.30.high_ref, bf16[1024,512]{1,0:T(8,128)(2,1)S(1)} %get-tuple-element.31.factor_ref, bf16[128,512]{1,0:T(8,128)(2,1)S(1)} %shard_map.107.rows_ref, ...), custom_call_target="tpu_custom_call" | custom-call | flops 1024 | bytes 7921024 | tf_op jit(solution)/shard_map/pallas_call | solution.py:369
  65.9 1.8 %collective-permute-done.15.refs_1_ = bf16[2,64,512]{2,1,0:T(8,128)(2,1)S(1)} collective-permute-done((bf16[2,64,512]{2,1,0:T(8,128)(2,1)S(1)}, bf16[2,64,512]{2,1,0:T(8,128)(2,1)S(1)}, u32[]{:S(2)}, u32[]{:S(2)}) %collective-permute-start.15) | collective-permute-done | bytes 131104 | tf_op jit(solution)/shard_map/ppermute | solution.py:404
  67.6 0.8 shard_map.111.refs_1_
  68.5 1.7 %collective-permute-start.20 = (bf16[512,512]{1,0:T(8,128)(2,1)S(1)}, bf16[512,512]{1,0:T(8,128)(2,1)S(1)}, u32[]{:S(2)}, u32[]{:S(2)}) collective-permute-start(bf16[512,512]{1,0:T(8,128)(2,1)S(1)} %shard_map.111.refs_1_), channel_id=1, source_target_pairs={{0,2},{1,3},{4,6},{5,7},{8,10},{9,11},{12,14},{13,15},{16,18},{17,... | collective-permute-start | bytes 1572872 | tf_op jit(solution)/shard_map/ppermute | solution.py:409
  70.2 2.3 %collective-permute-start.18 = (f32[2,512]{1,0:T(2,128)S(1)}, f32[2,512]{1,0:T(2,128)S(1)}, u32[]{:S(2)}, u32[]{:S(2)}) collective-permute-start(f32[2,512]{1,0:T(2,128)S(1)} %shard_map.110.first_ref), channel_id=1, source_target_pairs={{0,4},{4,0},{8,12},{12,8},{16,20},{20,16},{24,28},{28,24},{1,5},{5... | collective-permute-start | bytes 12296 | tf_op jit(solution)/shard_map/ppermute | solution.py:404
  72.5 1.6 %collective-permute-done.18.second_ref = f32[2,512]{1,0:T(2,128)S(1)} collective-permute-done((f32[2,512]{1,0:T(2,128)S(1)}, f32[2,512]{1,0:T(2,128)S(1)}, u32[]{:S(2)}, u32[]{:S(2)}) %collective-permute-start.18) | collective-permute-done | bytes 4128 | tf_op jit(solution)/shard_map/ppermute | solution.py:404
  74.1 5.6 %collective-permute-start.21 = (f32[2,512]{1,0:T(2,128)S(1)}, f32[2,512]{1,0:T(2,128)S(1)}, u32[]{:S(2)}, u32[]{:S(2)}) collective-permute-start(f32[2,512]{1,0:T(2,128)S(1)} %shard_map.113.first_ref), channel_id=1, source_target_pairs={{0,8},{4,12},{8,0},{12,4},{16,24},{20,28},{24,16},{28,20},{1,9},{5... | collective-permute-start | bytes 12296 | tf_op jit(solution)/shard_map/ppermute | solution.py:404
  79.8 3.6 %shard_map.112 = (f32[1024,512]{1,0:T(8,128)S(1)}, f32[1024,512]{1,0:T(8,128)S(1)}) custom-call(s32[1]{0:T(128)} %bitcast.place_ref, bf16[1024,512]{1,0:T(8,128)(2,1)S(1)} %get-tuple-element.30.high_ref, bf16[1024,512]{1,0:T(8,128)(2,1)S(1)} %bitcast.43, bf16[1024,512]{1,0:T(8,128)(2,1)S(1)} %get-tuple-element.31.factor_ref, ...), custom_call_target="tpu_custom_call" | custom-call | flops 1024 | bytes 11881024 | tf_op jit(solution)/shard_map/pallas_call | solution.py:305
  83.4 1.5 %shard_map.116.total_ref = f32[1024,512]{1,0:T(8,128)S(1)} custom-call(s32[1]{0:T(128)} %bitcast.place_ref, f32[1024,512]{1,0:T(8,128)S(1)} %get-tuple-element.54.total_ref, bf16[512,512]{1,0:T(8,128)(2,1)S(1)} %collective-permute-done.19.refs_0_, bf16[2,1024,512]{2,1,0:T(8,128)(2,1)S(1)} %get-tuple-element.46.refs_1_, ...), custom_call_target="tpu_custom_call" | custom-call | flops 1024 | bytes 5941024 | tf_op jit(solution)/shard_map/pallas_call | solution.py:331
  84.8 1.5 %shard_map.114.total_ref = f32[1024,512]{1,0:T(8,128)S(1)} custom-call(s32[1]{0:T(128)} %bitcast.place_ref, f32[1024,512]{1,0:T(8,128)S(1)} %get-tuple-element.53.total_ref, bf16[512,512]{1,0:T(8,128)(2,1)S(1)} %collective-permute-done.19.refs_0_, bf16[2,1024,512]{2,1,0:T(8,128)(2,1)S(1)} %get-tuple-element.46.refs_1_, ...), custom_call_target="tpu_custom_call" | custom-call | flops 1024 | bytes 5941024 | tf_op jit(solution)/shard_map/pallas_call | solution.py:331
  86.3 1.5 %shard_map.118 = bf16[1024,512]{1,0:T(8,128)(2,1)S(1)} custom-call(s32[1]{0:T(128)} %bitcast.place_ref, f32[1024,512]{1,0:T(8,128)S(1)} %shard_map.116.total_ref, bf16[512,512]{1,0:T(8,128)(2,1)S(1)} %collective-permute-done.20.refs_0_, bf16[2,1024,512]{2,1,0:T(8,128)(2,1)S(1)} %get-tuple-element.46.refs_1_, bf16[2,1024,512]{2,1,0:T(8,128)(2,1)S(1)} %get-tuple-element.47.refs_2_), custom_call_target="tpu_custom_call" | custom-call | flops 1024 | bytes 5941024 | tf_op jit(solution)/shard_map/pallas_call | solution.py:331
  87.8 0.1 collective-permute-start.22
  87.9 0.4 collective-permute-start.23
  88.3 4.1 %collective-permute-done.23.second_ref = f32[2,512]{1,0:T(2,128)S(1)} collective-permute-done((f32[2,512]{1,0:T(2,128)S(1)}, f32[2,512]{1,0:T(2,128)S(1)}, u32[]{:S(2)}, u32[]{:S(2)}) %collective-permute-start.23) | collective-permute-done | bytes 4128 | tf_op jit(solution)/shard_map/ppermute | solution.py:404
  92.4 1.5 %shard_map.115.own_ref = f32[1024,512]{1,0:T(8,128)S(1)} custom-call(s32[1]{0:T(128)} %bitcast.place_ref, f32[1024,512]{1,0:T(8,128)S(1)} %shard_map.114.total_ref, bf16[512,512]{1,0:T(8,128)(2,1)S(1)} %collective-permute-done.20.refs_0_, bf16[2,1024,512]{2,1,0:T(8,128)(2,1)S(1)} %get-tuple-element.46.refs_1_, ...), custom_call_target="tpu_custom_call" | custom-call | flops 1024 | bytes 5941024 | tf_op jit(solution)/shard_map/pallas_call | solution.py:331
  93.9 1.1 %shard_map.120 = (bf16[1024,512]{1,0:T(8,128)(2,1)}, f32[1,512]{1,0:T(1,128)}) custom-call(f32[1024,512]{1,0:T(8,128)S(1)} %shard_map.115.own_ref, bf16[1024,512]{1,0:T(8,128)(2,1)S(1)} %collective-permute-done.22.partner_ref, f32[2,512]{1,0:T(2,128)S(1)} %shard_map.119.own_density_ref, f32[2,512]{1,0:T(2,128)S(1)} %collective-permute-done.24.partner_density_ref), custom_call_target="tpu_custom_call" | custom-call | flops 1024 | bytes 3961024 | tf_op jit(solution)/shard_map/pallas_call | solution.py:394
  (33 shorter events, 0.1 us)
Async XLA Ops:
  0.6 14.2 %collective-permute-start = (bf16[1024,512]{1,0:T(8,128)(2,1)}, bf16[1024,512]{1,0:T(8,128)(2,1)S(1)}, u32[]{:S(2)}, u32[]{:S(2)}) collective-permute-start(bf16[1024,512]{1,0:T(8,128)(2,1)} %bitcast.36), channel_id=1, source_target_pairs={{0,1},{1,0},{2,3},{3,2},{4,5},{5,4},{6,7},{7,6},{8,9},{9,8},{10,11... | collective-permute-start | bytes 3145736 | tf_op jit(solution)/shard_map/ppermute | solution.py:404
  1.1 36.2 %collective-permute-start.9 = (bf16[1024,512]{1,0:T(8,128)(2,1)}, bf16[1024,512]{1,0:T(8,128)(2,1)S(1)}, u32[]{:S(2)}, u32[]{:S(2)}) collective-permute-start(bf16[1024,512]{1,0:T(8,128)(2,1)} %bitcast.37), channel_id=1, source_target_pairs={{0,2},{1,3},{4,6},{5,7},{8,10},{9,11},{12,14},{13,15},{16,18},{17,... | collective-permute-start | bytes 3145736 | tf_op jit(solution)/shard_map/ppermute | solution.py:409
  8.9 17.2 %copy-start = (bf16[1,2,512,512]{3,2,1,0:T(8,128)(2,1)S(1)}, bf16[1,2,512,512]{3,2,1,0:T(8,128)(2,1)}, u32[]{:S(2)}) copy-start(bf16[1,2,512,512]{3,2,1,0:T(8,128)(2,1)} %param.10) | copy-start | bytes 3145732
  8.9 17.2 %copy-start.1 = (bf16[512,512]{1,0:T(8,128)(2,1)S(1)}, bf16[512,512]{1,0:T(8,128)(2,1)}, u32[]{:S(2)}) copy-start(bf16[512,512]{1,0:T(8,128)(2,1)} %coupling_ref.3) | copy-start | bytes 1572868
  9.1 26.2 %copy-start.2 = (bf16[4,64,512]{2,1,0:T(8,128)(2,1)S(1)}, bf16[4,64,512]{2,1,0:T(8,128)(2,1)}, u32[]{:S(2)}) copy-start(bf16[4,64,512]{2,1,0:T(8,128)(2,1)} %phonon_ref.1) | copy-start | bytes 786436
  9.1 26.2 %copy-start.3 = (s32[8,6]{1,0:T(8,128)S(1)}, s32[8,6]{1,0:T(8,128)}, u32[]{:S(2)}) copy-start(s32[8,6]{1,0:T(8,128)} %source_ref.1) | copy-start | bytes 580
  9.1 26.2 %copy-start.4 = (s32[8,6]{1,0:T(8,128)S(1)}, s32[8,6]{1,0:T(8,128)}, u32[]{:S(2)}) copy-start(s32[8,6]{1,0:T(8,128)} %mode_ref.1) | copy-start | bytes 580
  9.2 10.8 %collective-permute-start.2 = (bf16[136,512]{1,0:T(8,128)(2,1)S(1)}, bf16[136,512]{1,0:T(8,128)(2,1)S(1)}, u32[]{:S(2)}, u32[]{:S(2)}) collective-permute-start(bf16[136,512]{1,0:T(8,128)(2,1)S(1)} %get-tuple-element.78), channel_id=1, source_target_pairs={{0,8},{4,12},{8,0},{12,4},{16,24},{20,28},{24,16},{28,20},{1,9},{5... | collective-permute-start | bytes 417800 | tf_op jit(solution)/shard_map/ppermute | solution.py:404
  10.9 13.0 %collective-permute-start.3 = (bf16[136,512]{1,0:T(8,128)(2,1)S(1)}, bf16[136,512]{1,0:T(8,128)(2,1)S(1)}, u32[]{:S(2)}, u32[]{:S(2)}) collective-permute-start(bf16[136,512]{1,0:T(8,128)(2,1)S(1)} %get-tuple-element.79), channel_id=1, source_target_pairs={{0,12},{4,8},{8,4},{12,0},{16,28},{20,24},{24,20},{28,16},{1,13},{... | collective-permute-start | bytes 417800 | tf_op jit(solution)/shard_map/ppermute | solution.py:404
  12.3 13.8 %collective-permute-start.4 = (bf16[136,512]{1,0:T(8,128)(2,1)S(1)}, bf16[136,512]{1,0:T(8,128)(2,1)S(1)}, u32[]{:S(2)}, u32[]{:S(2)}) collective-permute-start(bf16[136,512]{1,0:T(8,128)(2,1)S(1)} %get-tuple-element.80), channel_id=1, source_target_pairs={{0,16},{4,20},{8,24},{12,28},{16,0},{20,4},{24,8},{28,12},{1,17},{... | collective-permute-start | bytes 417800 | tf_op jit(solution)/shard_map/ppermute | solution.py:404
  14.9 20.4 %collective-permute-start.5 = (bf16[136,512]{1,0:T(8,128)(2,1)S(1)}, bf16[136,512]{1,0:T(8,128)(2,1)S(1)}, u32[]{:S(2)}, u32[]{:S(2)}) collective-permute-start(bf16[136,512]{1,0:T(8,128)(2,1)S(1)} %get-tuple-element.81), channel_id=1, source_target_pairs={{0,20},{4,16},{8,28},{12,24},{16,4},{20,0},{24,12},{28,8},{1,21},{... | collective-permute-start | bytes 417800 | tf_op jit(solution)/shard_map/ppermute | solution.py:404
  20.0 15.3 %collective-permute-start.7 = (bf16[136,512]{1,0:T(8,128)(2,1)S(1)}, bf16[136,512]{1,0:T(8,128)(2,1)S(1)}, u32[]{:S(2)}, u32[]{:S(2)}) collective-permute-start(bf16[136,512]{1,0:T(8,128)(2,1)S(1)} %get-tuple-element.76), channel_id=1, source_target_pairs={{0,28},{4,24},{8,20},{12,16},{16,12},{20,8},{24,4},{28,0},{1,29},{... | collective-permute-start | bytes 417800 | tf_op jit(solution)/shard_map/ppermute | solution.py:404
  23.9 11.4 %collective-permute-start.6 = (bf16[136,512]{1,0:T(8,128)(2,1)S(1)}, bf16[136,512]{1,0:T(8,128)(2,1)S(1)}, u32[]{:S(2)}, u32[]{:S(2)}) collective-permute-start(bf16[136,512]{1,0:T(8,128)(2,1)S(1)} %get-tuple-element.82), channel_id=1, source_target_pairs={{0,24},{4,28},{8,16},{12,20},{16,8},{20,12},{24,0},{28,4},{1,25},{... | collective-permute-start | bytes 417800 | tf_op jit(solution)/shard_map/ppermute | solution.py:404
  26.1 9.2 %collective-permute-start.1 = (bf16[136,512]{1,0:T(8,128)(2,1)S(1)}, bf16[136,512]{1,0:T(8,128)(2,1)S(1)}, u32[]{:S(2)}, u32[]{:S(2)}) collective-permute-start(bf16[136,512]{1,0:T(8,128)(2,1)S(1)} %get-tuple-element.33), channel_id=1, source_target_pairs={{0,4},{4,0},{8,12},{12,8},{16,20},{20,16},{24,28},{28,24},{1,5},{5... | collective-permute-start | bytes 417800 | tf_op jit(solution)/shard_map/ppermute | solution.py:404
  37.4 18.3 %collective-permute-start.10 = (bf16[1024,512]{1,0:T(8,128)(2,1)S(1)}, bf16[1024,512]{1,0:T(8,128)(2,1)S(1)}, u32[]{:S(2)}, u32[]{:S(2)}) collective-permute-start(bf16[1024,512]{1,0:T(8,128)(2,1)S(1)} %collective-permute-done.9.self_ref), channel_id=1, source_target_pairs={{0,1},{1,0},{2,3},{3,2},{4,5},{5,4},{6,7},{7,6},{8,9},{9,8},{10,11... | collective-permute-start | bytes 3145736 | tf_op jit(solution)/shard_map/ppermute | solution.py:404
  37.4 8.2 %collective-permute-start.8 = (bf16[2,64,512]{2,1,0:T(8,128)(2,1)S(1)}, bf16[2,64,512]{2,1,0:T(8,128)(2,1)S(1)}, u32[]{:S(2)}, u32[]{:S(2)}) collective-permute-start(bf16[2,64,512]{2,1,0:T(8,128)(2,1)S(1)} %get-tuple-element.38), channel_id=1, source_target_pairs={{0,4},{4,0},{8,12},{12,8},{16,20},{20,16},{24,28},{28,24},{1,5},{5... | collective-permute-start | bytes 393224 | tf_op jit(solution)/shard_map/ppermute | solution.py:404
  38.0 12.0 %collective-permute-start.11 = (bf16[2,64,512]{2,1,0:T(8,128)(2,1)S(1)}, bf16[2,64,512]{2,1,0:T(8,128)(2,1)S(1)}, u32[]{:S(2)}, u32[]{:S(2)}) collective-permute-start(bf16[2,64,512]{2,1,0:T(8,128)(2,1)S(1)} %get-tuple-element.41), channel_id=1, source_target_pairs={{0,8},{4,12},{8,0},{12,4},{16,24},{20,28},{24,16},{28,20},{1,9},{5... | collective-permute-start | bytes 393224 | tf_op jit(solution)/shard_map/ppermute | solution.py:404
  42.9 9.1 %collective-permute-start.12 = (bf16[2,64,512]{2,1,0:T(8,128)(2,1)S(1)}, bf16[2,64,512]{2,1,0:T(8,128)(2,1)S(1)}, u32[]{:S(2)}, u32[]{:S(2)}) collective-permute-start(bf16[2,64,512]{2,1,0:T(8,128)(2,1)S(1)} %get-tuple-element.42), channel_id=1, source_target_pairs={{0,12},{4,8},{8,4},{12,0},{16,28},{20,24},{24,20},{28,16},{1,13},{... | collective-permute-start | bytes 393224 | tf_op jit(solution)/shard_map/ppermute | solution.py:404
  44.1 12.5 %collective-permute-start.14 = (bf16[128,512]{1,0:T(8,128)(2,1)S(1)}, bf16[128,512]{1,0:T(8,128)(2,1)S(1)}, u32[]{:S(2)}, u32[]{:S(2)}) collective-permute-start(bf16[128,512]{1,0:T(8,128)(2,1)S(1)} %shard_map.107.rows_ref), channel_id=1, source_target_pairs={{0,2},{1,3},{4,6},{5,7},{8,10},{9,11},{12,14},{13,15},{16,18},{17,... | collective-permute-start | bytes 393224 | tf_op jit(solution)/shard_map/ppermute | solution.py:409
  45.6 20.2 %collective-permute-start.13 = (bf16[2,64,512]{2,1,0:T(8,128)(2,1)S(1)}, bf16[2,64,512]{2,1,0:T(8,128)(2,1)S(1)}, u32[]{:S(2)}, u32[]{:S(2)}) collective-permute-start(bf16[2,64,512]{2,1,0:T(8,128)(2,1)S(1)} %get-tuple-element.43), channel_id=1, source_target_pairs={{0,16},{4,20},{8,24},{12,28},{16,0},{20,4},{24,8},{28,12},{1,17},{... | collective-permute-start | bytes 393224 | tf_op jit(solution)/shard_map/ppermute | solution.py:404
  50.1 17.6 %collective-permute-start.15 = (bf16[2,64,512]{2,1,0:T(8,128)(2,1)S(1)}, bf16[2,64,512]{2,1,0:T(8,128)(2,1)S(1)}, u32[]{:S(2)}, u32[]{:S(2)}) collective-permute-start(bf16[2,64,512]{2,1,0:T(8,128)(2,1)S(1)} %get-tuple-element.49), channel_id=1, source_target_pairs={{0,20},{4,16},{8,28},{12,24},{16,4},{20,0},{24,12},{28,8},{1,21},{... | collective-permute-start | bytes 393224 | tf_op jit(solution)/shard_map/ppermute | solution.py:404
  52.0 15.6 %collective-permute-start.16 = (bf16[2,64,512]{2,1,0:T(8,128)(2,1)S(1)}, bf16[2,64,512]{2,1,0:T(8,128)(2,1)S(1)}, u32[]{:S(2)}, u32[]{:S(2)}) collective-permute-start(bf16[2,64,512]{2,1,0:T(8,128)(2,1)S(1)} %get-tuple-element.50), channel_id=1, source_target_pairs={{0,24},{4,28},{8,16},{12,20},{16,8},{20,12},{24,0},{28,4},{1,25},{... | collective-permute-start | bytes 393224 | tf_op jit(solution)/shard_map/ppermute | solution.py:404
  55.7 12.0 %collective-permute-start.17 = (bf16[2,64,512]{2,1,0:T(8,128)(2,1)S(1)}, bf16[2,64,512]{2,1,0:T(8,128)(2,1)S(1)}, u32[]{:S(2)}, u32[]{:S(2)}) collective-permute-start(bf16[2,64,512]{2,1,0:T(8,128)(2,1)S(1)} %get-tuple-element.51), channel_id=1, source_target_pairs={{0,28},{4,24},{8,20},{12,16},{16,12},{20,8},{24,4},{28,0},{1,29},{... | collective-permute-start | bytes 393224 | tf_op jit(solution)/shard_map/ppermute | solution.py:404
  56.6 26.7 %collective-permute-start.19 = (bf16[512,512]{1,0:T(8,128)(2,1)S(1)}, bf16[512,512]{1,0:T(8,128)(2,1)S(1)}, u32[]{:S(2)}, u32[]{:S(2)}) collective-permute-start(bf16[512,512]{1,0:T(8,128)(2,1)S(1)} %shard_map.108.refs_0_), channel_id=1, source_target_pairs={{0,2},{1,3},{4,6},{5,7},{8,10},{9,11},{12,14},{13,15},{16,18},{17,... | collective-permute-start | bytes 1572872 | tf_op jit(solution)/shard_map/ppermute | solution.py:409
  68.5 17.8 %collective-permute-start.20 = (bf16[512,512]{1,0:T(8,128)(2,1)S(1)}, bf16[512,512]{1,0:T(8,128)(2,1)S(1)}, u32[]{:S(2)}, u32[]{:S(2)}) collective-permute-start(bf16[512,512]{1,0:T(8,128)(2,1)S(1)} %shard_map.111.refs_1_), channel_id=1, source_target_pairs={{0,2},{1,3},{4,6},{5,7},{8,10},{9,11},{12,14},{13,15},{16,18},{17,... | collective-permute-start | bytes 1572872 | tf_op jit(solution)/shard_map/ppermute | solution.py:409
  70.2 3.9 %collective-permute-start.18 = (f32[2,512]{1,0:T(2,128)S(1)}, f32[2,512]{1,0:T(2,128)S(1)}, u32[]{:S(2)}, u32[]{:S(2)}) collective-permute-start(f32[2,512]{1,0:T(2,128)S(1)} %shard_map.110.first_ref), channel_id=1, source_target_pairs={{0,4},{4,0},{8,12},{12,8},{16,20},{20,16},{24,28},{28,24},{1,5},{5... | collective-permute-start | bytes 12296 | tf_op jit(solution)/shard_map/ppermute | solution.py:404
  74.1 9.2 %collective-permute-start.21 = (f32[2,512]{1,0:T(2,128)S(1)}, f32[2,512]{1,0:T(2,128)S(1)}, u32[]{:S(2)}, u32[]{:S(2)}) collective-permute-start(f32[2,512]{1,0:T(2,128)S(1)} %shard_map.113.first_ref), channel_id=1, source_target_pairs={{0,8},{4,12},{8,0},{12,4},{16,24},{20,28},{24,16},{28,20},{1,9},{5... | collective-permute-start | bytes 12296 | tf_op jit(solution)/shard_map/ppermute | solution.py:404
  87.8 6.2 %collective-permute-start.22 = (bf16[1024,512]{1,0:T(8,128)(2,1)S(1)}, bf16[1024,512]{1,0:T(8,128)(2,1)S(1)}, u32[]{:S(2)}, u32[]{:S(2)}) collective-permute-start(bf16[1024,512]{1,0:T(8,128)(2,1)S(1)} %shard_map.118), channel_id=1, source_target_pairs={{0,1},{1,0},{2,3},{3,2},{4,5},{5,4},{6,7},{7,6},{8,9},{9,8},{10,11... | collective-permute-start | bytes 3145736 | tf_op jit(solution)/shard_map/ppermute | solution.py:404
  87.9 4.6 %collective-permute-start.23 = (f32[2,512]{1,0:T(2,128)S(1)}, f32[2,512]{1,0:T(2,128)S(1)}, u32[]{:S(2)}, u32[]{:S(2)}) collective-permute-start(f32[2,512]{1,0:T(2,128)S(1)} %shard_map.117.first_ref), channel_id=1, source_target_pairs={{0,16},{4,20},{8,24},{12,28},{16,0},{20,4},{24,8},{28,12},{1,17},{... | collective-permute-start | bytes 12296 | tf_op jit(solution)/shard_map/ppermute | solution.py:404
  92.4 1.5 %collective-permute-start.24 = (f32[2,512]{1,0:T(2,128)S(1)}, f32[2,512]{1,0:T(2,128)S(1)}, u32[]{:S(2)}, u32[]{:S(2)}) collective-permute-start(f32[2,512]{1,0:T(2,128)S(1)} %shard_map.119.own_density_ref), channel_id=1, source_target_pairs={{0,1},{1,0},{2,3},{3,2},{4,5},{5,4},{6,7},{7,6},{8,9},{9,8},{10,11... | collective-permute-start | bytes 12296 | tf_op jit(solution)/shard_map/ppermute | solution.py:404

commit v5 on v4

--- a/solution.py
+++ b/solution.py
@@ -496,6 +496,14 @@
         energies,
     )
 
+    def energy_step(density, distance):
+        return add(density, exchange(density, "energy", distance))
+
+    distances = [1 << bit for bit in range(energies.bit_length() - 1)]
+    early = 1
+    density = after(density, back[half])
+    for distance in distances[:early]:
+        density = energy_step(density, distance)
     back[half] = after(back[half], density)
     own_cross = right_rows(scalars, column, back[half:], half)
     far_near = [shift(own_near, "slab", behind) for behind in range(2, slabs, 2)]
@@ -506,20 +514,14 @@
     )
     near_terms = [(rows, *matrices) for rows, matrices in zip(far_near, far)]
     cross_terms = [(rows, *matrices) for rows, matrices in zip(far_cross, far)]
-    def energy_step(density, distance):
-        return add(density, exchange(density, "energy", distance))
-
     def far_sum(total, terms, group, target, dtype=F32):
         return far_terms(place_one, total, terms, group, target, dtype, energies) if terms else total
 
-    distances = [1 << bit for bit in range(energies.bit_length() - 1)]
-    density = energy_step(density, distances[0])
     for_partner = far_sum(for_partner, near_terms, near, 1)
-    for_self = far_sum(after(for_self, density), near_terms, near, 0)
-    density = energy_step(density, distances[1])
+    for_self = far_sum(for_self, near_terms, near, 0)
+    for distance in distances[early:]:
+        density = energy_step(density, distance)
     for_partner = far_sum(after(for_partner, density, for_self), cross_terms, cross, 1, BF16).astype(BF16)
-    for distance in distances[2:]:
-        density = energy_step(density, distance)
     from_partner = exchange(for_partner, "slab", 1)
     density_partner = exchange(density, "slab", 1)
     for_self = far_sum(for_self, cross_terms, cross, 0)

time: 95.4 us -> 92.8 us (0.973)
  waiting for transfers between devices: 18.9 us -> 17.5 us
  starting transfers between devices: 46.9 us -> 45.9 us
    ppermute x21, waiting for transfers between devices: 18.9 us -> 16.8 us  [exchange(): return lax.ppermute(x, axis, [(i, i ^ distance) for i in range(size)])]
    ppermute x21, starting transfers between devices: 37.7 us -> 36.6 us  [exchange(): return lax.ppermute(x, axis, [(i, i ^ distance) for i in range(size)])]
  transfers between devices with their start and end apart: 25 -> 25, of which waited for: 5 -> 7; matrix products, arithmetic and copies ran while one was open for 2% -> 2% of each run, Pallas kernels for 23% -> 24%
where the time goes in v5:
time: 92.8 us; the launch traced here: 92.6 us
  starting transfers between devices  45.9 us (49%)
  Pallas kernels  24.7 us (27%)
  waiting for transfers between devices  17.5 us (19%)
  between operations  2.94 us (3%)
  local copies, waits for them, and re-layouts  1.45 us (2%)
    ppermute x21, starting transfers between devices, exchange(): return lax.ppermute(x, axis, [(i, i ^ distance) for i in range(size)])  36.6 us
    ppermute x21, waiting for transfers between devices, exchange(): return lax.ppermute(x, axis, [(i, i ^ distance) for i in range(size)])  16.8 us
    ppermute x4, starting transfers between devices, shift(): return lax.ppermute(x, axis, [(i, i + by) for i in range(size - by)])  9.22 us
    pallas_call x4, Pallas kernels, far_terms(): call(functools.partial(far_terms_kernel, target=target, group=group, ener...  5.86 us
    pallas_call x1, Pallas kernels, far_matrices(): call(far_matrices_kernel, [pair, pair] + [matrix] * goes_on, [SMEM] + [VM...  5.25 us
    pallas_call x1, Pallas kernels, own_terms(): call(functools.partial(own_terms_kernel, groups=groups, energies=energies...  3.56 us
    pallas_call x1, Pallas kernels, own_matrices(): call(own_matrices_kernel, [matrix, matrix, matrix], [SMEM] + [VMEM] * 3,...  2.55 us
    pallas_call x1, Pallas kernels, diagonal_sums(): call(functools.partial(diagonal_kernel, rows=n // energies), jax.ShapeDty...  2.43 us
  transfers between devices with their start and end apart: 25, of which 7 were waited for; matrix products, arithmetic and copies ran while one was open for 2% of the time, Pallas kernels for 24%

profile of v5, /device:TPU:0, one launch (start us, length us, event | category | flops | bytes accessed | tf_op | source)
XLA Modules:
  0.0 92.6 jit_solution(11031406913581617203)
XLA Ops:
  0.6 0.5 collective-permute-start
  1.1 4.5 %collective-permute-start.9 = (bf16[1024,512]{1,0:T(8,128)(2,1)}, bf16[1024,512]{1,0:T(8,128)(2,1)S(1)}, u32[]{:S(2)}, u32[]{:S(2)}) collective-permute-start(bf16[1024,512]{1,0:T(8,128)(2,1)} %bitcast.37), channel_id=1, source_target_pairs={{0,2},{1,3},{4,6},{5,7},{8,10},{9,11},{12,14},{13,15},{16,18},{17,... | collective-permute-start | bytes 3145736 | tf_op jit(solution)/shard_map/ppermute | solution.py:409
  7.6 1.3 %fusion = (bf16[1,1,1,512,512]{4,3,2,1,0:T(8,128)(2,1)S(1)}, bf16[1,1,1,512,512]{4,3,2,1,0:T(8,128)(2,1)S(1)}) fusion(bf16[1,1,2,512,512]{4,3,2,1,0:T(8,128)(2,1)} %param.9), kind=kLoop, calls=%fused_computation.24 | loop fusion | bytes 2097152 | tf_op jit(solution)/shard_map/unstack | solution.py:455
  8.9 0.2 dynamic-slice_bitcast_fusion
  9.1 0.1 pad_maximum_fusion
  9.2 1.6 %collective-permute-start.2 = (bf16[136,512]{1,0:T(8,128)(2,1)S(1)}, bf16[136,512]{1,0:T(8,128)(2,1)S(1)}, u32[]{:S(2)}, u32[]{:S(2)}) collective-permute-start(bf16[136,512]{1,0:T(8,128)(2,1)S(1)} %get-tuple-element.78), channel_id=1, source_target_pairs={{0,8},{4,12},{8,0},{12,4},{16,24},{20,28},{24,16},{28,20},{1,9},{5... | collective-permute-start | bytes 417800 | tf_op jit(solution)/shard_map/ppermute | solution.py:404
  10.9 1.4 %collective-permute-start.3 = (bf16[136,512]{1,0:T(8,128)(2,1)S(1)}, bf16[136,512]{1,0:T(8,128)(2,1)S(1)}, u32[]{:S(2)}, u32[]{:S(2)}) collective-permute-start(bf16[136,512]{1,0:T(8,128)(2,1)S(1)} %get-tuple-element.79), channel_id=1, source_target_pairs={{0,12},{4,8},{8,4},{12,0},{16,28},{20,24},{24,20},{28,16},{1,13},{... | collective-permute-start | bytes 417800 | tf_op jit(solution)/shard_map/ppermute | solution.py:404
  12.3 2.6 %collective-permute-start.4 = (bf16[136,512]{1,0:T(8,128)(2,1)S(1)}, bf16[136,512]{1,0:T(8,128)(2,1)S(1)}, u32[]{:S(2)}, u32[]{:S(2)}) collective-permute-start(bf16[136,512]{1,0:T(8,128)(2,1)S(1)} %get-tuple-element.80), channel_id=1, source_target_pairs={{0,16},{4,20},{8,24},{12,28},{16,0},{20,4},{24,8},{28,12},{1,17},{... | collective-permute-start | bytes 417800 | tf_op jit(solution)/shard_map/ppermute | solution.py:404
  14.9 0.3 collective-permute-start.5
  15.2 4.7 %collective-permute-done.2.refs_2_ = bf16[136,512]{1,0:T(8,128)(2,1)S(1)} collective-permute-done((bf16[136,512]{1,0:T(8,128)(2,1)S(1)}, bf16[136,512]{1,0:T(8,128)(2,1)S(1)}, u32[]{:S(2)}, u32[]{:S(2)}) %collective-permute-start.2) | collective-permute-done | bytes 139296 | tf_op jit(solution)/shard_map/ppermute | solution.py:404
  20.0 3.9 %collective-permute-start.7 = (bf16[136,512]{1,0:T(8,128)(2,1)S(1)}, bf16[136,512]{1,0:T(8,128)(2,1)S(1)}, u32[]{:S(2)}, u32[]{:S(2)}) collective-permute-start(bf16[136,512]{1,0:T(8,128)(2,1)S(1)} %get-tuple-element.76), channel_id=1, source_target_pairs={{0,28},{4,24},{8,20},{12,16},{16,12},{20,8},{24,4},{28,0},{1,29},{... | collective-permute-start | bytes 417800 | tf_op jit(solution)/shard_map/ppermute | solution.py:404
  23.8 0.0 collective-permute-done.3.refs_3_
  23.9 2.2 %collective-permute-start.6 = (bf16[136,512]{1,0:T(8,128)(2,1)S(1)}, bf16[136,512]{1,0:T(8,128)(2,1)S(1)}, u32[]{:S(2)}, u32[]{:S(2)}) collective-permute-start(bf16[136,512]{1,0:T(8,128)(2,1)S(1)} %get-tuple-element.82), channel_id=1, source_target_pairs={{0,24},{4,28},{8,16},{12,20},{16,8},{20,12},{24,0},{28,4},{1,25},{... | collective-permute-start | bytes 417800 | tf_op jit(solution)/shard_map/ppermute | solution.py:404
  26.1 2.5 %shard_map.104 = (bf16[1024,512]{1,0:T(8,128)(2,1)S(1)}, bf16[1024,512]{1,0:T(8,128)(2,1)S(1)}, bf16[1024,512]{1,0:T(8,128)(2,1)S(1)}) custom-call(s32[1]{0:T(128)} %bitcast.1.slab_ref, bf16[1024,512]{1,0:T(8,128)(2,1)S(1)} %bitcast.38, bf16[1024,512]{1,0:T(8,128)(2,1)S(1)} %collective-permute-done.partner_ref, bf16[512,512]{1,0:T(8,128)(2,1)S(1)} %copy-done.1), custom_call_target="tpu_custom_call" | custom-call | flops 1024 | bytes 1024 | tf_op jit(solution)/shard_map/pallas_call | solution.py:222
  28.7 6.6 %collective-permute-done.5.refs_5_ = bf16[136,512]{1,0:T(8,128)(2,1)S(1)} collective-permute-done((bf16[136,512]{1,0:T(8,128)(2,1)S(1)}, bf16[136,512]{1,0:T(8,128)(2,1)S(1)}, u32[]{:S(2)}, u32[]{:S(2)}) %collective-permute-start.5) | collective-permute-done | bytes 139296 | tf_op jit(solution)/shard_map/ppermute | solution.py:404
  35.3 2.0 %shard_map.106 = (bf16[2,64,512]{2,1,0:T(8,128)(2,1)S(1)}, bf16[2,64,512]{2,1,0:T(8,128)(2,1)S(1)}, bf16[2,64,512]{2,1,0:T(8,128)(2,1)S(1)}, bf16[2,64,512]{2,1,...) custom-call(s32[1]{0:T(128)} %bitcast.place_ref, ...), custom_call_target="tpu_custom_call" | custom-call | flops 1024 | bytes 6601024 | tf_op jit(solution)/shard_map/pallas_call | solution.py:128
  37.4 0.1 collective-permute-start.10
  37.4 0.6 collective-permute-start.8
  38.0 4.9 %collective-permute-start.11 = (bf16[2,64,512]{2,1,0:T(8,128)(2,1)S(1)}, bf16[2,64,512]{2,1,0:T(8,128)(2,1)S(1)}, u32[]{:S(2)}, u32[]{:S(2)}) collective-permute-start(bf16[2,64,512]{2,1,0:T(8,128)(2,1)S(1)} %get-tuple-element.41), channel_id=1, source_target_pairs={{0,8},{4,12},{8,0},{12,4},{16,24},{20,28},{24,16},{28,20},{1,9},{5... | collective-permute-start | bytes 393224 | tf_op jit(solution)/shard_map/ppermute | solution.py:404
  42.9 0.8 collective-permute-start.12
  43.8 0.3 shard_map.107.rows_ref
  44.1 1.5 %collective-permute-start.14 = (bf16[128,512]{1,0:T(8,128)(2,1)S(1)}, bf16[128,512]{1,0:T(8,128)(2,1)S(1)}, u32[]{:S(2)}, u32[]{:S(2)}) collective-permute-start(bf16[128,512]{1,0:T(8,128)(2,1)S(1)} %shard_map.107.rows_ref), channel_id=1, source_target_pairs={{0,2},{1,3},{4,6},{5,7},{8,10},{9,11},{12,14},{13,15},{16,18},{17,... | collective-permute-start | bytes 393224 | tf_op jit(solution)/shard_map/ppermute | solution.py:409
  45.6 4.5 %collective-permute-start.13 = (bf16[2,64,512]{2,1,0:T(8,128)(2,1)S(1)}, bf16[2,64,512]{2,1,0:T(8,128)(2,1)S(1)}, u32[]{:S(2)}, u32[]{:S(2)}) collective-permute-start(bf16[2,64,512]{2,1,0:T(8,128)(2,1)S(1)} %get-tuple-element.43), channel_id=1, source_target_pairs={{0,16},{4,20},{8,24},{12,28},{16,0},{20,4},{24,8},{28,12},{1,17},{... | collective-permute-start | bytes 393224 | tf_op jit(solution)/shard_map/ppermute | solution.py:404
  50.1 2.0 %collective-permute-start.16 = (bf16[2,64,512]{2,1,0:T(8,128)(2,1)S(1)}, bf16[2,64,512]{2,1,0:T(8,128)(2,1)S(1)}, u32[]{:S(2)}, u32[]{:S(2)}) collective-permute-start(bf16[2,64,512]{2,1,0:T(8,128)(2,1)S(1)} %get-tuple-element.50), channel_id=1, source_target_pairs={{0,20},{4,16},{8,28},{12,24},{16,4},{20,0},{24,12},{28,8},{1,21},{... | collective-permute-start | bytes 393224 | tf_op jit(solution)/shard_map/ppermute | solution.py:404
  52.0 3.6 %collective-permute-start.17 = (bf16[2,64,512]{2,1,0:T(8,128)(2,1)S(1)}, bf16[2,64,512]{2,1,0:T(8,128)(2,1)S(1)}, u32[]{:S(2)}, u32[]{:S(2)}) collective-permute-start(bf16[2,64,512]{2,1,0:T(8,128)(2,1)S(1)} %get-tuple-element.51), channel_id=1, source_target_pairs={{0,24},{4,28},{8,16},{12,20},{16,8},{20,12},{24,0},{28,4},{1,25},{... | collective-permute-start | bytes 393224 | tf_op jit(solution)/shard_map/ppermute | solution.py:404
  55.7 0.1 collective-permute-start.18
  55.8 0.8 shard_map.108.refs_0_
  56.6 5.2 %shard_map.109 = (bf16[2,1024,512]{2,1,0:T(8,128)(2,1)S(1)}, bf16[2,1024,512]{2,1,0:T(8,128)(2,1)S(1)}) custom-call(s32[1]{0:T(128)} %bitcast.1.slab_ref, bf16[1024,512]{1,0:T(8,128)(2,1)S(1)} %get-tuple-element.45.chain_ref, bf16[1024,512]{1,0:T(8,128)(2,1)S(1)} %collective-permute-done.9.self_ref, ...), custom_call_target="tpu_custom_call" | custom-call | flops 1024 | bytes 17161024 | tf_op jit(solution)/shard_map/pallas_call | solution.py:265
  61.9 2.4 %shard_map.110.first_ref = f32[2,512]{1,0:T(2,128)S(1)} custom-call(s32[1]{0:T(128)} %bitcast.place_ref, bf16[1024,512]{1,0:T(8,128)(2,1)S(1)} %bitcast.41, bf16[1024,512]{1,0:T(8,128)(2,1)S(1)} %get-tuple-element.30.high_ref, bf16[1024,512]{1,0:T(8,128)(2,1)S(1)} %get-tuple-element.31.factor_ref, bf16[128,512]{1,0:T(8,128)(2,1)S(1)} %shard_map.107.rows_ref, ...), custom_call_target="tpu_custom_call" | custom-call | flops 1024 | bytes 7921024 | tf_op jit(solution)/shard_map/pallas_call | solution.py:369
  64.3 1.4 %collective-permute-done.13.refs_0_ = bf16[2,64,512]{2,1,0:T(8,128)(2,1)S(1)} collective-permute-done((bf16[2,64,512]{2,1,0:T(8,128)(2,1)S(1)}, bf16[2,64,512]{2,1,0:T(8,128)(2,1)S(1)}, u32[]{:S(2)}, u32[]{:S(2)}) %collective-permute-start.13) | collective-permute-done | bytes 131104 | tf_op jit(solution)/shard_map/ppermute | solution.py:404
  65.7 0.3 collective-permute-start.15
  65.9 1.5 %collective-permute-start.19 = (bf16[512,512]{1,0:T(8,128)(2,1)S(1)}, bf16[512,512]{1,0:T(8,128)(2,1)S(1)}, u32[]{:S(2)}, u32[]{:S(2)}) collective-permute-start(bf16[512,512]{1,0:T(8,128)(2,1)S(1)} %shard_map.108.refs_0_), channel_id=1, source_target_pairs={{0,2},{1,3},{4,6},{5,7},{8,10},{9,11},{12,14},{13,15},{16,18},{17,... | collective-permute-start | bytes 1572872 | tf_op jit(solution)/shard_map/ppermute | solution.py:409
  67.4 1.8 %collective-permute-done.15.second_ref = f32[2,512]{1,0:T(2,128)S(1)} collective-permute-done((f32[2,512]{1,0:T(2,128)S(1)}, f32[2,512]{1,0:T(2,128)S(1)}, u32[]{:S(2)}, u32[]{:S(2)}) %collective-permute-start.15) | collective-permute-done | bytes 4128 | tf_op jit(solution)/shard_map/ppermute | solution.py:404
  69.3 0.8 shard_map.112.refs_1_
  70.1 1.7 %collective-permute-start.20 = (bf16[512,512]{1,0:T(8,128)(2,1)S(1)}, bf16[512,512]{1,0:T(8,128)(2,1)S(1)}, u32[]{:S(2)}, u32[]{:S(2)}) collective-permute-start(bf16[512,512]{1,0:T(8,128)(2,1)S(1)} %shard_map.112.refs_1_), channel_id=1, source_target_pairs={{0,2},{1,3},{4,6},{5,7},{8,10},{9,11},{12,14},{13,15},{16,18},{17,... | collective-permute-start | bytes 1572872 | tf_op jit(solution)/shard_map/ppermute | solution.py:409
  71.8 4.3 %collective-permute-start.21 = (f32[2,512]{1,0:T(2,128)S(1)}, f32[2,512]{1,0:T(2,128)S(1)}, u32[]{:S(2)}, u32[]{:S(2)}) collective-permute-start(f32[2,512]{1,0:T(2,128)S(1)} %shard_map.111.first_ref), channel_id=1, source_target_pairs={{0,8},{4,12},{8,0},{12,4},{16,24},{20,28},{24,16},{28,20},{1,9},{5... | collective-permute-start | bytes 12296 | tf_op jit(solution)/shard_map/ppermute | solution.py:404
  76.2 1.6 %collective-permute-done.21.second_ref = f32[2,512]{1,0:T(2,128)S(1)} collective-permute-done((f32[2,512]{1,0:T(2,128)S(1)}, f32[2,512]{1,0:T(2,128)S(1)}, u32[]{:S(2)}, u32[]{:S(2)}) %collective-permute-start.21) | collective-permute-done | bytes 4128 | tf_op jit(solution)/shard_map/ppermute | solution.py:404
  77.7 2.3 %collective-permute-start.22 = (f32[2,512]{1,0:T(2,128)S(1)}, f32[2,512]{1,0:T(2,128)S(1)}, u32[]{:S(2)}, u32[]{:S(2)}) collective-permute-start(f32[2,512]{1,0:T(2,128)S(1)} %shard_map.117.first_ref), channel_id=1, source_target_pairs={{0,16},{4,20},{8,24},{12,28},{16,0},{20,4},{24,8},{28,12},{1,17},{... | collective-permute-start | bytes 12296 | tf_op jit(solution)/shard_map/ppermute | solution.py:404
  80.0 3.6 %shard_map.113 = (f32[1024,512]{1,0:T(8,128)S(1)}, f32[1024,512]{1,0:T(8,128)S(1)}) custom-call(s32[1]{0:T(128)} %bitcast.place_ref, bf16[1024,512]{1,0:T(8,128)(2,1)S(1)} %get-tuple-element.30.high_ref, bf16[1024,512]{1,0:T(8,128)(2,1)S(1)} %bitcast.43, bf16[1024,512]{1,0:T(8,128)(2,1)S(1)} %get-tuple-element.31.factor_ref, ...), custom_call_target="tpu_custom_call" | custom-call | flops 1024 | bytes 11881024 | tf_op jit(solution)/shard_map/pallas_call | solution.py:305
  83.6 1.5 %shard_map.116.total_ref = f32[1024,512]{1,0:T(8,128)S(1)} custom-call(s32[1]{0:T(128)} %bitcast.place_ref, f32[1024,512]{1,0:T(8,128)S(1)} %get-tuple-element.54.total_ref, bf16[512,512]{1,0:T(8,128)(2,1)S(1)} %collective-permute-done.19.refs_0_, bf16[2,1024,512]{2,1,0:T(8,128)(2,1)S(1)} %get-tuple-element.46.refs_1_, ...), custom_call_target="tpu_custom_call" | custom-call | flops 1024 | bytes 5941024 | tf_op jit(solution)/shard_map/pallas_call | solution.py:331
  85.1 1.5 %shard_map.114.total_ref = f32[1024,512]{1,0:T(8,128)S(1)} custom-call(s32[1]{0:T(128)} %bitcast.place_ref, f32[1024,512]{1,0:T(8,128)S(1)} %get-tuple-element.53.total_ref, bf16[512,512]{1,0:T(8,128)(2,1)S(1)} %collective-permute-done.19.refs_0_, bf16[2,1024,512]{2,1,0:T(8,128)(2,1)S(1)} %get-tuple-element.46.refs_1_, ...), custom_call_target="tpu_custom_call" | custom-call | flops 1024 | bytes 5941024 | tf_op jit(solution)/shard_map/pallas_call | solution.py:331
  86.6 0.7 collective-permute-done.20.refs_0_
  87.2 1.5 %shard_map.119 = bf16[1024,512]{1,0:T(8,128)(2,1)S(1)} custom-call(s32[1]{0:T(128)} %bitcast.place_ref, f32[1024,512]{1,0:T(8,128)S(1)} %shard_map.116.total_ref, bf16[512,512]{1,0:T(8,128)(2,1)S(1)} %collective-permute-done.20.refs_0_, bf16[2,1024,512]{2,1,0:T(8,128)(2,1)S(1)} %get-tuple-element.46.refs_1_, bf16[2,1024,512]{2,1,0:T(8,128)(2,1)S(1)} %get-tuple-element.47.refs_2_), custom_call_target="tpu_custom_call" | custom-call | flops 1024 | bytes 5941024 | tf_op jit(solution)/shard_map/pallas_call | solution.py:331
  88.7 0.1 collective-permute-start.23
  88.8 0.5 collective-permute-start.24
  89.3 1.5 %shard_map.115.own_ref = f32[1024,512]{1,0:T(8,128)S(1)} custom-call(s32[1]{0:T(128)} %bitcast.place_ref, f32[1024,512]{1,0:T(8,128)S(1)} %shard_map.114.total_ref, bf16[512,512]{1,0:T(8,128)(2,1)S(1)} %collective-permute-done.20.refs_0_, bf16[2,1024,512]{2,1,0:T(8,128)(2,1)S(1)} %get-tuple-element.46.refs_1_, ...), custom_call_target="tpu_custom_call" | custom-call | flops 1024 | bytes 5941024 | tf_op jit(solution)/shard_map/pallas_call | solution.py:331
  90.8 0.7 collective-permute-done.24.partner_density_ref
  91.4 1.1 %shard_map.120 = (bf16[1024,512]{1,0:T(8,128)(2,1)}, f32[1,512]{1,0:T(1,128)}) custom-call(f32[1024,512]{1,0:T(8,128)S(1)} %shard_map.115.own_ref, bf16[1024,512]{1,0:T(8,128)(2,1)S(1)} %collective-permute-done.23.partner_ref, f32[2,512]{1,0:T(2,128)S(1)} %shard_map.118.own_density_ref, f32[2,512]{1,0:T(2,128)S(1)} %collective-permute-done.24.partner_density_ref), custom_call_target="tpu_custom_call" | custom-call | flops 1024 | bytes 3961024 | tf_op jit(solution)/shard_map/pallas_call | solution.py:394
  (33 shorter events, 0.1 us)
Async XLA Ops:
  0.6 14.2 %collective-permute-start = (bf16[1024,512]{1,0:T(8,128)(2,1)}, bf16[1024,512]{1,0:T(8,128)(2,1)S(1)}, u32[]{:S(2)}, u32[]{:S(2)}) collective-permute-start(bf16[1024,512]{1,0:T(8,128)(2,1)} %bitcast.36), channel_id=1, source_target_pairs={{0,1},{1,0},{2,3},{3,2},{4,5},{5,4},{6,7},{7,6},{8,9},{9,8},{10,11... | collective-permute-start | bytes 3145736 | tf_op jit(solution)/shard_map/ppermute | solution.py:404
  1.1 36.2 %collective-permute-start.9 = (bf16[1024,512]{1,0:T(8,128)(2,1)}, bf16[1024,512]{1,0:T(8,128)(2,1)S(1)}, u32[]{:S(2)}, u32[]{:S(2)}) collective-permute-start(bf16[1024,512]{1,0:T(8,128)(2,1)} %bitcast.37), channel_id=1, source_target_pairs={{0,2},{1,3},{4,6},{5,7},{8,10},{9,11},{12,14},{13,15},{16,18},{17,... | collective-permute-start | bytes 3145736 | tf_op jit(solution)/shard_map/ppermute | solution.py:409
  8.9 17.2 %copy-start = (bf16[1,2,512,512]{3,2,1,0:T(8,128)(2,1)S(1)}, bf16[1,2,512,512]{3,2,1,0:T(8,128)(2,1)}, u32[]{:S(2)}) copy-start(bf16[1,2,512,512]{3,2,1,0:T(8,128)(2,1)} %param.10) | copy-start | bytes 3145732
  8.9 17.2 %copy-start.1 = (bf16[512,512]{1,0:T(8,128)(2,1)S(1)}, bf16[512,512]{1,0:T(8,128)(2,1)}, u32[]{:S(2)}) copy-start(bf16[512,512]{1,0:T(8,128)(2,1)} %coupling_ref.3) | copy-start | bytes 1572868
  9.1 26.2 %copy-start.2 = (bf16[4,64,512]{2,1,0:T(8,128)(2,1)S(1)}, bf16[4,64,512]{2,1,0:T(8,128)(2,1)}, u32[]{:S(2)}) copy-start(bf16[4,64,512]{2,1,0:T(8,128)(2,1)} %phonon_ref.1) | copy-start | bytes 786436
  9.1 26.2 %copy-start.3 = (s32[8,6]{1,0:T(8,128)S(1)}, s32[8,6]{1,0:T(8,128)}, u32[]{:S(2)}) copy-start(s32[8,6]{1,0:T(8,128)} %source_ref.1) | copy-start | bytes 580
  9.1 26.2 %copy-start.4 = (s32[8,6]{1,0:T(8,128)S(1)}, s32[8,6]{1,0:T(8,128)}, u32[]{:S(2)}) copy-start(s32[8,6]{1,0:T(8,128)} %mode_ref.1) | copy-start | bytes 580
  9.2 10.8 %collective-permute-start.2 = (bf16[136,512]{1,0:T(8,128)(2,1)S(1)}, bf16[136,512]{1,0:T(8,128)(2,1)S(1)}, u32[]{:S(2)}, u32[]{:S(2)}) collective-permute-start(bf16[136,512]{1,0:T(8,128)(2,1)S(1)} %get-tuple-element.78), channel_id=1, source_target_pairs={{0,8},{4,12},{8,0},{12,4},{16,24},{20,28},{24,16},{28,20},{1,9},{5... | collective-permute-start | bytes 417800 | tf_op jit(solution)/shard_map/ppermute | solution.py:404
  10.9 13.0 %collective-permute-start.3 = (bf16[136,512]{1,0:T(8,128)(2,1)S(1)}, bf16[136,512]{1,0:T(8,128)(2,1)S(1)}, u32[]{:S(2)}, u32[]{:S(2)}) collective-permute-start(bf16[136,512]{1,0:T(8,128)(2,1)S(1)} %get-tuple-element.79), channel_id=1, source_target_pairs={{0,12},{4,8},{8,4},{12,0},{16,28},{20,24},{24,20},{28,16},{1,13},{... | collective-permute-start | bytes 417800 | tf_op jit(solution)/shard_map/ppermute | solution.py:404
  12.3 13.8 %collective-permute-start.4 = (bf16[136,512]{1,0:T(8,128)(2,1)S(1)}, bf16[136,512]{1,0:T(8,128)(2,1)S(1)}, u32[]{:S(2)}, u32[]{:S(2)}) collective-permute-start(bf16[136,512]{1,0:T(8,128)(2,1)S(1)} %get-tuple-element.80), channel_id=1, source_target_pairs={{0,16},{4,20},{8,24},{12,28},{16,0},{20,4},{24,8},{28,12},{1,17},{... | collective-permute-start | bytes 417800 | tf_op jit(solution)/shard_map/ppermute | solution.py:404
  14.9 20.4 %collective-permute-start.5 = (bf16[136,512]{1,0:T(8,128)(2,1)S(1)}, bf16[136,512]{1,0:T(8,128)(2,1)S(1)}, u32[]{:S(2)}, u32[]{:S(2)}) collective-permute-start(bf16[136,512]{1,0:T(8,128)(2,1)S(1)} %get-tuple-element.81), channel_id=1, source_target_pairs={{0,20},{4,16},{8,28},{12,24},{16,4},{20,0},{24,12},{28,8},{1,21},{... | collective-permute-start | bytes 417800 | tf_op jit(solution)/shard_map/ppermute | solution.py:404
  20.0 15.3 %collective-permute-start.7 = (bf16[136,512]{1,0:T(8,128)(2,1)S(1)}, bf16[136,512]{1,0:T(8,128)(2,1)S(1)}, u32[]{:S(2)}, u32[]{:S(2)}) collective-permute-start(bf16[136,512]{1,0:T(8,128)(2,1)S(1)} %get-tuple-element.76), channel_id=1, source_target_pairs={{0,28},{4,24},{8,20},{12,16},{16,12},{20,8},{24,4},{28,0},{1,29},{... | collective-permute-start | bytes 417800 | tf_op jit(solution)/shard_map/ppermute | solution.py:404
  23.9 11.4 %collective-permute-start.6 = (bf16[136,512]{1,0:T(8,128)(2,1)S(1)}, bf16[136,512]{1,0:T(8,128)(2,1)S(1)}, u32[]{:S(2)}, u32[]{:S(2)}) collective-permute-start(bf16[136,512]{1,0:T(8,128)(2,1)S(1)} %get-tuple-element.82), channel_id=1, source_target_pairs={{0,24},{4,28},{8,16},{12,20},{16,8},{20,12},{24,0},{28,4},{1,25},{... | collective-permute-start | bytes 417800 | tf_op jit(solution)/shard_map/ppermute | solution.py:404
  26.1 9.2 %collective-permute-start.1 = (bf16[136,512]{1,0:T(8,128)(2,1)S(1)}, bf16[136,512]{1,0:T(8,128)(2,1)S(1)}, u32[]{:S(2)}, u32[]{:S(2)}) collective-permute-start(bf16[136,512]{1,0:T(8,128)(2,1)S(1)} %get-tuple-element.33), channel_id=1, source_target_pairs={{0,4},{4,0},{8,12},{12,8},{16,20},{20,16},{24,28},{28,24},{1,5},{5... | collective-permute-start | bytes 417800 | tf_op jit(solution)/shard_map/ppermute | solution.py:404
  37.4 18.3 %collective-permute-start.10 = (bf16[1024,512]{1,0:T(8,128)(2,1)S(1)}, bf16[1024,512]{1,0:T(8,128)(2,1)S(1)}, u32[]{:S(2)}, u32[]{:S(2)}) collective-permute-start(bf16[1024,512]{1,0:T(8,128)(2,1)S(1)} %collective-permute-done.9.self_ref), channel_id=1, source_target_pairs={{0,1},{1,0},{2,3},{3,2},{4,5},{5,4},{6,7},{7,6},{8,9},{9,8},{10,11... | collective-permute-start | bytes 3145736 | tf_op jit(solution)/shard_map/ppermute | solution.py:404
  37.4 8.2 %collective-permute-start.8 = (bf16[2,64,512]{2,1,0:T(8,128)(2,1)S(1)}, bf16[2,64,512]{2,1,0:T(8,128)(2,1)S(1)}, u32[]{:S(2)}, u32[]{:S(2)}) collective-permute-start(bf16[2,64,512]{2,1,0:T(8,128)(2,1)S(1)} %get-tuple-element.38), channel_id=1, source_target_pairs={{0,4},{4,0},{8,12},{12,8},{16,20},{20,16},{24,28},{28,24},{1,5},{5... | collective-permute-start | bytes 393224 | tf_op jit(solution)/shard_map/ppermute | solution.py:404
  38.0 12.0 %collective-permute-start.11 = (bf16[2,64,512]{2,1,0:T(8,128)(2,1)S(1)}, bf16[2,64,512]{2,1,0:T(8,128)(2,1)S(1)}, u32[]{:S(2)}, u32[]{:S(2)}) collective-permute-start(bf16[2,64,512]{2,1,0:T(8,128)(2,1)S(1)} %get-tuple-element.41), channel_id=1, source_target_pairs={{0,8},{4,12},{8,0},{12,4},{16,24},{20,28},{24,16},{28,20},{1,9},{5... | collective-permute-start | bytes 393224 | tf_op jit(solution)/shard_map/ppermute | solution.py:404
  42.9 9.1 %collective-permute-start.12 = (bf16[2,64,512]{2,1,0:T(8,128)(2,1)S(1)}, bf16[2,64,512]{2,1,0:T(8,128)(2,1)S(1)}, u32[]{:S(2)}, u32[]{:S(2)}) collective-permute-start(bf16[2,64,512]{2,1,0:T(8,128)(2,1)S(1)} %get-tuple-element.42), channel_id=1, source_target_pairs={{0,12},{4,8},{8,4},{12,0},{16,28},{20,24},{24,20},{28,16},{1,13},{... | collective-permute-start | bytes 393224 | tf_op jit(solution)/shard_map/ppermute | solution.py:404
  44.1 12.5 %collective-permute-start.14 = (bf16[128,512]{1,0:T(8,128)(2,1)S(1)}, bf16[128,512]{1,0:T(8,128)(2,1)S(1)}, u32[]{:S(2)}, u32[]{:S(2)}) collective-permute-start(bf16[128,512]{1,0:T(8,128)(2,1)S(1)} %shard_map.107.rows_ref), channel_id=1, source_target_pairs={{0,2},{1,3},{4,6},{5,7},{8,10},{9,11},{12,14},{13,15},{16,18},{17,... | collective-permute-start | bytes 393224 | tf_op jit(solution)/shard_map/ppermute | solution.py:409
  45.6 20.0 %collective-permute-start.13 = (bf16[2,64,512]{2,1,0:T(8,128)(2,1)S(1)}, bf16[2,64,512]{2,1,0:T(8,128)(2,1)S(1)}, u32[]{:S(2)}, u32[]{:S(2)}) collective-permute-start(bf16[2,64,512]{2,1,0:T(8,128)(2,1)S(1)} %get-tuple-element.43), channel_id=1, source_target_pairs={{0,16},{4,20},{8,24},{12,28},{16,0},{20,4},{24,8},{28,12},{1,17},{... | collective-permute-start | bytes 393224 | tf_op jit(solution)/shard_map/ppermute | solution.py:404
  50.1 19.2 %collective-permute-start.16 = (bf16[2,64,512]{2,1,0:T(8,128)(2,1)S(1)}, bf16[2,64,512]{2,1,0:T(8,128)(2,1)S(1)}, u32[]{:S(2)}, u32[]{:S(2)}) collective-permute-start(bf16[2,64,512]{2,1,0:T(8,128)(2,1)S(1)} %get-tuple-element.50), channel_id=1, source_target_pairs={{0,20},{4,16},{8,28},{12,24},{16,4},{20,0},{24,12},{28,8},{1,21},{... | collective-permute-start | bytes 393224 | tf_op jit(solution)/shard_map/ppermute | solution.py:404
  52.0 17.2 %collective-permute-start.17 = (bf16[2,64,512]{2,1,0:T(8,128)(2,1)S(1)}, bf16[2,64,512]{2,1,0:T(8,128)(2,1)S(1)}, u32[]{:S(2)}, u32[]{:S(2)}) collective-permute-start(bf16[2,64,512]{2,1,0:T(8,128)(2,1)S(1)} %get-tuple-element.51), channel_id=1, source_target_pairs={{0,24},{4,28},{8,16},{12,20},{16,8},{20,12},{24,0},{28,4},{1,25},{... | collective-permute-start | bytes 393224 | tf_op jit(solution)/shard_map/ppermute | solution.py:404
  55.7 13.6 %collective-permute-start.18 = (bf16[2,64,512]{2,1,0:T(8,128)(2,1)S(1)}, bf16[2,64,512]{2,1,0:T(8,128)(2,1)S(1)}, u32[]{:S(2)}, u32[]{:S(2)}) collective-permute-start(bf16[2,64,512]{2,1,0:T(8,128)(2,1)S(1)} %get-tuple-element.52), channel_id=1, source_target_pairs={{0,28},{4,24},{8,20},{12,16},{16,12},{20,8},{24,4},{28,0},{1,29},{... | collective-permute-start | bytes 393224 | tf_op jit(solution)/shard_map/ppermute | solution.py:404
  65.7 3.6 %collective-permute-start.15 = (f32[2,512]{1,0:T(2,128)S(1)}, f32[2,512]{1,0:T(2,128)S(1)}, u32[]{:S(2)}, u32[]{:S(2)}) collective-permute-start(f32[2,512]{1,0:T(2,128)S(1)} %shard_map.110.first_ref), channel_id=1, source_target_pairs={{0,4},{4,0},{8,12},{12,8},{16,20},{20,16},{24,28},{28,24},{1,5},{5... | collective-permute-start | bytes 12296 | tf_op jit(solution)/shard_map/ppermute | solution.py:404
  65.9 17.7 %collective-permute-start.19 = (bf16[512,512]{1,0:T(8,128)(2,1)S(1)}, bf16[512,512]{1,0:T(8,128)(2,1)S(1)}, u32[]{:S(2)}, u32[]{:S(2)}) collective-permute-start(bf16[512,512]{1,0:T(8,128)(2,1)S(1)} %shard_map.108.refs_0_), channel_id=1, source_target_pairs={{0,2},{1,3},{4,6},{5,7},{8,10},{9,11},{12,14},{13,15},{16,18},{17,... | collective-permute-start | bytes 1572872 | tf_op jit(solution)/shard_map/ppermute | solution.py:409
  70.1 17.1 %collective-permute-start.20 = (bf16[512,512]{1,0:T(8,128)(2,1)S(1)}, bf16[512,512]{1,0:T(8,128)(2,1)S(1)}, u32[]{:S(2)}, u32[]{:S(2)}) collective-permute-start(bf16[512,512]{1,0:T(8,128)(2,1)S(1)} %shard_map.112.refs_1_), channel_id=1, source_target_pairs={{0,2},{1,3},{4,6},{5,7},{8,10},{9,11},{12,14},{13,15},{16,18},{17,... | collective-permute-start | bytes 1572872 | tf_op jit(solution)/shard_map/ppermute | solution.py:409
  71.8 5.9 %collective-permute-start.21 = (f32[2,512]{1,0:T(2,128)S(1)}, f32[2,512]{1,0:T(2,128)S(1)}, u32[]{:S(2)}, u32[]{:S(2)}) collective-permute-start(f32[2,512]{1,0:T(2,128)S(1)} %shard_map.111.first_ref), channel_id=1, source_target_pairs={{0,8},{4,12},{8,0},{12,4},{16,24},{20,28},{24,16},{28,20},{1,9},{5... | collective-permute-start | bytes 12296 | tf_op jit(solution)/shard_map/ppermute | solution.py:404
  77.7 5.9 %collective-permute-start.22 = (f32[2,512]{1,0:T(2,128)S(1)}, f32[2,512]{1,0:T(2,128)S(1)}, u32[]{:S(2)}, u32[]{:S(2)}) collective-permute-start(f32[2,512]{1,0:T(2,128)S(1)} %shard_map.117.first_ref), channel_id=1, source_target_pairs={{0,16},{4,20},{8,24},{12,28},{16,0},{20,4},{24,8},{28,12},{1,17},{... | collective-permute-start | bytes 12296 | tf_op jit(solution)/shard_map/ppermute | solution.py:404
  88.7 2.7 %collective-permute-start.23 = (bf16[1024,512]{1,0:T(8,128)(2,1)S(1)}, bf16[1024,512]{1,0:T(8,128)(2,1)S(1)}, u32[]{:S(2)}, u32[]{:S(2)}) collective-permute-start(bf16[1024,512]{1,0:T(8,128)(2,1)S(1)} %shard_map.119), channel_id=1, source_target_pairs={{0,1},{1,0},{2,3},{3,2},{4,5},{5,4},{6,7},{7,6},{8,9},{9,8},{10,11... | collective-permute-start | bytes 3145736 | tf_op jit(solution)/shard_map/ppermute | solution.py:404
  88.8 2.7 %collective-permute-start.24 = (f32[2,512]{1,0:T(2,128)S(1)}, f32[2,512]{1,0:T(2,128)S(1)}, u32[]{:S(2)}, u32[]{:S(2)}) collective-permute-start(f32[2,512]{1,0:T(2,128)S(1)} %shard_map.118.own_density_ref), channel_id=1, source_target_pairs={{0,1},{1,0},{2,3},{3,2},{4,5},{5,4},{6,7},{7,6},{8,9},{9,8},{10,11... | collective-permute-start | bytes 12296 | tf_op jit(solution)/shard_map/ppermute | solution.py:404

commit v6 on v5

--- a/solution.py
+++ b/solution.py
@@ -521,9 +521,9 @@
     for_self = far_sum(for_self, near_terms, near, 0)
     for distance in distances[early:]:
         density = energy_step(density, distance)
-    for_partner = far_sum(after(for_partner, density, for_self), cross_terms, cross, 1, BF16).astype(BF16)
+    density_partner = exchange(after(density, for_self), "slab", 1)
+    for_partner = far_sum(after(for_partner, density_partner, for_self), cross_terms, cross, 1, BF16).astype(BF16)
     from_partner = exchange(for_partner, "slab", 1)
-    density_partner = exchange(density, "slab", 1)
     for_self = far_sum(for_self, cross_terms, cross, 0)
     current, density = finish(for_self, from_partner, density, density_partner)
     return (current.reshape(1, 1, 2, n, n), density)

time: 92.8 us -> 92.4 us (level)
  waiting for transfers between devices: 17.5 us -> 15.9 us
  starting transfers between devices: 45.9 us -> 47 us
    ppermute x21, starting transfers between devices: 36.6 us -> 38 us  [exchange(): return lax.ppermute(x, axis, [(i, i ^ distance) for i in range(size)])]
    ppermute x21, waiting for transfers between devices: 16.8 us -> 15.9 us  [exchange(): return lax.ppermute(x, axis, [(i, i ^ distance) for i in range(size)])]
  transfers between devices with their start and end apart: 25 -> 25, of which waited for: 7 -> 5; matrix products, arithmetic and copies ran while one was open for 2% -> 2% of each run, Pallas kernels for 24% -> 24%
where the time goes in v6:
time: 92.4 us; the launch traced here: 92.1 us
  starting transfers between devices  47 us (51%)
  Pallas kernels  24.7 us (27%)
  waiting for transfers between devices  15.9 us (17%)
  between operations  2.96 us (3%)
  local copies, waits for them, and re-layouts  1.47 us (2%)
    ppermute x21, starting transfers between devices, exchange(): return lax.ppermute(x, axis, [(i, i ^ distance) for i in range(size)])  38 us
    ppermute x21, waiting for transfers between devices, exchange(): return lax.ppermute(x, axis, [(i, i ^ distance) for i in range(size)])  15.9 us
    ppermute x4, starting transfers between devices, shift(): return lax.ppermute(x, axis, [(i, i + by) for i in range(size - by)])  9.03 us
    pallas_call x4, Pallas kernels, far_terms(): call(functools.partial(far_terms_kernel, target=target, group=group, ener...  5.86 us
    pallas_call x1, Pallas kernels, far_matrices(): call(far_matrices_kernel, [pair, pair] + [matrix] * goes_on, [SMEM] + [VM...  5.26 us
    pallas_call x1, Pallas kernels, own_terms(): call(functools.partial(own_terms_kernel, groups=groups, energies=energies...  3.56 us
    pallas_call x1, Pallas kernels, own_matrices(): call(own_matrices_kernel, [matrix, matrix, matrix], [SMEM] + [VMEM] * 3,...  2.55 us
    pallas_call x1, Pallas kernels, diagonal_sums(): call(functools.partial(diagonal_kernel, rows=n // energies), jax.ShapeDty...  2.43 us
  transfers between devices with their start and end apart: 25, of which 5 were waited for; matrix products, arithmetic and copies ran while one was open for 2% of the time, Pallas kernels for 24%

profile of v6, /device:TPU:0, one launch (start us, length us, event | category | flops | bytes accessed | tf_op | source)
XLA Modules:
  0.0 92.1 jit_solution(1520625335195770166)
XLA Ops:
  0.6 0.5 collective-permute-start
  1.1 4.5 %collective-permute-start.9 = (bf16[1024,512]{1,0:T(8,128)(2,1)}, bf16[1024,512]{1,0:T(8,128)(2,1)S(1)}, u32[]{:S(2)}, u32[]{:S(2)}) collective-permute-start(bf16[1024,512]{1,0:T(8,128)(2,1)} %bitcast.37), channel_id=1, source_target_pairs={{0,2},{1,3},{4,6},{5,7},{8,10},{9,11},{12,14},{13,15},{16,18},{17,... | collective-permute-start | bytes 3145736 | tf_op jit(solution)/shard_map/ppermute | solution.py:409
  7.6 1.3 %fusion = (bf16[1,1,1,512,512]{4,3,2,1,0:T(8,128)(2,1)S(1)}, bf16[1,1,1,512,512]{4,3,2,1,0:T(8,128)(2,1)S(1)}) fusion(bf16[1,1,2,512,512]{4,3,2,1,0:T(8,128)(2,1)} %param.9), kind=kLoop, calls=%fused_computation.24 | loop fusion | bytes 2097152 | tf_op jit(solution)/shard_map/unstack | solution.py:455
  8.9 0.0 copy-start
  8.9 0.0 copy-start.1
  8.9 0.2 dynamic-slice_bitcast_fusion
  9.1 0.1 pad_maximum_fusion
  9.2 1.6 %collective-permute-start.2 = (bf16[136,512]{1,0:T(8,128)(2,1)S(1)}, bf16[136,512]{1,0:T(8,128)(2,1)S(1)}, u32[]{:S(2)}, u32[]{:S(2)}) collective-permute-start(bf16[136,512]{1,0:T(8,128)(2,1)S(1)} %get-tuple-element.80), channel_id=1, source_target_pairs={{0,8},{4,12},{8,0},{12,4},{16,24},{20,28},{24,16},{28,20},{1,9},{5... | collective-permute-start | bytes 417800 | tf_op jit(solution)/shard_map/ppermute | solution.py:404
  10.9 1.4 %collective-permute-start.3 = (bf16[136,512]{1,0:T(8,128)(2,1)S(1)}, bf16[136,512]{1,0:T(8,128)(2,1)S(1)}, u32[]{:S(2)}, u32[]{:S(2)}) collective-permute-start(bf16[136,512]{1,0:T(8,128)(2,1)S(1)} %get-tuple-element.81), channel_id=1, source_target_pairs={{0,12},{4,8},{8,4},{12,0},{16,28},{20,24},{24,20},{28,16},{1,13},{... | collective-permute-start | bytes 417800 | tf_op jit(solution)/shard_map/ppermute | solution.py:404
  12.3 2.6 %collective-permute-start.4 = (bf16[136,512]{1,0:T(8,128)(2,1)S(1)}, bf16[136,512]{1,0:T(8,128)(2,1)S(1)}, u32[]{:S(2)}, u32[]{:S(2)}) collective-permute-start(bf16[136,512]{1,0:T(8,128)(2,1)S(1)} %get-tuple-element.82), channel_id=1, source_target_pairs={{0,16},{4,20},{8,24},{12,28},{16,0},{20,4},{24,8},{28,12},{1,17},{... | collective-permute-start | bytes 417800 | tf_op jit(solution)/shard_map/ppermute | solution.py:404
  14.9 0.3 collective-permute-start.5
  15.2 4.7 %collective-permute-done.2.refs_2_ = bf16[136,512]{1,0:T(8,128)(2,1)S(1)} collective-permute-done((bf16[136,512]{1,0:T(8,128)(2,1)S(1)}, bf16[136,512]{1,0:T(8,128)(2,1)S(1)}, u32[]{:S(2)}, u32[]{:S(2)}) %collective-permute-start.2) | collective-permute-done | bytes 139296 | tf_op jit(solution)/shard_map/ppermute | solution.py:404
  20.0 3.9 %collective-permute-start.7 = (bf16[136,512]{1,0:T(8,128)(2,1)S(1)}, bf16[136,512]{1,0:T(8,128)(2,1)S(1)}, u32[]{:S(2)}, u32[]{:S(2)}) collective-permute-start(bf16[136,512]{1,0:T(8,128)(2,1)S(1)} %get-tuple-element.78), channel_id=1, source_target_pairs={{0,28},{4,24},{8,20},{12,16},{16,12},{20,8},{24,4},{28,0},{1,29},{... | collective-permute-start | bytes 417800 | tf_op jit(solution)/shard_map/ppermute | solution.py:404
  23.8 0.0 collective-permute-done.3.refs_3_
  23.9 2.2 %collective-permute-start.6 = (bf16[136,512]{1,0:T(8,128)(2,1)S(1)}, bf16[136,512]{1,0:T(8,128)(2,1)S(1)}, u32[]{:S(2)}, u32[]{:S(2)}) collective-permute-start(bf16[136,512]{1,0:T(8,128)(2,1)S(1)} %get-tuple-element.84), channel_id=1, source_target_pairs={{0,24},{4,28},{8,16},{12,20},{16,8},{20,12},{24,0},{28,4},{1,25},{... | collective-permute-start | bytes 417800 | tf_op jit(solution)/shard_map/ppermute | solution.py:404
  26.1 2.5 %shard_map.104 = (bf16[1024,512]{1,0:T(8,128)(2,1)S(1)}, bf16[1024,512]{1,0:T(8,128)(2,1)S(1)}, bf16[1024,512]{1,0:T(8,128)(2,1)S(1)}) custom-call(s32[1]{0:T(128)} %bitcast.1.slab_ref, bf16[1024,512]{1,0:T(8,128)(2,1)S(1)} %bitcast.38, bf16[1024,512]{1,0:T(8,128)(2,1)S(1)} %collective-permute-done.partner_ref, bf16[512,512]{1,0:T(8,128)(2,1)S(1)} %copy-done.1), custom_call_target="tpu_custom_call" | custom-call | flops 1024 | bytes 1024 | tf_op jit(solution)/shard_map/pallas_call | solution.py:222
  28.7 6.6 %collective-permute-done.5.refs_5_ = bf16[136,512]{1,0:T(8,128)(2,1)S(1)} collective-permute-done((bf16[136,512]{1,0:T(8,128)(2,1)S(1)}, bf16[136,512]{1,0:T(8,128)(2,1)S(1)}, u32[]{:S(2)}, u32[]{:S(2)}) %collective-permute-start.5) | collective-permute-done | bytes 139296 | tf_op jit(solution)/shard_map/ppermute | solution.py:404
  35.3 2.0 %shard_map.106 = (bf16[2,64,512]{2,1,0:T(8,128)(2,1)S(1)}, bf16[2,64,512]{2,1,0:T(8,128)(2,1)S(1)}, bf16[2,64,512]{2,1,0:T(8,128)(2,1)S(1)}, bf16[2,64,512]{2,1,...) custom-call(s32[1]{0:T(128)} %bitcast.place_ref, ...), custom_call_target="tpu_custom_call" | custom-call | flops 1024 | bytes 6601024 | tf_op jit(solution)/shard_map/pallas_call | solution.py:128
  37.4 0.1 collective-permute-start.10
  37.5 0.6 collective-permute-start.8
  38.0 4.9 %collective-permute-start.11 = (bf16[2,64,512]{2,1,0:T(8,128)(2,1)S(1)}, bf16[2,64,512]{2,1,0:T(8,128)(2,1)S(1)}, u32[]{:S(2)}, u32[]{:S(2)}) collective-permute-start(bf16[2,64,512]{2,1,0:T(8,128)(2,1)S(1)} %get-tuple-element.42), channel_id=1, source_target_pairs={{0,8},{4,12},{8,0},{12,4},{16,24},{20,28},{24,16},{28,20},{1,9},{5... | collective-permute-start | bytes 393224 | tf_op jit(solution)/shard_map/ppermute | solution.py:404
  42.9 0.8 collective-permute-start.12
  43.8 0.3 shard_map.107.rows_ref
  44.1 1.5 %collective-permute-start.14 = (bf16[128,512]{1,0:T(8,128)(2,1)S(1)}, bf16[128,512]{1,0:T(8,128)(2,1)S(1)}, u32[]{:S(2)}, u32[]{:S(2)}) collective-permute-start(bf16[128,512]{1,0:T(8,128)(2,1)S(1)} %shard_map.107.rows_ref), channel_id=1, source_target_pairs={{0,2},{1,3},{4,6},{5,7},{8,10},{9,11},{12,14},{13,15},{16,18},{17,... | collective-permute-start | bytes 393224 | tf_op jit(solution)/shard_map/ppermute | solution.py:409
  45.6 4.5 %collective-permute-start.13 = (bf16[2,64,512]{2,1,0:T(8,128)(2,1)S(1)}, bf16[2,64,512]{2,1,0:T(8,128)(2,1)S(1)}, u32[]{:S(2)}, u32[]{:S(2)}) collective-permute-start(bf16[2,64,512]{2,1,0:T(8,128)(2,1)S(1)} %get-tuple-element.44), channel_id=1, source_target_pairs={{0,16},{4,20},{8,24},{12,28},{16,0},{20,4},{24,8},{28,12},{1,17},{... | collective-permute-start | bytes 393224 | tf_op jit(solution)/shard_map/ppermute | solution.py:404
  50.1 2.0 %collective-permute-start.16 = (bf16[2,64,512]{2,1,0:T(8,128)(2,1)S(1)}, bf16[2,64,512]{2,1,0:T(8,128)(2,1)S(1)}, u32[]{:S(2)}, u32[]{:S(2)}) collective-permute-start(bf16[2,64,512]{2,1,0:T(8,128)(2,1)S(1)} %get-tuple-element.51), channel_id=1, source_target_pairs={{0,20},{4,16},{8,28},{12,24},{16,4},{20,0},{24,12},{28,8},{1,21},{... | collective-permute-start | bytes 393224 | tf_op jit(solution)/shard_map/ppermute | solution.py:404
  52.0 3.6 %collective-permute-start.17 = (bf16[2,64,512]{2,1,0:T(8,128)(2,1)S(1)}, bf16[2,64,512]{2,1,0:T(8,128)(2,1)S(1)}, u32[]{:S(2)}, u32[]{:S(2)}) collective-permute-start(bf16[2,64,512]{2,1,0:T(8,128)(2,1)S(1)} %get-tuple-element.52), channel_id=1, source_target_pairs={{0,24},{4,28},{8,16},{12,20},{16,8},{20,12},{24,0},{28,4},{1,25},{... | collective-permute-start | bytes 393224 | tf_op jit(solution)/shard_map/ppermute | solution.py:404
  55.7 0.1 collective-permute-start.18
  55.8 0.8 shard_map.108.refs_0_
  56.6 1.5 %collective-permute-start.19 = (bf16[512,512]{1,0:T(8,128)(2,1)S(1)}, bf16[512,512]{1,0:T(8,128)(2,1)S(1)}, u32[]{:S(2)}, u32[]{:S(2)}) collective-permute-start(bf16[512,512]{1,0:T(8,128)(2,1)S(1)} %shard_map.108.refs_0_), channel_id=1, source_target_pairs={{0,2},{1,3},{4,6},{5,7},{8,10},{9,11},{12,14},{13,15},{16,18},{17,... | collective-permute-start | bytes 1572872 | tf_op jit(solution)/shard_map/ppermute | solution.py:409
  58.2 5.3 %shard_map.109 = (bf16[2,1024,512]{2,1,0:T(8,128)(2,1)S(1)}, bf16[2,1024,512]{2,1,0:T(8,128)(2,1)S(1)}) custom-call(s32[1]{0:T(128)} %bitcast.1.slab_ref, bf16[1024,512]{1,0:T(8,128)(2,1)S(1)} %get-tuple-element.46.chain_ref, bf16[1024,512]{1,0:T(8,128)(2,1)S(1)} %collective-permute-done.9.self_ref, ...), custom_call_target="tpu_custom_call" | custom-call | flops 1024 | bytes 17161024 | tf_op jit(solution)/shard_map/pallas_call | solution.py:265
  63.4 2.4 %shard_map.110.first_ref = f32[2,512]{1,0:T(2,128)S(1)} custom-call(s32[1]{0:T(128)} %bitcast.place_ref, bf16[1024,512]{1,0:T(8,128)(2,1)S(1)} %bitcast.41, bf16[1024,512]{1,0:T(8,128)(2,1)S(1)} %get-tuple-element.31.high_ref, bf16[1024,512]{1,0:T(8,128)(2,1)S(1)} %get-tuple-element.32.factor_ref, bf16[128,512]{1,0:T(8,128)(2,1)S(1)} %shard_map.107.rows_ref, ...), custom_call_target="tpu_custom_call" | custom-call | flops 1024 | bytes 7921024 | tf_op jit(solution)/shard_map/pallas_call | solution.py:369
  65.9 1.6 %collective-permute-start.15 = (f32[2,512]{1,0:T(2,128)S(1)}, f32[2,512]{1,0:T(2,128)S(1)}, u32[]{:S(2)}, u32[]{:S(2)}) collective-permute-start(f32[2,512]{1,0:T(2,128)S(1)} %shard_map.110.first_ref), channel_id=1, source_target_pairs={{0,4},{4,0},{8,12},{12,8},{16,20},{20,16},{24,28},{28,24},{1,5},{5... | collective-permute-start | bytes 12296 | tf_op jit(solution)/shard_map/ppermute | solution.py:404
  67.5 2.1 %collective-permute-done.15.second_ref = f32[2,512]{1,0:T(2,128)S(1)} collective-permute-done((f32[2,512]{1,0:T(2,128)S(1)}, f32[2,512]{1,0:T(2,128)S(1)}, u32[]{:S(2)}, u32[]{:S(2)}) %collective-permute-start.15) | collective-permute-done | bytes 4128 | tf_op jit(solution)/shard_map/ppermute | solution.py:404
  69.6 0.8 shard_map.112.refs_1_
  70.4 1.5 %collective-permute-start.20 = (bf16[512,512]{1,0:T(8,128)(2,1)S(1)}, bf16[512,512]{1,0:T(8,128)(2,1)S(1)}, u32[]{:S(2)}, u32[]{:S(2)}) collective-permute-start(bf16[512,512]{1,0:T(8,128)(2,1)S(1)} %shard_map.112.refs_1_), channel_id=1, source_target_pairs={{0,2},{1,3},{4,6},{5,7},{8,10},{9,11},{12,14},{13,15},{16,18},{17,... | collective-permute-start | bytes 1572872 | tf_op jit(solution)/shard_map/ppermute | solution.py:409
  71.9 4.3 %collective-permute-start.21 = (f32[2,512]{1,0:T(2,128)S(1)}, f32[2,512]{1,0:T(2,128)S(1)}, u32[]{:S(2)}, u32[]{:S(2)}) collective-permute-start(f32[2,512]{1,0:T(2,128)S(1)} %shard_map.111.first_ref), channel_id=1, source_target_pairs={{0,8},{4,12},{8,0},{12,4},{16,24},{20,28},{24,16},{28,20},{1,9},{5... | collective-permute-start | bytes 12296 | tf_op jit(solution)/shard_map/ppermute | solution.py:404
  76.2 1.6 %collective-permute-done.21.second_ref = f32[2,512]{1,0:T(2,128)S(1)} collective-permute-done((f32[2,512]{1,0:T(2,128)S(1)}, f32[2,512]{1,0:T(2,128)S(1)}, u32[]{:S(2)}, u32[]{:S(2)}) %collective-permute-start.21) | collective-permute-done | bytes 4128 | tf_op jit(solution)/shard_map/ppermute | solution.py:404
  77.8 2.3 %collective-permute-start.22 = (f32[2,512]{1,0:T(2,128)S(1)}, f32[2,512]{1,0:T(2,128)S(1)}, u32[]{:S(2)}, u32[]{:S(2)}) collective-permute-start(f32[2,512]{1,0:T(2,128)S(1)} %shard_map.117.first_ref), channel_id=1, source_target_pairs={{0,16},{4,20},{8,24},{12,28},{16,0},{20,4},{24,8},{28,12},{1,17},{... | collective-permute-start | bytes 12296 | tf_op jit(solution)/shard_map/ppermute | solution.py:404
  80.1 3.6 %shard_map.113 = (f32[1024,512]{1,0:T(8,128)S(1)}, f32[1024,512]{1,0:T(8,128)S(1)}) custom-call(s32[1]{0:T(128)} %bitcast.place_ref, bf16[1024,512]{1,0:T(8,128)(2,1)S(1)} %get-tuple-element.31.high_ref, bf16[1024,512]{1,0:T(8,128)(2,1)S(1)} %bitcast.43, bf16[1024,512]{1,0:T(8,128)(2,1)S(1)} %get-tuple-element.32.factor_ref, ...), custom_call_target="tpu_custom_call" | custom-call | flops 1024 | bytes 11881024 | tf_op jit(solution)/shard_map/pallas_call | solution.py:305
  83.7 1.5 %shard_map.114.total_ref = f32[1024,512]{1,0:T(8,128)S(1)} custom-call(s32[1]{0:T(128)} %bitcast.place_ref, f32[1024,512]{1,0:T(8,128)S(1)} %get-tuple-element.54.total_ref, bf16[512,512]{1,0:T(8,128)(2,1)S(1)} %collective-permute-done.19.refs_0_, bf16[2,1024,512]{2,1,0:T(8,128)(2,1)S(1)} %get-tuple-element.47.refs_1_, ...), custom_call_target="tpu_custom_call" | custom-call | flops 1024 | bytes 5941024 | tf_op jit(solution)/shard_map/pallas_call | solution.py:331
  85.1 0.1 collective-permute-start.23
  85.2 1.5 %shard_map.116.total_ref = f32[1024,512]{1,0:T(8,128)S(1)} custom-call(s32[1]{0:T(128)} %bitcast.place_ref, f32[1024,512]{1,0:T(8,128)S(1)} %get-tuple-element.55.total_ref, bf16[512,512]{1,0:T(8,128)(2,1)S(1)} %collective-permute-done.19.refs_0_, bf16[2,1024,512]{2,1,0:T(8,128)(2,1)S(1)} %get-tuple-element.47.refs_1_, ...), custom_call_target="tpu_custom_call" | custom-call | flops 1024 | bytes 5941024 | tf_op jit(solution)/shard_map/pallas_call | solution.py:331
  86.7 1.5 %shard_map.119 = bf16[1024,512]{1,0:T(8,128)(2,1)S(1)} custom-call(s32[1]{0:T(128)} %bitcast.place_ref, f32[1024,512]{1,0:T(8,128)S(1)} %shard_map.116.total_ref, bf16[512,512]{1,0:T(8,128)(2,1)S(1)} %collective-permute-done.20.refs_0_, bf16[2,1024,512]{2,1,0:T(8,128)(2,1)S(1)} %get-tuple-element.47.refs_1_, bf16[2,1024,512]{2,1,0:T(8,128)(2,1)S(1)} %get-tuple-element.48.refs_2_), custom_call_target="tpu_custom_call" | custom-call | flops 1024 | bytes 5941024 | tf_op jit(solution)/shard_map/pallas_call | solution.py:331
  88.2 0.6 collective-permute-start.24
  88.7 1.5 %shard_map.115.own_ref = f32[1024,512]{1,0:T(8,128)S(1)} custom-call(s32[1]{0:T(128)} %bitcast.place_ref, f32[1024,512]{1,0:T(8,128)S(1)} %shard_map.114.total_ref, bf16[512,512]{1,0:T(8,128)(2,1)S(1)} %collective-permute-done.20.refs_0_, bf16[2,1024,512]{2,1,0:T(8,128)(2,1)S(1)} %get-tuple-element.47.refs_1_, ...), custom_call_target="tpu_custom_call" | custom-call | flops 1024 | bytes 5941024 | tf_op jit(solution)/shard_map/pallas_call | solution.py:331
  90.2 0.8 collective-permute-done.24.partner_ref
  91.0 1.1 %shard_map.120 = (bf16[1024,512]{1,0:T(8,128)(2,1)}, f32[1,512]{1,0:T(1,128)}) custom-call(f32[1024,512]{1,0:T(8,128)S(1)} %shard_map.115.own_ref, bf16[1024,512]{1,0:T(8,128)(2,1)S(1)} %collective-permute-done.24.partner_ref, f32[2,512]{1,0:T(2,128)S(1)} %shard_map.118.own_density_ref, f32[2,512]{1,0:T(2,128)S(1)} %collective-permute-done.23.partner_density_ref), custom_call_target="tpu_custom_call" | custom-call | flops 1024 | bytes 3961024 | tf_op jit(solution)/shard_map/pallas_call | solution.py:394
  (33 shorter events, 0.1 us)
Async XLA Ops:
  0.6 14.3 %collective-permute-start = (bf16[1024,512]{1,0:T(8,128)(2,1)}, bf16[1024,512]{1,0:T(8,128)(2,1)S(1)}, u32[]{:S(2)}, u32[]{:S(2)}) collective-permute-start(bf16[1024,512]{1,0:T(8,128)(2,1)} %bitcast.36), channel_id=1, source_target_pairs={{0,1},{1,0},{2,3},{3,2},{4,5},{5,4},{6,7},{7,6},{8,9},{9,8},{10,11... | collective-permute-start | bytes 3145736 | tf_op jit(solution)/shard_map/ppermute | solution.py:404
  1.1 36.2 %collective-permute-start.9 = (bf16[1024,512]{1,0:T(8,128)(2,1)}, bf16[1024,512]{1,0:T(8,128)(2,1)S(1)}, u32[]{:S(2)}, u32[]{:S(2)}) collective-permute-start(bf16[1024,512]{1,0:T(8,128)(2,1)} %bitcast.37), channel_id=1, source_target_pairs={{0,2},{1,3},{4,6},{5,7},{8,10},{9,11},{12,14},{13,15},{16,18},{17,... | collective-permute-start | bytes 3145736 | tf_op jit(solution)/shard_map/ppermute | solution.py:409
  8.9 17.2 %copy-start = (bf16[1,2,512,512]{3,2,1,0:T(8,128)(2,1)S(1)}, bf16[1,2,512,512]{3,2,1,0:T(8,128)(2,1)}, u32[]{:S(2)}) copy-start(bf16[1,2,512,512]{3,2,1,0:T(8,128)(2,1)} %param.10) | copy-start | bytes 3145732
  8.9 17.2 %copy-start.1 = (bf16[512,512]{1,0:T(8,128)(2,1)S(1)}, bf16[512,512]{1,0:T(8,128)(2,1)}, u32[]{:S(2)}) copy-start(bf16[512,512]{1,0:T(8,128)(2,1)} %coupling_ref.3) | copy-start | bytes 1572868
  9.1 26.2 %copy-start.2 = (bf16[4,64,512]{2,1,0:T(8,128)(2,1)S(1)}, bf16[4,64,512]{2,1,0:T(8,128)(2,1)}, u32[]{:S(2)}) copy-start(bf16[4,64,512]{2,1,0:T(8,128)(2,1)} %phonon_ref.1) | copy-start | bytes 786436
  9.1 26.2 %copy-start.3 = (s32[8,6]{1,0:T(8,128)S(1)}, s32[8,6]{1,0:T(8,128)}, u32[]{:S(2)}) copy-start(s32[8,6]{1,0:T(8,128)} %source_ref.1) | copy-start | bytes 580
  9.1 26.2 %copy-start.4 = (s32[8,6]{1,0:T(8,128)S(1)}, s32[8,6]{1,0:T(8,128)}, u32[]{:S(2)}) copy-start(s32[8,6]{1,0:T(8,128)} %mode_ref.1) | copy-start | bytes 580
  9.2 10.8 %collective-permute-start.2 = (bf16[136,512]{1,0:T(8,128)(2,1)S(1)}, bf16[136,512]{1,0:T(8,128)(2,1)S(1)}, u32[]{:S(2)}, u32[]{:S(2)}) collective-permute-start(bf16[136,512]{1,0:T(8,128)(2,1)S(1)} %get-tuple-element.80), channel_id=1, source_target_pairs={{0,8},{4,12},{8,0},{12,4},{16,24},{20,28},{24,16},{28,20},{1,9},{5... | collective-permute-start | bytes 417800 | tf_op jit(solution)/shard_map/ppermute | solution.py:404
  10.9 13.0 %collective-permute-start.3 = (bf16[136,512]{1,0:T(8,128)(2,1)S(1)}, bf16[136,512]{1,0:T(8,128)(2,1)S(1)}, u32[]{:S(2)}, u32[]{:S(2)}) collective-permute-start(bf16[136,512]{1,0:T(8,128)(2,1)S(1)} %get-tuple-element.81), channel_id=1, source_target_pairs={{0,12},{4,8},{8,4},{12,0},{16,28},{20,24},{24,20},{28,16},{1,13},{... | collective-permute-start | bytes 417800 | tf_op jit(solution)/shard_map/ppermute | solution.py:404
  12.3 13.8 %collective-permute-start.4 = (bf16[136,512]{1,0:T(8,128)(2,1)S(1)}, bf16[136,512]{1,0:T(8,128)(2,1)S(1)}, u32[]{:S(2)}, u32[]{:S(2)}) collective-permute-start(bf16[136,512]{1,0:T(8,128)(2,1)S(1)} %get-tuple-element.82), channel_id=1, source_target_pairs={{0,16},{4,20},{8,24},{12,28},{16,0},{20,4},{24,8},{28,12},{1,17},{... | collective-permute-start | bytes 417800 | tf_op jit(solution)/shard_map/ppermute | solution.py:404
  14.9 20.4 %collective-permute-start.5 = (bf16[136,512]{1,0:T(8,128)(2,1)S(1)}, bf16[136,512]{1,0:T(8,128)(2,1)S(1)}, u32[]{:S(2)}, u32[]{:S(2)}) collective-permute-start(bf16[136,512]{1,0:T(8,128)(2,1)S(1)} %get-tuple-element.83), channel_id=1, source_target_pairs={{0,20},{4,16},{8,28},{12,24},{16,4},{20,0},{24,12},{28,8},{1,21},{... | collective-permute-start | bytes 417800 | tf_op jit(solution)/shard_map/ppermute | solution.py:404
  20.0 15.3 %collective-permute-start.7 = (bf16[136,512]{1,0:T(8,128)(2,1)S(1)}, bf16[136,512]{1,0:T(8,128)(2,1)S(1)}, u32[]{:S(2)}, u32[]{:S(2)}) collective-permute-start(bf16[136,512]{1,0:T(8,128)(2,1)S(1)} %get-tuple-element.78), channel_id=1, source_target_pairs={{0,28},{4,24},{8,20},{12,16},{16,12},{20,8},{24,4},{28,0},{1,29},{... | collective-permute-start | bytes 417800 | tf_op jit(solution)/shard_map/ppermute | solution.py:404
  23.9 11.4 %collective-permute-start.6 = (bf16[136,512]{1,0:T(8,128)(2,1)S(1)}, bf16[136,512]{1,0:T(8,128)(2,1)S(1)}, u32[]{:S(2)}, u32[]{:S(2)}) collective-permute-start(bf16[136,512]{1,0:T(8,128)(2,1)S(1)} %get-tuple-element.84), channel_id=1, source_target_pairs={{0,24},{4,28},{8,16},{12,20},{16,8},{20,12},{24,0},{28,4},{1,25},{... | collective-permute-start | bytes 417800 | tf_op jit(solution)/shard_map/ppermute | solution.py:404
  26.1 9.2 %collective-permute-start.1 = (bf16[136,512]{1,0:T(8,128)(2,1)S(1)}, bf16[136,512]{1,0:T(8,128)(2,1)S(1)}, u32[]{:S(2)}, u32[]{:S(2)}) collective-permute-start(bf16[136,512]{1,0:T(8,128)(2,1)S(1)} %get-tuple-element.34), channel_id=1, source_target_pairs={{0,4},{4,0},{8,12},{12,8},{16,20},{20,16},{24,28},{28,24},{1,5},{5... | collective-permute-start | bytes 417800 | tf_op jit(solution)/shard_map/ppermute | solution.py:404
  37.4 18.3 %collective-permute-start.10 = (bf16[1024,512]{1,0:T(8,128)(2,1)S(1)}, bf16[1024,512]{1,0:T(8,128)(2,1)S(1)}, u32[]{:S(2)}, u32[]{:S(2)}) collective-permute-start(bf16[1024,512]{1,0:T(8,128)(2,1)S(1)} %collective-permute-done.9.self_ref), channel_id=1, source_target_pairs={{0,1},{1,0},{2,3},{3,2},{4,5},{5,4},{6,7},{7,6},{8,9},{9,8},{10,11... | collective-permute-start | bytes 3145736 | tf_op jit(solution)/shard_map/ppermute | solution.py:404
  37.5 8.2 %collective-permute-start.8 = (bf16[2,64,512]{2,1,0:T(8,128)(2,1)S(1)}, bf16[2,64,512]{2,1,0:T(8,128)(2,1)S(1)}, u32[]{:S(2)}, u32[]{:S(2)}) collective-permute-start(bf16[2,64,512]{2,1,0:T(8,128)(2,1)S(1)} %get-tuple-element.39), channel_id=1, source_target_pairs={{0,4},{4,0},{8,12},{12,8},{16,20},{20,16},{24,28},{28,24},{1,5},{5... | collective-permute-start | bytes 393224 | tf_op jit(solution)/shard_map/ppermute | solution.py:404
  38.0 12.0 %collective-permute-start.11 = (bf16[2,64,512]{2,1,0:T(8,128)(2,1)S(1)}, bf16[2,64,512]{2,1,0:T(8,128)(2,1)S(1)}, u32[]{:S(2)}, u32[]{:S(2)}) collective-permute-start(bf16[2,64,512]{2,1,0:T(8,128)(2,1)S(1)} %get-tuple-element.42), channel_id=1, source_target_pairs={{0,8},{4,12},{8,0},{12,4},{16,24},{20,28},{24,16},{28,20},{1,9},{5... | collective-permute-start | bytes 393224 | tf_op jit(solution)/shard_map/ppermute | solution.py:404
  42.9 9.1 %collective-permute-start.12 = (bf16[2,64,512]{2,1,0:T(8,128)(2,1)S(1)}, bf16[2,64,512]{2,1,0:T(8,128)(2,1)S(1)}, u32[]{:S(2)}, u32[]{:S(2)}) collective-permute-start(bf16[2,64,512]{2,1,0:T(8,128)(2,1)S(1)} %get-tuple-element.43), channel_id=1, source_target_pairs={{0,12},{4,8},{8,4},{12,0},{16,28},{20,24},{24,20},{28,16},{1,13},{... | collective-permute-start | bytes 393224 | tf_op jit(solution)/shard_map/ppermute | solution.py:404
  44.1 12.5 %collective-permute-start.14 = (bf16[128,512]{1,0:T(8,128)(2,1)S(1)}, bf16[128,512]{1,0:T(8,128)(2,1)S(1)}, u32[]{:S(2)}, u32[]{:S(2)}) collective-permute-start(bf16[128,512]{1,0:T(8,128)(2,1)S(1)} %shard_map.107.rows_ref), channel_id=1, source_target_pairs={{0,2},{1,3},{4,6},{5,7},{8,10},{9,11},{12,14},{13,15},{16,18},{17,... | collective-permute-start | bytes 393224 | tf_op jit(solution)/shard_map/ppermute | solution.py:409
  45.6 20.2 %collective-permute-start.13 = (bf16[2,64,512]{2,1,0:T(8,128)(2,1)S(1)}, bf16[2,64,512]{2,1,0:T(8,128)(2,1)S(1)}, u32[]{:S(2)}, u32[]{:S(2)}) collective-permute-start(bf16[2,64,512]{2,1,0:T(8,128)(2,1)S(1)} %get-tuple-element.44), channel_id=1, source_target_pairs={{0,16},{4,20},{8,24},{12,28},{16,0},{20,4},{24,8},{28,12},{1,17},{... | collective-permute-start | bytes 393224 | tf_op jit(solution)/shard_map/ppermute | solution.py:404
  50.1 19.5 %collective-permute-start.16 = (bf16[2,64,512]{2,1,0:T(8,128)(2,1)S(1)}, bf16[2,64,512]{2,1,0:T(8,128)(2,1)S(1)}, u32[]{:S(2)}, u32[]{:S(2)}) collective-permute-start(bf16[2,64,512]{2,1,0:T(8,128)(2,1)S(1)} %get-tuple-element.51), channel_id=1, source_target_pairs={{0,20},{4,16},{8,28},{12,24},{16,4},{20,0},{24,12},{28,8},{1,21},{... | collective-permute-start | bytes 393224 | tf_op jit(solution)/shard_map/ppermute | solution.py:404
  52.0 17.5 %collective-permute-start.17 = (bf16[2,64,512]{2,1,0:T(8,128)(2,1)S(1)}, bf16[2,64,512]{2,1,0:T(8,128)(2,1)S(1)}, u32[]{:S(2)}, u32[]{:S(2)}) collective-permute-start(bf16[2,64,512]{2,1,0:T(8,128)(2,1)S(1)} %get-tuple-element.52), channel_id=1, source_target_pairs={{0,24},{4,28},{8,16},{12,20},{16,8},{20,12},{24,0},{28,4},{1,25},{... | collective-permute-start | bytes 393224 | tf_op jit(solution)/shard_map/ppermute | solution.py:404
  55.7 13.9 %collective-permute-start.18 = (bf16[2,64,512]{2,1,0:T(8,128)(2,1)S(1)}, bf16[2,64,512]{2,1,0:T(8,128)(2,1)S(1)}, u32[]{:S(2)}, u32[]{:S(2)}) collective-permute-start(bf16[2,64,512]{2,1,0:T(8,128)(2,1)S(1)} %get-tuple-element.53), channel_id=1, source_target_pairs={{0,28},{4,24},{8,20},{12,16},{16,12},{20,8},{24,4},{28,0},{1,29},{... | collective-permute-start | bytes 393224 | tf_op jit(solution)/shard_map/ppermute | solution.py:404
  56.6 27.0 %collective-permute-start.19 = (bf16[512,512]{1,0:T(8,128)(2,1)S(1)}, bf16[512,512]{1,0:T(8,128)(2,1)S(1)}, u32[]{:S(2)}, u32[]{:S(2)}) collective-permute-start(bf16[512,512]{1,0:T(8,128)(2,1)S(1)} %shard_map.108.refs_0_), channel_id=1, source_target_pairs={{0,2},{1,3},{4,6},{5,7},{8,10},{9,11},{12,14},{13,15},{16,18},{17,... | collective-permute-start | bytes 1572872 | tf_op jit(solution)/shard_map/ppermute | solution.py:409
  65.9 3.7 %collective-permute-start.15 = (f32[2,512]{1,0:T(2,128)S(1)}, f32[2,512]{1,0:T(2,128)S(1)}, u32[]{:S(2)}, u32[]{:S(2)}) collective-permute-start(f32[2,512]{1,0:T(2,128)S(1)} %shard_map.110.first_ref), channel_id=1, source_target_pairs={{0,4},{4,0},{8,12},{12,8},{16,20},{20,16},{24,28},{28,24},{1,5},{5... | collective-permute-start | bytes 12296 | tf_op jit(solution)/shard_map/ppermute | solution.py:404
  70.4 16.3 %collective-permute-start.20 = (bf16[512,512]{1,0:T(8,128)(2,1)S(1)}, bf16[512,512]{1,0:T(8,128)(2,1)S(1)}, u32[]{:S(2)}, u32[]{:S(2)}) collective-permute-start(bf16[512,512]{1,0:T(8,128)(2,1)S(1)} %shard_map.112.refs_1_), channel_id=1, source_target_pairs={{0,2},{1,3},{4,6},{5,7},{8,10},{9,11},{12,14},{13,15},{16,18},{17,... | collective-permute-start | bytes 1572872 | tf_op jit(solution)/shard_map/ppermute | solution.py:409
  71.9 5.9 %collective-permute-start.21 = (f32[2,512]{1,0:T(2,128)S(1)}, f32[2,512]{1,0:T(2,128)S(1)}, u32[]{:S(2)}, u32[]{:S(2)}) collective-permute-start(f32[2,512]{1,0:T(2,128)S(1)} %shard_map.111.first_ref), channel_id=1, source_target_pairs={{0,8},{4,12},{8,0},{12,4},{16,24},{20,28},{24,16},{28,20},{1,9},{5... | collective-permute-start | bytes 12296 | tf_op jit(solution)/shard_map/ppermute | solution.py:404
  77.8 5.9 %collective-permute-start.22 = (f32[2,512]{1,0:T(2,128)S(1)}, f32[2,512]{1,0:T(2,128)S(1)}, u32[]{:S(2)}, u32[]{:S(2)}) collective-permute-start(f32[2,512]{1,0:T(2,128)S(1)} %shard_map.117.first_ref), channel_id=1, source_target_pairs={{0,16},{4,20},{8,24},{12,28},{16,0},{20,4},{24,8},{28,12},{1,17},{... | collective-permute-start | bytes 12296 | tf_op jit(solution)/shard_map/ppermute | solution.py:404
  85.1 1.5 %collective-permute-start.23 = (f32[2,512]{1,0:T(2,128)S(1)}, f32[2,512]{1,0:T(2,128)S(1)}, u32[]{:S(2)}, u32[]{:S(2)}) collective-permute-start(f32[2,512]{1,0:T(2,128)S(1)} %shard_map.118.own_density_ref), channel_id=1, source_target_pairs={{0,1},{1,0},{2,3},{3,2},{4,5},{5,4},{6,7},{7,6},{8,9},{9,8},{10,11... | collective-permute-start | bytes 12296 | tf_op jit(solution)/shard_map/ppermute | solution.py:404
  88.2 2.8 %collective-permute-start.24 = (bf16[1024,512]{1,0:T(8,128)(2,1)S(1)}, bf16[1024,512]{1,0:T(8,128)(2,1)S(1)}, u32[]{:S(2)}, u32[]{:S(2)}) collective-permute-start(bf16[1024,512]{1,0:T(8,128)(2,1)S(1)} %shard_map.119), channel_id=1, source_target_pairs={{0,1},{1,0},{2,3},{3,2},{4,5},{5,4},{6,7},{7,6},{8,9},{9,8},{10,11... | collective-permute-start | bytes 3145736 | tf_op jit(solution)/shard_map/ppermute | solution.py:404

commit v7 on v6

--- a/solution.py
+++ b/solution.py
@@ -384,18 +384,30 @@
     return call(add_kernel, shape, [VMEM] * 2, vmem=4)(first, second)
 
 
-def finish_kernel(own_ref, partner_ref, own_density_ref, partner_density_ref, green_ref, density_ref):
-    green_ref[...] = (own_ref[...] + partner_ref[...].astype(F32)).astype(BF16)
+def finish_kernel(own_ref, partner_ref, own_density_ref, partner_density_ref, green_hbm, density_ref, green, sems):
+    parts = green.shape[0]
+    rows = green.shape[1]
+    copies = []
+    for part in range(parts):
+        at = slice(part * rows, (part + 1) * rows)
+        green[part] = (own_ref[at, :] + partner_ref[at, :].astype(F32)).astype(BF16)
+        copies.append(pltpu.make_async_copy(green.at[part], green_hbm.at[part], sems.at[part]))
+        copies[-1].start()
     density_ref[...] = -(own_density_ref[0:1, :] + partner_density_ref[1:2, :])
+    for copy in copies:
+        copy.wait()
 
 
 def finish(own, partner, own_density, partner_density):
     n = own.shape[1]
-    return call(
+    shape = (4, n // 2, n)
+    return pl.pallas_call(
         finish_kernel,
-        [jax.ShapeDtypeStruct((2 * n, n), BF16), jax.ShapeDtypeStruct((1, n), F32)],
-        [VMEM] * 4,
-        cost=1.2,
+        out_shape=[jax.ShapeDtypeStruct(shape, BF16), jax.ShapeDtypeStruct((1, n), F32)],
+        in_specs=[VMEM] * 4,
+        out_specs=[pl.BlockSpec(memory_space=pl.ANY), VMEM],
+        scratch_shapes=[pltpu.VMEM(shape, BF16), pltpu.SemaphoreType.DMA((4,))],
+        compiler_params=pltpu.CompilerParams(vmem_limit_bytes=16 * 2**20),
     )(own, partner, own_density, partner_density)
 
 

time: 92.4 us -> 93 us (level)
  no operation moved by 1% of the time
where the time goes in v7:
time: 93 us; the launch traced here: 92.8 us
  starting transfers between devices  47 us (51%)
  Pallas kernels  25.2 us (27%)
  waiting for transfers between devices  15.9 us (17%)
  between operations  3.12 us (3%)
  local copies, waits for them, and re-layouts  1.47 us (2%)
    ppermute x21, starting transfers between devices, exchange(): return lax.ppermute(x, axis, [(i, i ^ distance) for i in range(size)])  38 us
    ppermute x21, waiting for transfers between devices, exchange(): return lax.ppermute(x, axis, [(i, i ^ distance) for i in range(size)])  15.9 us
    ppermute x4, starting transfers between devices, shift(): return lax.ppermute(x, axis, [(i, i + by) for i in range(size - by)])  9.03 us
    pallas_call x4, Pallas kernels, far_terms(): call(functools.partial(far_terms_kernel, target=target, group=group, ener...  5.86 us
    pallas_call x1, Pallas kernels, far_matrices(): call(far_matrices_kernel, [pair, pair] + [matrix] * goes_on, [SMEM] + [VM...  5.26 us
    pallas_call x1, Pallas kernels, own_terms(): call(functools.partial(own_terms_kernel, groups=groups, energies=energies...  3.56 us
    pallas_call x1, Pallas kernels, own_matrices(): call(own_matrices_kernel, [matrix, matrix, matrix], [SMEM] + [VMEM] * 3,...  2.55 us
    pallas_call x1, Pallas kernels, diagonal_sums(): call(functools.partial(diagonal_kernel, rows=n // energies), jax.ShapeDty...  2.43 us
  transfers between devices with their start and end apart: 25, of which 5 were waited for; matrix products, arithmetic and copies ran while one was open for 2% of the time, Pallas kernels for 24%

profile of v7, /device:TPU:0, one launch (start us, length us, event | category | flops | bytes accessed | tf_op | source)
XLA Modules:
  0.0 92.8 jit_solution(6259425377721084833)
XLA Ops:
  0.6 0.5 collective-permute-start
  1.1 4.5 %collective-permute-start.9 = (bf16[1024,512]{1,0:T(8,128)(2,1)}, bf16[1024,512]{1,0:T(8,128)(2,1)S(1)}, u32[]{:S(2)}, u32[]{:S(2)}) collective-permute-start(bf16[1024,512]{1,0:T(8,128)(2,1)} %bitcast.37), channel_id=1, source_target_pairs={{0,2},{1,3},{4,6},{5,7},{8,10},{9,11},{12,14},{13,15},{16,18},{17,... | collective-permute-start | bytes 3145736 | tf_op jit(solution)/shard_map/ppermute | solution.py:421
  7.6 1.3 %fusion = (bf16[1,1,1,512,512]{4,3,2,1,0:T(8,128)(2,1)S(1)}, bf16[1,1,1,512,512]{4,3,2,1,0:T(8,128)(2,1)S(1)}) fusion(bf16[1,1,2,512,512]{4,3,2,1,0:T(8,128)(2,1)} %param.9), kind=kLoop, calls=%fused_computation.24 | loop fusion | bytes 2097152 | tf_op jit(solution)/shard_map/unstack | solution.py:467
  8.9 0.0 copy-start
  8.9 0.2 dynamic-slice_bitcast_fusion
  9.1 0.0 copy-start.3
  9.1 0.1 pad_maximum_fusion
  9.2 1.6 %collective-permute-start.2 = (bf16[136,512]{1,0:T(8,128)(2,1)S(1)}, bf16[136,512]{1,0:T(8,128)(2,1)S(1)}, u32[]{:S(2)}, u32[]{:S(2)}) collective-permute-start(bf16[136,512]{1,0:T(8,128)(2,1)S(1)} %get-tuple-element.80), channel_id=1, source_target_pairs={{0,8},{4,12},{8,0},{12,4},{16,24},{20,28},{24,16},{28,20},{1,9},{5... | collective-permute-start | bytes 417800 | tf_op jit(solution)/shard_map/ppermute | solution.py:416
  10.9 1.4 %collective-permute-start.3 = (bf16[136,512]{1,0:T(8,128)(2,1)S(1)}, bf16[136,512]{1,0:T(8,128)(2,1)S(1)}, u32[]{:S(2)}, u32[]{:S(2)}) collective-permute-start(bf16[136,512]{1,0:T(8,128)(2,1)S(1)} %get-tuple-element.81), channel_id=1, source_target_pairs={{0,12},{4,8},{8,4},{12,0},{16,28},{20,24},{24,20},{28,16},{1,13},{... | collective-permute-start | bytes 417800 | tf_op jit(solution)/shard_map/ppermute | solution.py:416
  12.3 2.6 %collective-permute-start.4 = (bf16[136,512]{1,0:T(8,128)(2,1)S(1)}, bf16[136,512]{1,0:T(8,128)(2,1)S(1)}, u32[]{:S(2)}, u32[]{:S(2)}) collective-permute-start(bf16[136,512]{1,0:T(8,128)(2,1)S(1)} %get-tuple-element.82), channel_id=1, source_target_pairs={{0,16},{4,20},{8,24},{12,28},{16,0},{20,4},{24,8},{28,12},{1,17},{... | collective-permute-start | bytes 417800 | tf_op jit(solution)/shard_map/ppermute | solution.py:416
  14.9 0.3 collective-permute-start.5
  15.2 4.7 %collective-permute-done.2.refs_2_ = bf16[136,512]{1,0:T(8,128)(2,1)S(1)} collective-permute-done((bf16[136,512]{1,0:T(8,128)(2,1)S(1)}, bf16[136,512]{1,0:T(8,128)(2,1)S(1)}, u32[]{:S(2)}, u32[]{:S(2)}) %collective-permute-start.2) | collective-permute-done | bytes 139296 | tf_op jit(solution)/shard_map/ppermute | solution.py:416
  20.0 3.9 %collective-permute-start.7 = (bf16[136,512]{1,0:T(8,128)(2,1)S(1)}, bf16[136,512]{1,0:T(8,128)(2,1)S(1)}, u32[]{:S(2)}, u32[]{:S(2)}) collective-permute-start(bf16[136,512]{1,0:T(8,128)(2,1)S(1)} %get-tuple-element.78), channel_id=1, source_target_pairs={{0,28},{4,24},{8,20},{12,16},{16,12},{20,8},{24,4},{28,0},{1,29},{... | collective-permute-start | bytes 417800 | tf_op jit(solution)/shard_map/ppermute | solution.py:416
  23.8 0.0 collective-permute-done.3.refs_3_
  23.9 2.2 %collective-permute-start.6 = (bf16[136,512]{1,0:T(8,128)(2,1)S(1)}, bf16[136,512]{1,0:T(8,128)(2,1)S(1)}, u32[]{:S(2)}, u32[]{:S(2)}) collective-permute-start(bf16[136,512]{1,0:T(8,128)(2,1)S(1)} %get-tuple-element.84), channel_id=1, source_target_pairs={{0,24},{4,28},{8,16},{12,20},{16,8},{20,12},{24,0},{28,4},{1,25},{... | collective-permute-start | bytes 417800 | tf_op jit(solution)/shard_map/ppermute | solution.py:416
  26.1 2.5 %shard_map.104 = (bf16[1024,512]{1,0:T(8,128)(2,1)S(1)}, bf16[1024,512]{1,0:T(8,128)(2,1)S(1)}, bf16[1024,512]{1,0:T(8,128)(2,1)S(1)}) custom-call(s32[1]{0:T(128)} %bitcast.1.slab_ref, bf16[1024,512]{1,0:T(8,128)(2,1)S(1)} %bitcast.38, bf16[1024,512]{1,0:T(8,128)(2,1)S(1)} %collective-permute-done.partner_ref, bf16[512,512]{1,0:T(8,128)(2,1)S(1)} %copy-done.1), custom_call_target="tpu_custom_call" | custom-call | flops 1024 | bytes 1024 | tf_op jit(solution)/shard_map/pallas_call | solution.py:222
  28.7 6.6 %collective-permute-done.5.refs_5_ = bf16[136,512]{1,0:T(8,128)(2,1)S(1)} collective-permute-done((bf16[136,512]{1,0:T(8,128)(2,1)S(1)}, bf16[136,512]{1,0:T(8,128)(2,1)S(1)}, u32[]{:S(2)}, u32[]{:S(2)}) %collective-permute-start.5) | collective-permute-done | bytes 139296 | tf_op jit(solution)/shard_map/ppermute | solution.py:416
  35.3 2.0 %shard_map.106 = (bf16[2,64,512]{2,1,0:T(8,128)(2,1)S(1)}, bf16[2,64,512]{2,1,0:T(8,128)(2,1)S(1)}, bf16[2,64,512]{2,1,0:T(8,128)(2,1)S(1)}, bf16[2,64,512]{2,1,...) custom-call(s32[1]{0:T(128)} %bitcast.place_ref, ...), custom_call_target="tpu_custom_call" | custom-call | flops 1024 | bytes 6601024 | tf_op jit(solution)/shard_map/pallas_call | solution.py:128
  37.4 0.1 collective-permute-start.10
  37.5 0.6 collective-permute-start.8
  38.0 4.9 %collective-permute-start.11 = (bf16[2,64,512]{2,1,0:T(8,128)(2,1)S(1)}, bf16[2,64,512]{2,1,0:T(8,128)(2,1)S(1)}, u32[]{:S(2)}, u32[]{:S(2)}) collective-permute-start(bf16[2,64,512]{2,1,0:T(8,128)(2,1)S(1)} %get-tuple-element.42), channel_id=1, source_target_pairs={{0,8},{4,12},{8,0},{12,4},{16,24},{20,28},{24,16},{28,20},{1,9},{5... | collective-permute-start | bytes 393224 | tf_op jit(solution)/shard_map/ppermute | solution.py:416
  42.9 0.8 collective-permute-start.12
  43.8 0.3 shard_map.107.rows_ref
  44.1 1.5 %collective-permute-start.14 = (bf16[128,512]{1,0:T(8,128)(2,1)S(1)}, bf16[128,512]{1,0:T(8,128)(2,1)S(1)}, u32[]{:S(2)}, u32[]{:S(2)}) collective-permute-start(bf16[128,512]{1,0:T(8,128)(2,1)S(1)} %shard_map.107.rows_ref), channel_id=1, source_target_pairs={{0,2},{1,3},{4,6},{5,7},{8,10},{9,11},{12,14},{13,15},{16,18},{17,... | collective-permute-start | bytes 393224 | tf_op jit(solution)/shard_map/ppermute | solution.py:421
  45.6 4.5 %collective-permute-start.13 = (bf16[2,64,512]{2,1,0:T(8,128)(2,1)S(1)}, bf16[2,64,512]{2,1,0:T(8,128)(2,1)S(1)}, u32[]{:S(2)}, u32[]{:S(2)}) collective-permute-start(bf16[2,64,512]{2,1,0:T(8,128)(2,1)S(1)} %get-tuple-element.44), channel_id=1, source_target_pairs={{0,16},{4,20},{8,24},{12,28},{16,0},{20,4},{24,8},{28,12},{1,17},{... | collective-permute-start | bytes 393224 | tf_op jit(solution)/shard_map/ppermute | solution.py:416
  50.1 2.0 %collective-permute-start.16 = (bf16[2,64,512]{2,1,0:T(8,128)(2,1)S(1)}, bf16[2,64,512]{2,1,0:T(8,128)(2,1)S(1)}, u32[]{:S(2)}, u32[]{:S(2)}) collective-permute-start(bf16[2,64,512]{2,1,0:T(8,128)(2,1)S(1)} %get-tuple-element.51), channel_id=1, source_target_pairs={{0,20},{4,16},{8,28},{12,24},{16,4},{20,0},{24,12},{28,8},{1,21},{... | collective-permute-start | bytes 393224 | tf_op jit(solution)/shard_map/ppermute | solution.py:416
  52.0 3.6 %collective-permute-start.17 = (bf16[2,64,512]{2,1,0:T(8,128)(2,1)S(1)}, bf16[2,64,512]{2,1,0:T(8,128)(2,1)S(1)}, u32[]{:S(2)}, u32[]{:S(2)}) collective-permute-start(bf16[2,64,512]{2,1,0:T(8,128)(2,1)S(1)} %get-tuple-element.52), channel_id=1, source_target_pairs={{0,24},{4,28},{8,16},{12,20},{16,8},{20,12},{24,0},{28,4},{1,25},{... | collective-permute-start | bytes 393224 | tf_op jit(solution)/shard_map/ppermute | solution.py:416
  55.7 0.1 collective-permute-start.18
  55.8 0.8 shard_map.108.refs_0_
  56.6 1.5 %collective-permute-start.19 = (bf16[512,512]{1,0:T(8,128)(2,1)S(1)}, bf16[512,512]{1,0:T(8,128)(2,1)S(1)}, u32[]{:S(2)}, u32[]{:S(2)}) collective-permute-start(bf16[512,512]{1,0:T(8,128)(2,1)S(1)} %shard_map.108.refs_0_), channel_id=1, source_target_pairs={{0,2},{1,3},{4,6},{5,7},{8,10},{9,11},{12,14},{13,15},{16,18},{17,... | collective-permute-start | bytes 1572872 | tf_op jit(solution)/shard_map/ppermute | solution.py:421
  58.2 5.3 %shard_map.109 = (bf16[2,1024,512]{2,1,0:T(8,128)(2,1)S(1)}, bf16[2,1024,512]{2,1,0:T(8,128)(2,1)S(1)}) custom-call(s32[1]{0:T(128)} %bitcast.1.slab_ref, bf16[1024,512]{1,0:T(8,128)(2,1)S(1)} %get-tuple-element.46.chain_ref, bf16[1024,512]{1,0:T(8,128)(2,1)S(1)} %collective-permute-done.9.self_ref, ...), custom_call_target="tpu_custom_call" | custom-call | flops 1024 | bytes 17161024 | tf_op jit(solution)/shard_map/pallas_call | solution.py:265
  63.4 2.4 %shard_map.110.first_ref = f32[2,512]{1,0:T(2,128)S(1)} custom-call(s32[1]{0:T(128)} %bitcast.place_ref, bf16[1024,512]{1,0:T(8,128)(2,1)S(1)} %bitcast.41, bf16[1024,512]{1,0:T(8,128)(2,1)S(1)} %get-tuple-element.31.high_ref, bf16[1024,512]{1,0:T(8,128)(2,1)S(1)} %get-tuple-element.32.factor_ref, bf16[128,512]{1,0:T(8,128)(2,1)S(1)} %shard_map.107.rows_ref, ...), custom_call_target="tpu_custom_call" | custom-call | flops 1024 | bytes 7921024 | tf_op jit(solution)/shard_map/pallas_call | solution.py:369
  65.9 1.6 %collective-permute-start.15 = (f32[2,512]{1,0:T(2,128)S(1)}, f32[2,512]{1,0:T(2,128)S(1)}, u32[]{:S(2)}, u32[]{:S(2)}) collective-permute-start(f32[2,512]{1,0:T(2,128)S(1)} %shard_map.110.first_ref), channel_id=1, source_target_pairs={{0,4},{4,0},{8,12},{12,8},{16,20},{20,16},{24,28},{28,24},{1,5},{5... | collective-permute-start | bytes 12296 | tf_op jit(solution)/shard_map/ppermute | solution.py:416
  67.5 2.1 %collective-permute-done.15.second_ref = f32[2,512]{1,0:T(2,128)S(1)} collective-permute-done((f32[2,512]{1,0:T(2,128)S(1)}, f32[2,512]{1,0:T(2,128)S(1)}, u32[]{:S(2)}, u32[]{:S(2)}) %collective-permute-start.15) | collective-permute-done | bytes 4128 | tf_op jit(solution)/shard_map/ppermute | solution.py:416
  69.6 0.8 shard_map.112.refs_1_
  70.4 1.5 %collective-permute-start.20 = (bf16[512,512]{1,0:T(8,128)(2,1)S(1)}, bf16[512,512]{1,0:T(8,128)(2,1)S(1)}, u32[]{:S(2)}, u32[]{:S(2)}) collective-permute-start(bf16[512,512]{1,0:T(8,128)(2,1)S(1)} %shard_map.112.refs_1_), channel_id=1, source_target_pairs={{0,2},{1,3},{4,6},{5,7},{8,10},{9,11},{12,14},{13,15},{16,18},{17,... | collective-permute-start | bytes 1572872 | tf_op jit(solution)/shard_map/ppermute | solution.py:421
  71.9 4.3 %collective-permute-start.21 = (f32[2,512]{1,0:T(2,128)S(1)}, f32[2,512]{1,0:T(2,128)S(1)}, u32[]{:S(2)}, u32[]{:S(2)}) collective-permute-start(f32[2,512]{1,0:T(2,128)S(1)} %shard_map.111.first_ref), channel_id=1, source_target_pairs={{0,8},{4,12},{8,0},{12,4},{16,24},{20,28},{24,16},{28,20},{1,9},{5... | collective-permute-start | bytes 12296 | tf_op jit(solution)/shard_map/ppermute | solution.py:416
  76.2 1.6 %collective-permute-done.21.second_ref = f32[2,512]{1,0:T(2,128)S(1)} collective-permute-done((f32[2,512]{1,0:T(2,128)S(1)}, f32[2,512]{1,0:T(2,128)S(1)}, u32[]{:S(2)}, u32[]{:S(2)}) %collective-permute-start.21) | collective-permute-done | bytes 4128 | tf_op jit(solution)/shard_map/ppermute | solution.py:416
  77.8 2.3 %collective-permute-start.22 = (f32[2,512]{1,0:T(2,128)S(1)}, f32[2,512]{1,0:T(2,128)S(1)}, u32[]{:S(2)}, u32[]{:S(2)}) collective-permute-start(f32[2,512]{1,0:T(2,128)S(1)} %shard_map.117.first_ref), channel_id=1, source_target_pairs={{0,16},{4,20},{8,24},{12,28},{16,0},{20,4},{24,8},{28,12},{1,17},{... | collective-permute-start | bytes 12296 | tf_op jit(solution)/shard_map/ppermute | solution.py:416
  80.1 3.6 %shard_map.113 = (f32[1024,512]{1,0:T(8,128)S(1)}, f32[1024,512]{1,0:T(8,128)S(1)}) custom-call(s32[1]{0:T(128)} %bitcast.place_ref, bf16[1024,512]{1,0:T(8,128)(2,1)S(1)} %get-tuple-element.31.high_ref, bf16[1024,512]{1,0:T(8,128)(2,1)S(1)} %bitcast.43, bf16[1024,512]{1,0:T(8,128)(2,1)S(1)} %get-tuple-element.32.factor_ref, ...), custom_call_target="tpu_custom_call" | custom-call | flops 1024 | bytes 11881024 | tf_op jit(solution)/shard_map/pallas_call | solution.py:305
  83.7 1.5 %shard_map.114.total_ref = f32[1024,512]{1,0:T(8,128)S(1)} custom-call(s32[1]{0:T(128)} %bitcast.place_ref, f32[1024,512]{1,0:T(8,128)S(1)} %get-tuple-element.54.total_ref, bf16[512,512]{1,0:T(8,128)(2,1)S(1)} %collective-permute-done.19.refs_0_, bf16[2,1024,512]{2,1,0:T(8,128)(2,1)S(1)} %get-tuple-element.47.refs_1_, ...), custom_call_target="tpu_custom_call" | custom-call | flops 1024 | bytes 5941024 | tf_op jit(solution)/shard_map/pallas_call | solution.py:331
  85.1 0.1 collective-permute-start.23
  85.2 1.5 %shard_map.116.total_ref = f32[1024,512]{1,0:T(8,128)S(1)} custom-call(s32[1]{0:T(128)} %bitcast.place_ref, f32[1024,512]{1,0:T(8,128)S(1)} %get-tuple-element.55.total_ref, bf16[512,512]{1,0:T(8,128)(2,1)S(1)} %collective-permute-done.19.refs_0_, bf16[2,1024,512]{2,1,0:T(8,128)(2,1)S(1)} %get-tuple-element.47.refs_1_, ...), custom_call_target="tpu_custom_call" | custom-call | flops 1024 | bytes 5941024 | tf_op jit(solution)/shard_map/pallas_call | solution.py:331
  86.7 1.5 %shard_map.119 = bf16[1024,512]{1,0:T(8,128)(2,1)S(1)} custom-call(s32[1]{0:T(128)} %bitcast.place_ref, f32[1024,512]{1,0:T(8,128)S(1)} %shard_map.116.total_ref, bf16[512,512]{1,0:T(8,128)(2,1)S(1)} %collective-permute-done.20.refs_0_, bf16[2,1024,512]{2,1,0:T(8,128)(2,1)S(1)} %get-tuple-element.47.refs_1_, bf16[2,1024,512]{2,1,0:T(8,128)(2,1)S(1)} %get-tuple-element.48.refs_2_), custom_call_target="tpu_custom_call" | custom-call | flops 1024 | bytes 5941024 | tf_op jit(solution)/shard_map/pallas_call | solution.py:331
  88.2 0.6 collective-permute-start.24
  88.7 1.5 %shard_map.115.own_ref = f32[1024,512]{1,0:T(8,128)S(1)} custom-call(s32[1]{0:T(128)} %bitcast.place_ref, f32[1024,512]{1,0:T(8,128)S(1)} %shard_map.114.total_ref, bf16[512,512]{1,0:T(8,128)(2,1)S(1)} %collective-permute-done.20.refs_0_, bf16[2,1024,512]{2,1,0:T(8,128)(2,1)S(1)} %get-tuple-element.47.refs_1_, ...), custom_call_target="tpu_custom_call" | custom-call | flops 1024 | bytes 5941024 | tf_op jit(solution)/shard_map/pallas_call | solution.py:331
  90.2 0.8 collective-permute-done.24.partner_ref
  91.0 1.6 %shard_map.120 = (bf16[4,256,512]{2,1,0:T(8,128)(2,1)}, f32[1,512]{1,0:T(1,128)}) custom-call(f32[1024,512]{1,0:T(8,128)S(1)} %shard_map.115.own_ref, bf16[1024,512]{1,0:T(8,128)(2,1)S(1)} %collective-permute-done.24.partner_ref, f32[2,512]{1,0:T(2,128)S(1)} %shard_map.118.own_density_ref, f32[2,512]{1,0:T(2,128)S(1)} %collective-permute-done.23.partner_density_ref), custom_call_target="tpu_custom_call" | custom-call | tf_op jit(solution)/shard_map/pallas_call | solution.py:404
  (33 shorter events, 0.1 us)
Async XLA Ops:
  0.6 14.3 %collective-permute-start = (bf16[1024,512]{1,0:T(8,128)(2,1)}, bf16[1024,512]{1,0:T(8,128)(2,1)S(1)}, u32[]{:S(2)}, u32[]{:S(2)}) collective-permute-start(bf16[1024,512]{1,0:T(8,128)(2,1)} %bitcast.36), channel_id=1, source_target_pairs={{0,1},{1,0},{2,3},{3,2},{4,5},{5,4},{6,7},{7,6},{8,9},{9,8},{10,11... | collective-permute-start | bytes 3145736 | tf_op jit(solution)/shard_map/ppermute | solution.py:416
  1.1 36.2 %collective-permute-start.9 = (bf16[1024,512]{1,0:T(8,128)(2,1)}, bf16[1024,512]{1,0:T(8,128)(2,1)S(1)}, u32[]{:S(2)}, u32[]{:S(2)}) collective-permute-start(bf16[1024,512]{1,0:T(8,128)(2,1)} %bitcast.37), channel_id=1, source_target_pairs={{0,2},{1,3},{4,6},{5,7},{8,10},{9,11},{12,14},{13,15},{16,18},{17,... | collective-permute-start | bytes 3145736 | tf_op jit(solution)/shard_map/ppermute | solution.py:421
  8.9 17.2 %copy-start = (bf16[1,2,512,512]{3,2,1,0:T(8,128)(2,1)S(1)}, bf16[1,2,512,512]{3,2,1,0:T(8,128)(2,1)}, u32[]{:S(2)}) copy-start(bf16[1,2,512,512]{3,2,1,0:T(8,128)(2,1)} %param.10) | copy-start | bytes 3145732
  8.9 17.2 %copy-start.1 = (bf16[512,512]{1,0:T(8,128)(2,1)S(1)}, bf16[512,512]{1,0:T(8,128)(2,1)}, u32[]{:S(2)}) copy-start(bf16[512,512]{1,0:T(8,128)(2,1)} %coupling_ref.3) | copy-start | bytes 1572868
  9.1 26.2 %copy-start.2 = (bf16[4,64,512]{2,1,0:T(8,128)(2,1)S(1)}, bf16[4,64,512]{2,1,0:T(8,128)(2,1)}, u32[]{:S(2)}) copy-start(bf16[4,64,512]{2,1,0:T(8,128)(2,1)} %phonon_ref.1) | copy-start | bytes 786436
  9.1 26.2 %copy-start.3 = (s32[8,6]{1,0:T(8,128)S(1)}, s32[8,6]{1,0:T(8,128)}, u32[]{:S(2)}) copy-start(s32[8,6]{1,0:T(8,128)} %source_ref.1) | copy-start | bytes 580
  9.1 26.2 %copy-start.4 = (s32[8,6]{1,0:T(8,128)S(1)}, s32[8,6]{1,0:T(8,128)}, u32[]{:S(2)}) copy-start(s32[8,6]{1,0:T(8,128)} %mode_ref.1) | copy-start | bytes 580
  9.2 10.8 %collective-permute-start.2 = (bf16[136,512]{1,0:T(8,128)(2,1)S(1)}, bf16[136,512]{1,0:T(8,128)(2,1)S(1)}, u32[]{:S(2)}, u32[]{:S(2)}) collective-permute-start(bf16[136,512]{1,0:T(8,128)(2,1)S(1)} %get-tuple-element.80), channel_id=1, source_target_pairs={{0,8},{4,12},{8,0},{12,4},{16,24},{20,28},{24,16},{28,20},{1,9},{5... | collective-permute-start | bytes 417800 | tf_op jit(solution)/shard_map/ppermute | solution.py:416
  10.9 13.0 %collective-permute-start.3 = (bf16[136,512]{1,0:T(8,128)(2,1)S(1)}, bf16[136,512]{1,0:T(8,128)(2,1)S(1)}, u32[]{:S(2)}, u32[]{:S(2)}) collective-permute-start(bf16[136,512]{1,0:T(8,128)(2,1)S(1)} %get-tuple-element.81), channel_id=1, source_target_pairs={{0,12},{4,8},{8,4},{12,0},{16,28},{20,24},{24,20},{28,16},{1,13},{... | collective-permute-start | bytes 417800 | tf_op jit(solution)/shard_map/ppermute | solution.py:416
  12.3 13.8 %collective-permute-start.4 = (bf16[136,512]{1,0:T(8,128)(2,1)S(1)}, bf16[136,512]{1,0:T(8,128)(2,1)S(1)}, u32[]{:S(2)}, u32[]{:S(2)}) collective-permute-start(bf16[136,512]{1,0:T(8,128)(2,1)S(1)} %get-tuple-element.82), channel_id=1, source_target_pairs={{0,16},{4,20},{8,24},{12,28},{16,0},{20,4},{24,8},{28,12},{1,17},{... | collective-permute-start | bytes 417800 | tf_op jit(solution)/shard_map/ppermute | solution.py:416
  14.9 20.4 %collective-permute-start.5 = (bf16[136,512]{1,0:T(8,128)(2,1)S(1)}, bf16[136,512]{1,0:T(8,128)(2,1)S(1)}, u32[]{:S(2)}, u32[]{:S(2)}) collective-permute-start(bf16[136,512]{1,0:T(8,128)(2,1)S(1)} %get-tuple-element.83), channel_id=1, source_target_pairs={{0,20},{4,16},{8,28},{12,24},{16,4},{20,0},{24,12},{28,8},{1,21},{... | collective-permute-start | bytes 417800 | tf_op jit(solution)/shard_map/ppermute | solution.py:416
  20.0 15.3 %collective-permute-start.7 = (bf16[136,512]{1,0:T(8,128)(2,1)S(1)}, bf16[136,512]{1,0:T(8,128)(2,1)S(1)}, u32[]{:S(2)}, u32[]{:S(2)}) collective-permute-start(bf16[136,512]{1,0:T(8,128)(2,1)S(1)} %get-tuple-element.78), channel_id=1, source_target_pairs={{0,28},{4,24},{8,20},{12,16},{16,12},{20,8},{24,4},{28,0},{1,29},{... | collective-permute-start | bytes 417800 | tf_op jit(solution)/shard_map/ppermute | solution.py:416
  23.9 11.4 %collective-permute-start.6 = (bf16[136,512]{1,0:T(8,128)(2,1)S(1)}, bf16[136,512]{1,0:T(8,128)(2,1)S(1)}, u32[]{:S(2)}, u32[]{:S(2)}) collective-permute-start(bf16[136,512]{1,0:T(8,128)(2,1)S(1)} %get-tuple-element.84), channel_id=1, source_target_pairs={{0,24},{4,28},{8,16},{12,20},{16,8},{20,12},{24,0},{28,4},{1,25},{... | collective-permute-start | bytes 417800 | tf_op jit(solution)/shard_map/ppermute | solution.py:416
  26.1 9.2 %collective-permute-start.1 = (bf16[136,512]{1,0:T(8,128)(2,1)S(1)}, bf16[136,512]{1,0:T(8,128)(2,1)S(1)}, u32[]{:S(2)}, u32[]{:S(2)}) collective-permute-start(bf16[136,512]{1,0:T(8,128)(2,1)S(1)} %get-tuple-element.34), channel_id=1, source_target_pairs={{0,4},{4,0},{8,12},{12,8},{16,20},{20,16},{24,28},{28,24},{1,5},{5... | collective-permute-start | bytes 417800 | tf_op jit(solution)/shard_map/ppermute | solution.py:416
  37.4 18.3 %collective-permute-start.10 = (bf16[1024,512]{1,0:T(8,128)(2,1)S(1)}, bf16[1024,512]{1,0:T(8,128)(2,1)S(1)}, u32[]{:S(2)}, u32[]{:S(2)}) collective-permute-start(bf16[1024,512]{1,0:T(8,128)(2,1)S(1)} %collective-permute-done.9.self_ref), channel_id=1, source_target_pairs={{0,1},{1,0},{2,3},{3,2},{4,5},{5,4},{6,7},{7,6},{8,9},{9,8},{10,11... | collective-permute-start | bytes 3145736 | tf_op jit(solution)/shard_map/ppermute | solution.py:416
  37.5 8.2 %collective-permute-start.8 = (bf16[2,64,512]{2,1,0:T(8,128)(2,1)S(1)}, bf16[2,64,512]{2,1,0:T(8,128)(2,1)S(1)}, u32[]{:S(2)}, u32[]{:S(2)}) collective-permute-start(bf16[2,64,512]{2,1,0:T(8,128)(2,1)S(1)} %get-tuple-element.39), channel_id=1, source_target_pairs={{0,4},{4,0},{8,12},{12,8},{16,20},{20,16},{24,28},{28,24},{1,5},{5... | collective-permute-start | bytes 393224 | tf_op jit(solution)/shard_map/ppermute | solution.py:416
  38.0 12.0 %collective-permute-start.11 = (bf16[2,64,512]{2,1,0:T(8,128)(2,1)S(1)}, bf16[2,64,512]{2,1,0:T(8,128)(2,1)S(1)}, u32[]{:S(2)}, u32[]{:S(2)}) collective-permute-start(bf16[2,64,512]{2,1,0:T(8,128)(2,1)S(1)} %get-tuple-element.42), channel_id=1, source_target_pairs={{0,8},{4,12},{8,0},{12,4},{16,24},{20,28},{24,16},{28,20},{1,9},{5... | collective-permute-start | bytes 393224 | tf_op jit(solution)/shard_map/ppermute | solution.py:416
  42.9 9.1 %collective-permute-start.12 = (bf16[2,64,512]{2,1,0:T(8,128)(2,1)S(1)}, bf16[2,64,512]{2,1,0:T(8,128)(2,1)S(1)}, u32[]{:S(2)}, u32[]{:S(2)}) collective-permute-start(bf16[2,64,512]{2,1,0:T(8,128)(2,1)S(1)} %get-tuple-element.43), channel_id=1, source_target_pairs={{0,12},{4,8},{8,4},{12,0},{16,28},{20,24},{24,20},{28,16},{1,13},{... | collective-permute-start | bytes 393224 | tf_op jit(solution)/shard_map/ppermute | solution.py:416
  44.1 12.5 %collective-permute-start.14 = (bf16[128,512]{1,0:T(8,128)(2,1)S(1)}, bf16[128,512]{1,0:T(8,128)(2,1)S(1)}, u32[]{:S(2)}, u32[]{:S(2)}) collective-permute-start(bf16[128,512]{1,0:T(8,128)(2,1)S(1)} %shard_map.107.rows_ref), channel_id=1, source_target_pairs={{0,2},{1,3},{4,6},{5,7},{8,10},{9,11},{12,14},{13,15},{16,18},{17,... | collective-permute-start | bytes 393224 | tf_op jit(solution)/shard_map/ppermute | solution.py:421
  45.6 20.2 %collective-permute-start.13 = (bf16[2,64,512]{2,1,0:T(8,128)(2,1)S(1)}, bf16[2,64,512]{2,1,0:T(8,128)(2,1)S(1)}, u32[]{:S(2)}, u32[]{:S(2)}) collective-permute-start(bf16[2,64,512]{2,1,0:T(8,128)(2,1)S(1)} %get-tuple-element.44), channel_id=1, source_target_pairs={{0,16},{4,20},{8,24},{12,28},{16,0},{20,4},{24,8},{28,12},{1,17},{... | collective-permute-start | bytes 393224 | tf_op jit(solution)/shard_map/ppermute | solution.py:416
  50.1 19.5 %collective-permute-start.16 = (bf16[2,64,512]{2,1,0:T(8,128)(2,1)S(1)}, bf16[2,64,512]{2,1,0:T(8,128)(2,1)S(1)}, u32[]{:S(2)}, u32[]{:S(2)}) collective-permute-start(bf16[2,64,512]{2,1,0:T(8,128)(2,1)S(1)} %get-tuple-element.51), channel_id=1, source_target_pairs={{0,20},{4,16},{8,28},{12,24},{16,4},{20,0},{24,12},{28,8},{1,21},{... | collective-permute-start | bytes 393224 | tf_op jit(solution)/shard_map/ppermute | solution.py:416
  52.0 17.5 %collective-permute-start.17 = (bf16[2,64,512]{2,1,0:T(8,128)(2,1)S(1)}, bf16[2,64,512]{2,1,0:T(8,128)(2,1)S(1)}, u32[]{:S(2)}, u32[]{:S(2)}) collective-permute-start(bf16[2,64,512]{2,1,0:T(8,128)(2,1)S(1)} %get-tuple-element.52), channel_id=1, source_target_pairs={{0,24},{4,28},{8,16},{12,20},{16,8},{20,12},{24,0},{28,4},{1,25},{... | collective-permute-start | bytes 393224 | tf_op jit(solution)/shard_map/ppermute | solution.py:416
  55.7 13.9 %collective-permute-start.18 = (bf16[2,64,512]{2,1,0:T(8,128)(2,1)S(1)}, bf16[2,64,512]{2,1,0:T(8,128)(2,1)S(1)}, u32[]{:S(2)}, u32[]{:S(2)}) collective-permute-start(bf16[2,64,512]{2,1,0:T(8,128)(2,1)S(1)} %get-tuple-element.53), channel_id=1, source_target_pairs={{0,28},{4,24},{8,20},{12,16},{16,12},{20,8},{24,4},{28,0},{1,29},{... | collective-permute-start | bytes 393224 | tf_op jit(solution)/shard_map/ppermute | solution.py:416
  56.6 27.0 %collective-permute-start.19 = (bf16[512,512]{1,0:T(8,128)(2,1)S(1)}, bf16[512,512]{1,0:T(8,128)(2,1)S(1)}, u32[]{:S(2)}, u32[]{:S(2)}) collective-permute-start(bf16[512,512]{1,0:T(8,128)(2,1)S(1)} %shard_map.108.refs_0_), channel_id=1, source_target_pairs={{0,2},{1,3},{4,6},{5,7},{8,10},{9,11},{12,14},{13,15},{16,18},{17,... | collective-permute-start | bytes 1572872 | tf_op jit(solution)/shard_map/ppermute | solution.py:421
  65.9 3.7 %collective-permute-start.15 = (f32[2,512]{1,0:T(2,128)S(1)}, f32[2,512]{1,0:T(2,128)S(1)}, u32[]{:S(2)}, u32[]{:S(2)}) collective-permute-start(f32[2,512]{1,0:T(2,128)S(1)} %shard_map.110.first_ref), channel_id=1, source_target_pairs={{0,4},{4,0},{8,12},{12,8},{16,20},{20,16},{24,28},{28,24},{1,5},{5... | collective-permute-start | bytes 12296 | tf_op jit(solution)/shard_map/ppermute | solution.py:416
  70.4 16.3 %collective-permute-start.20 = (bf16[512,512]{1,0:T(8,128)(2,1)S(1)}, bf16[512,512]{1,0:T(8,128)(2,1)S(1)}, u32[]{:S(2)}, u32[]{:S(2)}) collective-permute-start(bf16[512,512]{1,0:T(8,128)(2,1)S(1)} %shard_map.112.refs_1_), channel_id=1, source_target_pairs={{0,2},{1,3},{4,6},{5,7},{8,10},{9,11},{12,14},{13,15},{16,18},{17,... | collective-permute-start | bytes 1572872 | tf_op jit(solution)/shard_map/ppermute | solution.py:421
  71.9 5.9 %collective-permute-start.21 = (f32[2,512]{1,0:T(2,128)S(1)}, f32[2,512]{1,0:T(2,128)S(1)}, u32[]{:S(2)}, u32[]{:S(2)}) collective-permute-start(f32[2,512]{1,0:T(2,128)S(1)} %shard_map.111.first_ref), channel_id=1, source_target_pairs={{0,8},{4,12},{8,0},{12,4},{16,24},{20,28},{24,16},{28,20},{1,9},{5... | collective-permute-start | bytes 12296 | tf_op jit(solution)/shard_map/ppermute | solution.py:416
  77.8 5.9 %collective-permute-start.22 = (f32[2,512]{1,0:T(2,128)S(1)}, f32[2,512]{1,0:T(2,128)S(1)}, u32[]{:S(2)}, u32[]{:S(2)}) collective-permute-start(f32[2,512]{1,0:T(2,128)S(1)} %shard_map.117.first_ref), channel_id=1, source_target_pairs={{0,16},{4,20},{8,24},{12,28},{16,0},{20,4},{24,8},{28,12},{1,17},{... | collective-permute-start | bytes 12296 | tf_op jit(solution)/shard_map/ppermute | solution.py:416
  85.1 1.5 %collective-permute-start.23 = (f32[2,512]{1,0:T(2,128)S(1)}, f32[2,512]{1,0:T(2,128)S(1)}, u32[]{:S(2)}, u32[]{:S(2)}) collective-permute-start(f32[2,512]{1,0:T(2,128)S(1)} %shard_map.118.own_density_ref), channel_id=1, source_target_pairs={{0,1},{1,0},{2,3},{3,2},{4,5},{5,4},{6,7},{7,6},{8,9},{9,8},{10,11... | collective-permute-start | bytes 12296 | tf_op jit(solution)/shard_map/ppermute | solution.py:416
  88.2 2.8 %collective-permute-start.24 = (bf16[1024,512]{1,0:T(8,128)(2,1)S(1)}, bf16[1024,512]{1,0:T(8,128)(2,1)S(1)}, u32[]{:S(2)}, u32[]{:S(2)}) collective-permute-start(bf16[1024,512]{1,0:T(8,128)(2,1)S(1)} %shard_map.119), channel_id=1, source_target_pairs={{0,1},{1,0},{2,3},{3,2},{4,5},{5,4},{6,7},{7,6},{8,9},{9,8},{10,11... | collective-permute-start | bytes 3145736 | tf_op jit(solution)/shard_map/ppermute | solution.py:416
